TPU v7x, 32 devices: a whole 2x2x4 slice. The times are simulated.
32 devices in a mesh: dp: 2 (over core), ep: 4 (over z), tp: 4 (over y, x).
Axes of the slice: x: 2, y: 2, z: 4, core: 2. Of those that a mesh axis runs over, the one named last changes fastest.
Arguments:
- hidden_in: bfloat16 [8, 2048, 1024], P('dp', 'ep'), may hold values from -6 to 6
- cotangent: bfloat16 [8, 2048, 1024], P('dp', 'ep'), may hold values from -6 to 6
- segment_ids: int32 [8, 2048], P('dp'), may hold values from 0 to 4, as said below
- expert_routes: int32 [8, 2048, 8], P('dp', 'ep'), may hold values from 0 to 31, all different within a row; in each aligned block of 512 rows (0 to 511, 512 to 1023, ..., all dimensions but the last counted through in order) at most 256 rows name the same one
- attn_gain: bfloat16 [1024], replicated, may hold values from 0.5 to 1.5
- w_query: bfloat16 [1024, 1024], P(None, 'tp'), may hold values from -0.1875 to 0.1875
- key_projection_weight: bfloat16 [1024, 512], P(None, 'tp'), may hold values from -0.1875 to 0.1875
- value_projection_weight: bfloat16 [1024, 512], P(None, 'tp'), may hold values from -0.1875 to 0.1875
- w_out: bfloat16 [1024, 1024], P('tp'), may hold values from -4 to 4
- moe_gain: bfloat16 [1024], replicated, may hold values from 0.5 to 1.5
- w_router: bfloat16 [1024, 32], replicated, may hold values from -0.09375 to 0.09375
- w_gate: bfloat16 [32, 1024, 512], P('ep', None, 'tp'), may hold values from -0.1875 to 0.1875
- w_up: bfloat16 [32, 1024, 512], P('ep', None, 'tp'), may hold values from -0.1875 to 0.1875
- w_down: bfloat16 [32, 512, 1024], P('ep', 'tp'), may hold values from -1 to 1
Outputs:
- block_out: float32 [8, 2048, 1024], P('dp', 'ep', 'tp')
- grad_in: float32 [8, 2048, 1024], P('dp', 'ep')
- grad_attn_gain: float32 [1024], P(('dp', 'ep'))
- grad_w_query: float32 [1024, 1024], P(('dp', 'ep'), 'tp')
- grad_w_key: float32 [1024, 512], P(('dp', 'ep'), 'tp')
- grad_w_value: float32 [1024, 512], P(('dp', 'ep'), 'tp')
- grad_w_out: float32 [1024, 1024], P('tp', ('dp', 'ep'))
- grad_moe_gain: float32 [1024], P(('dp', 'ep'))
- grad_w_router: float32 [1024, 32], P(('dp', 'ep'))
- grad_w_gate: float32 [32, 1024, 512], P('ep', 'dp', 'tp')
- grad_w_up: float32 [32, 1024, 512], P('ep', 'dp', 'tp')
- grad_w_down: float32 [32, 512, 1024], P('ep', 'tp', 'dp')
Inputs may be any that keep to these rules, and one draw needn't show every extreme that they name: `expert_routes`: in each aligned block of 512 rows (the tokens of one sequence on one device) no expert is named by more than 256 rows, and in every draw some expert is named by exactly 256 rows of some block; the 8 entries of a row differ. `segment_ids`: within each packed sequence the ids never fall, begin at 0 and end at 4; document 2 begins within the first 512 tokens of the sequence and ends within its last 512.
All inputs are finite; a program needn't handle non-finite values.
Results may differ from a plain program's by a relative error of at most 0.028.
Values may be sent and summed in bfloat16 or wider, within the bound.
No kernel may reach another device: no remote copies, remote signals or barrier semaphores. Data moves between devices by JAX's collectives and lax.ppermute only.
A program may use at most 1.0625 GiB of HBM per device.

v0:
```python
import math

import jax
import jax.numpy as jnp
from jax import lax
from jax.sharding import PartitionSpec as P

HEAD_SIZE = 64


EPSILON = 1e-06


def matrix_multiply(left_side, right_side):
    return jnp.dot(left_side, right_side, preferred_element_type=jnp.float32)


def contract_rows(left_side, right_side):
    return lax.dot_general(
        left_side, right_side, (((0,), (0,)), ((), ())), preferred_element_type=jnp.float32
    )


def contract_last(left_side, right_side):
    return lax.dot_general(
        left_side, right_side, (((1,), (1,)), ((), ())), preferred_element_type=jnp.float32
    )


def inverse_rms(values):
    return lax.rsqrt(jnp.mean(values * values, axis=-1, keepdims=True) + EPSILON)


def norm_back(grad_normed, normed, factor, gain_vec):
    scaled = grad_normed * gain_vec
    return factor * (scaled - normed * jnp.mean(scaled * normed, axis=-1, keepdims=True))


def rotate(vectors, cosine_table, sine_table):
    halfway = vectors.shape[-1] // 2
    front_half = vectors[..., :halfway]
    back_half = vectors[..., halfway:]
    return jnp.concatenate(
        [
            front_half * cosine_table - back_half * sine_table,
            back_half * cosine_table + front_half * sine_table,
        ],
        axis=-1,
    )


def rotate_back(grads_in, cosine_table, sine_table):
    halfway = grads_in.shape[-1] // 2
    front_half = grads_in[..., :halfway]
    back_half = grads_in[..., halfway:]
    return jnp.concatenate(
        [
            front_half * cosine_table + back_half * sine_table,
            back_half * cosine_table - front_half * sine_table,
        ],
        axis=-1,
    )


def expert_forward(rows_in, gate_w, up_w, down_w):
    gate_val = jnp.einsum("secd,edf->secf", rows_in, gate_w, preferred_element_type=jnp.float32)
    up_val = jnp.einsum("secd,edf->secf", rows_in, up_w, preferred_element_type=jnp.float32)
    active = (jax.nn.silu(gate_val) * up_val).astype(jnp.bfloat16)
    result = jnp.einsum("secf,efd->secd", active, down_w, preferred_element_type=jnp.float32)
    return (result, gate_val, up_val)


def expert_backward(rows_in, grad_rows, gate_val, up_val, gate_w, up_w, down_w):
    sigmoid_val = jax.nn.sigmoid(gate_val)
    swish_val = gate_val * sigmoid_val
    active = (swish_val * up_val).astype(jnp.bfloat16)
    grad_active = jnp.einsum(
        "secd,efd->secf", grad_rows, down_w, preferred_element_type=jnp.float32
    )
    grad_gate_val = (
        grad_active * up_val * sigmoid_val * (1.0 + gate_val * (1.0 - sigmoid_val))
    ).astype(jnp.bfloat16)
    grad_up_val = (grad_active * swish_val).astype(jnp.bfloat16)
    down_grad = jnp.einsum("secf,secd->efd", active, grad_rows, preferred_element_type=jnp.float32)
    gate_grad = jnp.einsum(
        "secd,secf->edf", rows_in, grad_gate_val, preferred_element_type=jnp.float32
    )
    up_grad = jnp.einsum("secd,secf->edf", rows_in, grad_up_val, preferred_element_type=jnp.float32)
    grad_inputs = jnp.einsum(
        "secf,edf->secd", grad_gate_val, gate_w, preferred_element_type=jnp.float32
    )
    grad_inputs = grad_inputs + jnp.einsum(
        "secf,edf->secd", grad_up_val, up_w, preferred_element_type=jnp.float32
    )
    return (grad_inputs, gate_grad, up_grad, down_grad)


def per_device(
    hidden_in,
    cotangent,
    segment_ids,
    expert_routes,
    attn_gain,
    w_query,
    key_projection_weight,
    value_projection_weight,
    w_out,
    moe_gain,
    w_router,
    w_gate,
    w_up,
    w_down,
):
    seq_count = hidden_in.shape[0]
    slice_rows = hidden_in.shape[1]
    model_width = hidden_in.shape[2]
    local_rows = seq_count * slice_rows
    top_count = expert_routes.shape[2]
    expert_count = w_router.shape[1]
    seq_length = segment_ids.shape[1]
    heads_query = w_query.shape[1] // HEAD_SIZE
    heads_kv = key_projection_weight.shape[1] // HEAD_SIZE
    query_group_width = heads_query // heads_kv
    kv_width = heads_kv * HEAD_SIZE
    ep_count = lax.axis_size("ep")
    tp_count = lax.axis_size("tp")
    ep_index = lax.axis_index("ep")
    tp_index = lax.axis_index("tp")
    score_scale = HEAD_SIZE ** (-0.5)
    hidden = hidden_in.reshape(local_rows, model_width).astype(jnp.float32)
    grad_out = cotangent.reshape(local_rows, model_width).astype(jnp.float32)
    query_pos = ep_index * slice_rows + jnp.arange(slice_rows, dtype=jnp.int32)
    query_seg = lax.dynamic_slice_in_dim(segment_ids, ep_index * slice_rows, slice_rows, 1)
    halfway = HEAD_SIZE // 2
    inverse = 1.0 / 10000.0 ** (jnp.arange(halfway, dtype=jnp.float32) * 2.0 / HEAD_SIZE)
    row_pos = jnp.tile(query_pos, seq_count)
    angles = row_pos.astype(jnp.float32)[:, None] * inverse[None, :]
    cosine_table = jnp.cos(angles)[:, None, :]
    sine_table = jnp.sin(angles)[:, None, :]
    gain_first = attn_gain.astype(jnp.float32)
    factor_first = inverse_rms(hidden)
    normed_first = hidden * factor_first
    first_input = (normed_first * gain_first).astype(jnp.bfloat16)
    query_lin = matrix_multiply(first_input, w_query).reshape(local_rows, heads_query, HEAD_SIZE)
    key_linear = matrix_multiply(first_input, key_projection_weight).reshape(
        local_rows, heads_kv, HEAD_SIZE
    )
    value_reduced = matrix_multiply(first_input, value_projection_weight).astype(jnp.bfloat16)
    query_rotated = rotate(query_lin, cosine_table, sine_table).astype(jnp.bfloat16)
    key_rotated = (
        rotate(key_linear, cosine_table, sine_table)
        .astype(jnp.bfloat16)
        .reshape(local_rows, kv_width)
    )
    packed = jnp.stack([key_rotated, value_reduced], axis=1).reshape(
        seq_count, slice_rows, 2, kv_width
    )
    kv_all = lax.all_gather(packed, "ep", axis=1, tiled=True)
    query_pack = query_rotated.reshape(
        seq_count, slice_rows, heads_kv, query_group_width, HEAD_SIZE
    )
    key_block = math.gcd(seq_length, 2048)
    starts = jnp.arange(seq_length // key_block, dtype=jnp.int32) * key_block

    def block_scores(block_first_row):
        key_rows = kv_all[:, :, 0].reshape(seq_count, key_block, heads_kv, HEAD_SIZE)
        value_rows = kv_all[:, :, 1].reshape(seq_count, key_block, heads_kv, HEAD_SIZE)
        scores = (
            jnp.einsum(
                "btkgd,bskd->bkgts", query_pack, key_rows, preferred_element_type=jnp.float32
            )
            * score_scale
        )
        key_pos = block_first_row + jnp.arange(key_block, dtype=jnp.int32)
        allowed = (key_pos[None, None, :] <= query_pos[None, :, None]) & (
            segment_ids[:, None, :] == query_seg[:, :, None]
        )
        return (scores, allowed[:, None, None], key_rows, value_rows)

    def max_step(state_pair, block_first_row):
        running_top, running_total = state_pair
        scores, allowed, key_rows, value_rows = block_scores(block_first_row)
        masked = jnp.where(allowed, scores, -1e30)
        new_top = jnp.maximum(running_top, jnp.max(masked, axis=-1))
        shifted = jnp.where(allowed, jnp.exp(masked - new_top[..., None]), 0.0)
        running_total = running_total * jnp.exp(running_top - new_top) + jnp.sum(shifted, axis=-1)
        return ((new_top, running_total), None)

    start_top = jnp.full((seq_count, heads_kv, query_group_width, slice_rows), -1e30, jnp.float32)
    (row_top, row_total), _ = lax.scan(max_step, (start_top, jnp.zeros_like(start_top)), starts)
    log_total = row_top + jnp.log(row_total)

    def probabilities(scores, allowed):
        return jnp.where(
            allowed, jnp.exp(jnp.where(allowed, scores, -1e30) - log_total[..., None]), 0.0
        )

    def mix_step(running_total, block_first_row):
        scores, allowed, key_rows, value_rows = block_scores(block_first_row)
        probability = probabilities(scores, allowed).astype(jnp.bfloat16)
        return (
            running_total
            + jnp.einsum(
                "bkgts,bskd->bkgtd", probability, value_rows, preferred_element_type=jnp.float32
            ),
            None,
        )

    attn_heads, _ = lax.scan(
        mix_step,
        jnp.zeros((seq_count, heads_kv, query_group_width, slice_rows, HEAD_SIZE), jnp.float32),
        starts,
    )
    attn_vec = jnp.transpose(attn_heads, (0, 3, 1, 2, 4)).reshape(
        local_rows, heads_query * HEAD_SIZE
    )
    attn_low = attn_vec.astype(jnp.bfloat16)
    attn_out = lax.psum(matrix_multiply(attn_low, w_out).astype(jnp.bfloat16), "tp").astype(
        jnp.float32
    )
    middle = hidden + attn_out
    gain_second = moe_gain.astype(jnp.float32)
    factor_second = inverse_rms(middle)
    normed_second = middle * factor_second
    second_in = (normed_second * gain_second).astype(jnp.bfloat16)
    logits = matrix_multiply(second_in, w_router)
    routes_tok = expert_routes.reshape(local_rows, top_count)
    chosen = (
        routes_tok[:, :, None] == jnp.arange(expert_count, dtype=jnp.int32)[None, None, :]
    ).astype(jnp.float32)
    picked = jnp.sum(chosen * logits[:, None, :], axis=-1)
    gate_weights = jax.nn.softmax(picked, axis=-1)
    route_seq = expert_routes.reshape(seq_count, slice_rows * top_count)
    onehot = (
        route_seq[:, :, None] == jnp.arange(expert_count, dtype=jnp.int32)[None, None, :]
    ).astype(jnp.int32)
    earlier = jnp.cumsum(onehot, axis=1) - onehot
    slot_index = jnp.sum(earlier * onehot, axis=2)
    capacity = 2 * slice_rows * top_count // expert_count
    seq_number = jnp.arange(seq_count, dtype=jnp.int32)[:, None]
    place_index = ((route_seq * seq_count + seq_number) * capacity + slot_index).reshape(-1)
    slots_all = expert_count * seq_count * capacity
    experts_here = w_gate.shape[0]
    send_rows = (
        jnp.zeros((slots_all, model_width), jnp.bfloat16)
        .at[place_index]
        .set(jnp.repeat(second_in, top_count, axis=0))
    )
    arrived = lax.all_to_all(
        send_rows.reshape(ep_count, experts_here, seq_count * capacity, model_width),
        "ep",
        split_axis=0,
        concat_axis=0,
        tiled=True,
    )
    result, gate_val, up_val = expert_forward(arrived, w_gate, w_up, w_down)
    sent_back = lax.all_to_all(
        result.astype(jnp.bfloat16), "ep", split_axis=0, concat_axis=0, tiled=True
    ).astype(result.dtype)
    routed = sent_back.reshape(slots_all, model_width)[place_index].reshape(
        local_rows, top_count, model_width
    )
    moe_part = jnp.sum(gate_weights[:, :, None] * routed, axis=1)
    route_dots = jnp.sum(routed * grad_out[:, None, :], axis=-1)
    moe_cols = lax.psum_scatter(
        moe_part.astype(jnp.bfloat16), "tp", scatter_dimension=1, tiled=True
    ).astype(jnp.float32)
    col_width = model_width // tp_count
    block_out = (
        lax.dynamic_slice_in_dim(middle, tp_index * col_width, col_width, 1) + moe_cols
    ).reshape(seq_count, slice_rows, col_width)
    grad_route = (
        (gate_weights[:, :, None] * grad_out[:, None, :])
        .reshape(local_rows * top_count, model_width)
        .astype(jnp.bfloat16)
    )
    grad_send = jnp.zeros((slots_all, model_width), jnp.bfloat16).at[place_index].set(grad_route)
    grad_arrived = lax.all_to_all(
        grad_send.reshape(ep_count, experts_here, seq_count * capacity, model_width),
        "ep",
        split_axis=0,
        concat_axis=0,
        tiled=True,
    )
    grad_inputs, gate_grad, up_grad, down_grad = expert_backward(
        arrived, grad_arrived, gate_val, up_val, w_gate, w_up, w_down
    )
    grad_inputs = lax.all_to_all(
        grad_inputs.astype(jnp.bfloat16), "ep", split_axis=0, concat_axis=0, tiled=True
    ).astype(grad_inputs.dtype)
    gate_grad, up_grad, down_grad = (
        lax.psum_scatter(
            gate_grad.astype(jnp.bfloat16), "dp", scatter_dimension=1, tiled=True
        ).astype(jnp.float32),
        lax.psum_scatter(
            up_grad.astype(jnp.bfloat16), "dp", scatter_dimension=1, tiled=True
        ).astype(jnp.float32),
        lax.psum_scatter(
            down_grad.astype(jnp.bfloat16), "dp", scatter_dimension=2, tiled=True
        ).astype(jnp.float32),
    )
    grad_tokens = jnp.sum(
        grad_inputs.reshape(slots_all, model_width)[place_index].reshape(
            local_rows, top_count, model_width
        ),
        axis=1,
    )
    grad_second_part, grad_gates = (
        lax.psum(grad_tokens.astype(jnp.bfloat16), "tp").astype(jnp.float32),
        lax.psum(route_dots.astype(jnp.bfloat16), "tp").astype(jnp.float32),
    )
    grad_picked = gate_weights * (
        grad_gates - jnp.sum(gate_weights * grad_gates, axis=-1, keepdims=True)
    )
    grad_logits = jnp.sum(chosen * grad_picked[:, :, None], axis=1).astype(jnp.bfloat16)
    grad_router = contract_rows(second_in, grad_logits)
    grad_second = grad_second_part + contract_last(grad_logits, w_router)
    grad_moe_gain = jnp.sum(grad_second * normed_second, axis=0)
    grad_middle = grad_out + norm_back(grad_second, normed_second, factor_second, gain_second)
    grad_attn = grad_middle.astype(jnp.bfloat16)
    grad_wo = contract_rows(attn_low, grad_attn)
    grad_vec = contract_last(grad_attn, w_out).astype(jnp.bfloat16)
    grad_heads = jnp.transpose(
        grad_vec.reshape(seq_count, slice_rows, heads_kv, query_group_width, HEAD_SIZE),
        (0, 2, 3, 1, 4),
    )
    delta_rows = jnp.sum(grad_heads.astype(jnp.float32) * attn_heads, axis=-1)

    def back_step(grad_query, block_first_row):
        scores, allowed, key_rows, value_rows = block_scores(block_first_row)
        probability = probabilities(scores, allowed)
        low_probability = probability.astype(jnp.bfloat16)
        grad_value = jnp.einsum(
            "bkgts,bkgtd->bskd", low_probability, grad_heads, preferred_element_type=jnp.float32
        )
        grad_prob = jnp.einsum(
            "bkgtd,bskd->bkgts", grad_heads, value_rows, preferred_element_type=jnp.float32
        )
        grad_scores = (probability * (grad_prob - delta_rows[..., None])).astype(jnp.bfloat16)
        grad_query = (
            grad_query
            + jnp.einsum(
                "bkgts,bskd->bkgtd", grad_scores, key_rows, preferred_element_type=jnp.float32
            )
            * score_scale
        )
        grad_key = (
            jnp.einsum(
                "bkgts,btkgd->bskd", grad_scores, query_pack, preferred_element_type=jnp.float32
            )
            * score_scale
        )
        return (
            grad_query,
            jnp.stack(
                [
                    grad_key.reshape(seq_count, key_block, kv_width),
                    grad_value.reshape(seq_count, key_block, kv_width),
                ],
                axis=2,
            ),
        )

    grad_query_heads, kv_parts = lax.scan(
        back_step,
        jnp.zeros((seq_count, heads_kv, query_group_width, slice_rows, HEAD_SIZE), jnp.float32),
        starts,
    )
    kv_parts = jnp.moveaxis(kv_parts, 0, 1).reshape(seq_count, seq_length, 2, kv_width)
    grad_kv = (
        lax.psum_scatter(kv_parts.astype(jnp.bfloat16), "ep", scatter_dimension=1, tiled=True)
        .astype(jnp.float32)
        .reshape(local_rows, 2, kv_width)
    )
    grad_query_rot = jnp.transpose(grad_query_heads, (0, 3, 1, 2, 4)).reshape(
        local_rows, heads_query, HEAD_SIZE
    )
    grad_query_lin = (
        rotate_back(grad_query_rot, cosine_table, sine_table)
        .reshape(local_rows, heads_query * HEAD_SIZE)
        .astype(jnp.bfloat16)
    )
    grad_key_lin = (
        rotate_back(
            grad_kv[:, 0].reshape(local_rows, heads_kv, HEAD_SIZE), cosine_table, sine_table
        )
        .reshape(local_rows, kv_width)
        .astype(jnp.bfloat16)
    )
    grad_value_lin = grad_kv[:, 1].astype(jnp.bfloat16)
    grad_wq = contract_rows(first_input, grad_query_lin)
    grad_wk = contract_rows(first_input, grad_key_lin)
    grad_wv = contract_rows(first_input, grad_value_lin)
    first_part = (
        contract_last(grad_query_lin, w_query)
        + contract_last(grad_key_lin, key_projection_weight)
        + contract_last(grad_value_lin, value_projection_weight)
    )
    grad_first = lax.psum(first_part.astype(jnp.bfloat16), "tp").astype(jnp.float32)
    grad_attn_gain = jnp.sum(grad_first * normed_first, axis=0)
    grad_in = (grad_middle + norm_back(grad_first, normed_first, factor_first, gain_first)).reshape(
        seq_count, slice_rows, model_width
    )
    dense = (
        lax.psum_scatter(grad_attn_gain, ("dp", "ep"), scatter_dimension=0, tiled=True),
        lax.psum_scatter(grad_wq, ("dp", "ep"), scatter_dimension=0, tiled=True),
        lax.psum_scatter(grad_wk, ("dp", "ep"), scatter_dimension=0, tiled=True),
        lax.psum_scatter(grad_wv, ("dp", "ep"), scatter_dimension=0, tiled=True),
        lax.psum_scatter(grad_wo, ("dp", "ep"), scatter_dimension=1, tiled=True),
        lax.psum_scatter(grad_moe_gain, ("dp", "ep"), scatter_dimension=0, tiled=True),
        lax.psum_scatter(grad_router, ("dp", "ep"), scatter_dimension=0, tiled=True),
    )
    return (
        block_out,
        grad_in,
        dense[0],
        dense[1],
        dense[2],
        dense[3],
        dense[4],
        dense[5],
        dense[6],
        gate_grad,
        up_grad,
        down_grad,
    )


def solution(mesh):
    placed = (
        P("dp", "ep", None),
        P("dp", "ep", None),
        P("dp", None),
        P("dp", "ep", None),
        P(),
        P(None, "tp"),
        P(None, "tp"),
        P(None, "tp"),
        P("tp", None),
        P(),
        P(),
        P("ep", None, "tp"),
        P("ep", None, "tp"),
        P("ep", "tp", None),
    )
    return jax.shard_map(
        per_device,
        mesh=mesh,
        in_specs=placed,
        out_specs=(
            P("dp", "ep", "tp"),
            P("dp", "ep", None),
            P(("dp", "ep")),
            P(("dp", "ep"), "tp"),
            P(("dp", "ep"), "tp"),
            P(("dp", "ep"), "tp"),
            P("tp", ("dp", "ep")),
            P(("dp", "ep")),
            P(("dp", "ep"), None),
            P("ep", "dp", "tp"),
            P("ep", "dp", "tp"),
            P("ep", "tp", "dp"),
        ),
        check_vma=False,
    )
```

profile of v0, /device:TPU:0, one launch (start us, length us, event | category | flops | bytes accessed | tf_op | source)
XLA Modules:
  0.0 7627.4 jit_solution(2118580392125375451)
XLA Ops:
  38.9 69.6 reduce-window.6
  233.6 97.2 %all-reduce.7.cloned.1.call-done = bf16[2048,1024]{1,0:T(8,128)(2,1)} async-done(((bf16[2048,1024]{1,0:T(8,128)(2,1)}), bf16[2048,1024]{1,0:T(8,128)(2,1)}) %all-reduce.7.cloned.1.call-update) | async-done | bytes 4194320 | tf_op jit(solution)/shard_map/psum | solution.py:218
  352.0 255.8 %scatter_custom_fusion = bf16[32768,1024]{1,0:T(8,128)(2,1)} fusion(s32[16384]{0:T(1024)S(1)} %get-tuple-element.71, bf16[16384,1024]{1,0:T(8,128)(2,1)} %broadcast_bitcast_fusion, s32[16384]{0:T(1024)S(1)} %broadcast_clamp_fusion.1, bf16[]{:T(256)} %constant.72.clone.1), kind=kCustom, calls=%fused_computation.34 | custom fusion | bytes 67109376 | tf_op jit(solution)/shard_map/scatter | solution.py:247
  645.0 255.8 %scatter_custom_fusion.1 = bf16[32768,1024]{1,0:T(8,128)(2,1)} fusion(s32[16384]{0:T(1024)S(1)} %get-tuple-element.71, bf16[16384,1024]{1,0:T(8,128)(2,1)} %fusion.2, s32[16384]{0:T(1024)S(1)} %broadcast_clamp_fusion.1, bf16[]{:T(256)} %constant.72.clone.1), kind=kCustom, calls=%fused_computation.32 | custom fusion | bytes 67109376 | tf_op jit(solution)/shard_map/scatter | solution.py:277
  900.9 1161.7 %all-to-all-done = bf16[4,8,1024,1024]{3,2,1,0:T(8,128)(2,1)} async-done(((bf16[4,8,1024,1024]{3,2,1,0:T(8,128)(2,1)}), bf16[4,8,1024,1024]{3,2,1,0:T(8,128)(2,1)}, u32[]{:S(2)}, u32[]{:S(2)}) %all-to-all-start) | async-done | bytes 67108896 | tf_op jit(solution)/shard_map/all_to_all | solution.py:249
  2138.0 1378.8 %all-to-all-done.2 = bf16[4,8,1024,1024]{3,2,1,0:T(8,128)(2,1)} async-done(((bf16[4,8,1024,1024]{3,2,1,0:T(8,128)(2,1)}), bf16[4,8,1024,1024]{3,2,1,0:T(8,128)(2,1)}, u32[]{:S(2)}, u32[]{:S(2)}) %all-to-all-start.2) | async-done | bytes 67108896 | tf_op jit(solution)/shard_map/all_to_all | solution.py:278
  3516.8 43.1 fusion.29
  3590.0 44.3 copy.152
  3647.5 47.0 fusion.60
  3694.5 69.1 fusion.15
  3763.5 44.3 copy.155
  3807.8 1280.7 %all-to-all-done.1 = bf16[4,8,1024,1024]{3,2,1,0:T(8,128)(2,1)} async-done(((bf16[4,8,1024,1024]{3,2,1,0:T(8,128)(2,1)}), bf16[4,8,1024,1024]{3,2,1,0:T(8,128)(2,1)}, u32[]{:S(2)}, u32[]{:S(2)}) %all-to-all-start.1) | async-done | bytes 67108896 | tf_op jit(solution)/shard_map/all_to_all | solution.py:257
  5101.5 66.3 bitcast_convert_fusion.1
  5167.9 306.4 %gather_fusion = f32[16384,1024]{1,0:T(8,128)} fusion(f32[32768,1024]{1,0:T(8,128)} %bitcast_convert_fusion.1, s32[16384]{0:T(1024)S(1)} %broadcast_clamp_fusion), kind=kCustom, calls=%fused_computation | custom fusion | bytes 134283264 | tf_op jit(solution)/shard_map/gather | solution.py:260
  5474.3 1068.1 %all-to-all-done.3 = bf16[4,8,1024,1024]{3,2,1,0:T(8,128)(2,1)} async-done(((bf16[4,8,1024,1024]{3,2,1,0:T(8,128)(2,1)}), bf16[4,8,1024,1024]{3,2,1,0:T(8,128)(2,1)}, u32[]{:S(2)}, u32[]{:S(2)}) %all-to-all-start.3) | async-done | bytes 67108896 | tf_op jit(solution)/shard_map/all_to_all | solution.py:288
  6542.4 66.2 bitcast_convert_fusion
  6608.6 306.5 %gather_fusion.1 = f32[16384,1024]{1,0:T(8,128)} fusion(f32[32768,1024]{1,0:T(8,128)} %bitcast_convert_fusion, s32[16384]{0:T(1024)S(1)} %broadcast_clamp_fusion), kind=kCustom, calls=%fused_computation.1 | custom fusion | bytes 134283264 | tf_op jit(solution)/shard_map/gather | solution.py:303
  6939.6 37.0 fusion.4
  6993.5 49.0 all-reduce.9.cloned.1.call-done
  7101.8 40.4 multiply_convert_fusion
  7343.9 99.8 %all-reduce.11.cloned.1.call-done = bf16[2048,1024]{1,0:T(8,128)(2,1)} async-done(((bf16[2048,1024]{1,0:T(8,128)(2,1)}), bf16[2048,1024]{1,0:T(8,128)(2,1)}) %all-reduce.11.cloned.1.call-update) | async-done | bytes 4194320 | tf_op jit(solution)/shard_map/psum | solution.py:399
  7477.3 37.3 reduce-scatter.21.cloned.1.call-done
  7514.6 37.5 reduce-scatter.15.cloned.1.call-done
  7552.1 34.5 reduce-scatter.19.cloned.1.call-done
  (296 shorter events, 715.0 us)
Async XLA Ops:
  7.2 3509.6 %copy-start = (bf16[8,128,1024]{2,1,0:T(8,128)(2,1)S(1)}, bf16[8,128,1024]{2,1,0:T(8,128)(2,1)}, u32[]{:S(2)}) copy-start(bf16[8,128,1024]{2,1,0:T(8,128)(2,1)} %param.27) | copy-start | bytes 6291460
  7.2 127.9 %all-gather.2.cloned.1.call-start = ((), (), s32[]{:S(2)}) async-start(), calls=%async_computation.14 | async-start | bytes 5242880 | tf_op jit(solution)/shard_map/all_gather | solution.py:158
  28.6 302.1 %all-reduce.7.cloned.1.call-start = ((), (), s32[]{:S(2)}) async-start(), calls=%async_computation.15 | async-start | bytes 8388608 | tf_op jit(solution)/shard_map/psum | solution.py:218
  30.6 305.2 %copy-start.58 = (f32[1024]{0:T(1024)}, f32[1024]{0:T(1024)S(1)}, u32[]{:S(2)}) copy-start(f32[1024]{0:T(1024)S(1)} %convert_element_type.239) | copy-start | bytes 12292
  607.8 1454.8 %all-to-all-start = ((bf16[4,8,1024,1024]{3,2,1,0:T(8,128)(2,1)}), bf16[4,8,1024,1024]{3,2,1,0:T(8,128)(2,1)}, u32[]{:S(2)}, u32[]{:S(2)}) async-start(bf16[4,8,1024,1024]{3,2,1,0:T(8,128)(2,1)} %bitcast.21), calls=%async_computation | async-start | bytes 134217728 | tf_op jit(solution)/shard_map/all_to_all | solution.py:249
  2062.6 1454.2 %all-to-all-start.2 = ((bf16[4,8,1024,1024]{3,2,1,0:T(8,128)(2,1)}), bf16[4,8,1024,1024]{3,2,1,0:T(8,128)(2,1)}, u32[]{:S(2)}, u32[]{:S(2)}) async-start(bf16[4,8,1024,1024]{3,2,1,0:T(8,128)(2,1)} %bitcast.37), calls=%async_computation.3 | async-start | bytes 134217728 | tf_op jit(solution)/shard_map/all_to_all | solution.py:278
  3634.3 1454.2 %all-to-all-start.1 = ((bf16[4,8,1024,1024]{3,2,1,0:T(8,128)(2,1)}), bf16[4,8,1024,1024]{3,2,1,0:T(8,128)(2,1)}, u32[]{:S(2)}, u32[]{:S(2)}) async-start(bf16[4,8,1024,1024]{3,2,1,0:T(8,128)(2,1)} %copy.152), calls=%async_computation.1 | async-start | bytes 134217728 | tf_op jit(solution)/shard_map/all_to_all | solution.py:257
  3807.8 1293.7 %copy-start.37 = (s32[16384,1]{0,1:T(1,128)S(1)}, s32[16384,1]{0,1:T(1,128)}, u32[]{:S(2)}) copy-start(s32[16384,1]{0,1:T(1,128)} %copy-done.36) | copy-start | bytes 196612
  5088.4 1454.0 %all-to-all-start.3 = ((bf16[4,8,1024,1024]{3,2,1,0:T(8,128)(2,1)}), bf16[4,8,1024,1024]{3,2,1,0:T(8,128)(2,1)}, u32[]{:S(2)}, u32[]{:S(2)}) async-start(bf16[4,8,1024,1024]{3,2,1,0:T(8,128)(2,1)} %copy.155), calls=%async_computation.4 | async-start | bytes 134217728 | tf_op jit(solution)/shard_map/all_to_all | solution.py:288
  5101.5 1941.0 %all-reduce.9.cloned.1.call-start = ((), (), s32[]{:S(2)}) async-start(), calls=%async_computation.17 | async-start | bytes 8388608 | tf_op jit(solution)/shard_map/psum | solution.py:309
  6939.5 336.6 %reduce-scatter.13.cloned.1.call-start = ((), (), s32[]{:S(2)}) async-start(), calls=%async_computation.18 | async-start | bytes 5242880 | tf_op jit(solution)/shard_map/reduce_scatter | solution.py:371
  7162.9 142.4 %reduce-scatter.29.cloned.1.call-start = ((), (), s32[]{:S(2)}) async-start(), calls=%async_computation.27 | async-start | bytes 3145728 | tf_op jit(solution)/shard_map/reduce_scatter | solution.py:298
  7190.7 117.4 %reduce-scatter.27.cloned.1.call-start = ((), (), s32[]{:S(2)}) async-start(), calls=%async_computation.26 | async-start | bytes 3145728 | tf_op jit(solution)/shard_map/reduce_scatter | solution.py:295
  7222.5 88.3 %reduce-scatter.25.cloned.1.call-start = ((), (), s32[]{:S(2)}) async-start(), calls=%async_computation.25 | async-start | bytes 3145728 | tf_op jit(solution)/shard_map/reduce_scatter | solution.py:292
  7253.8 82.3 %reduce-scatter.11.cloned.1.call-start = ((), (), s32[]{:S(2)}) async-start(), calls=%async_computation.16 | async-start | bytes 5242880 | tf_op jit(solution)/shard_map/reduce_scatter | solution.py:265
  7254.6 189.1 %all-reduce.11.cloned.1.call-start = ((), (), s32[]{:S(2)}) async-start(), calls=%async_computation.19 | async-start | bytes 8388608 | tf_op jit(solution)/shard_map/psum | solution.py:399
  7284.2 193.1 %reduce-scatter.23.cloned.1.call-start = ((), (), s32[]{:S(2)}) async-start(), calls=%async_computation.24 | async-start | bytes 147456 | tf_op jit(solution)/shard_map/reduce_scatter | solution.py:411
  7288.0 226.6 %reduce-scatter.21.cloned.1.call-start = ((), (), s32[]{:S(2)}) async-start(), calls=%async_computation.23 | async-start | bytes 1179648 | tf_op jit(solution)/shard_map/reduce_scatter | solution.py:409
  7294.4 257.7 %reduce-scatter.15.cloned.1.call-start = ((), (), s32[]{:S(2)}) async-start(), calls=%async_computation.20 | async-start | bytes 1179648 | tf_op jit(solution)/shard_map/reduce_scatter | solution.py:406
  7299.4 287.2 %reduce-scatter.19.cloned.1.call-start = ((), (), s32[]{:S(2)}) async-start(), calls=%async_computation.22 | async-start | bytes 589824 | tf_op jit(solution)/shard_map/reduce_scatter | solution.py:408
  7303.9 316.7 %reduce-scatter.17.cloned.1.call-start = ((), (), s32[]{:S(2)}) async-start(), calls=%async_computation.21 | async-start | bytes 589824 | tf_op jit(solution)/shard_map/reduce_scatter | solution.py:407
  7308.1 135.6 %copy-start.48 = (f32[1,4,4,128]{3,1,2,0:T(4,128)S(1)}, f32[1,4,4,128]{3,1,2,0:T(4,128)}, u32[]{:S(2)}) copy-start(f32[1,4,4,128]{3,1,2,0:T(4,128)} %copy-done.47) | copy-start | bytes 24580
  7308.1 135.6 %copy-start.52 = (f32[1024]{0:T(1024)S(1)}, f32[1024]{0:T(1024)}, u32[]{:S(2)}) copy-start(f32[1024]{0:T(1024)} %copy-done.51) | copy-start | bytes 12292
  7467.3 153.4 %copy-start.1 = (bf16[8,128,1024]{2,1,0:T(8,128)(2,1)S(1)}, bf16[8,128,1024]{2,1,0:T(8,128)(2,1)}, u32[]{:S(2)}) copy-start(bf16[8,128,1024]{2,1,0:T(8,128)(2,1)} %param.27) | copy-start | bytes 6291460
  (59 other events, 1441.8 us)
Sparse Core Ops, SparseCore 0:
  28.7 83.2 all-gather.1
  224.2 106.5 all-reduce.6
  6939.6 102.8 all-reduce.8
  7163.0 76.7 reduce-scatter.12
  7242.0 10.1 reduce-scatter.28
  7254.8 10.7 reduce-scatter.26
  7268.5 10.7 reduce-scatter.24
  7282.3 53.8 reduce-scatter.10
  7339.8 103.8 all-reduce.10
  7446.4 30.8 reduce-scatter.22
  7480.3 34.2 reduce-scatter.20
  7517.4 34.6 reduce-scatter.14
  7555.0 31.5 reduce-scatter.18
  7589.3 31.2 reduce-scatter.16
where the time goes:
time: 7660 us; the launch traced here: 7630 us
  waiting for transfers between devices  5300 us (69%)
  local copies, waits for them, and re-layouts  1280 us (17%)
  matrix products  546 us (7%)
  other arithmetic  396 us (5%)
    all_to_all x1, waiting for transfers between devices, per_device(): lax.all_to_all(grad_send.reshape(ep_count, experts_here, seq_count * capa...  1380 us
    all_to_all x1, waiting for transfers between devices, per_device(): lax.all_to_all(result.astype(jnp.bfloat16), 'ep', split_axis=0, concat_ax...  1280 us
    all_to_all x1, waiting for transfers between devices, per_device(): lax.all_to_all(send_rows.reshape(ep_count, experts_here, seq_count * capa...  1160 us
    all_to_all x1, waiting for transfers between devices, per_device(): lax.all_to_all(grad_inputs.astype(jnp.bfloat16), 'ep', split_axis=0, conc...  1070 us
    gather x1, local copies, waits for them, and re-layouts, per_device(): grad_inputs.reshape(slots_all, model_width)[place_index]  307 us
    gather x1, local copies, waits for them, and re-layouts, per_device(): sent_back.reshape(slots_all, model_width)[place_index]  306 us
    scatter x2, local copies, waits for them, and re-layouts, per_device(): send_rows = jnp.zeros((slots_all, model_width), jnp.bfloat16).at[place_in...  256 us
    scatter x1, local copies, waits for them, and re-layouts, per_device(): jnp.zeros((slots_all, model_width), jnp.bfloat16).at[place_index]  256 us
  transfers between devices with their start and end apart: 18, of which 13 were waited for; matrix products, arithmetic and copies ran while one was open for 16% of the time, Pallas kernels for 0%

commit v1 on v0

--- a/solution.py
+++ b/solution.py
@@ -3,12 +3,15 @@
 import jax
 import jax.numpy as jnp
 from jax import lax
+from jax.experimental import pallas as pl
+from jax.experimental.pallas import tpu as pltpu
 from jax.sharding import PartitionSpec as P
 
 HEAD_SIZE = 64
 
 
 EPSILON = 1e-06
+VMEM_BYTES = 58 * 1024 * 1024
 
 
 def matrix_multiply(left_side, right_side):
@@ -425,6 +428,968 @@
         down_grad,
     )
 
+def take_part(values, index, size, axis):
+    return lax.dynamic_slice_in_dim(values, index * size, size, axis)
+
+
+def shift_by(values, axis_name, distance):
+    count = lax.axis_size(axis_name)
+    return lax.ppermute(
+        values, axis_name, [(source, (source + distance) % count) for source in range(count)]
+    )
+
+
+def attend_kernel(
+    low_ref, mid_ref, q_ref, k_ref, v_ref, start_ref, out_ref, lse_ref, top_ref, total_ref, acc_ref
+):
+    query_block = pl.program_id(1)
+    width = q_ref.shape[2]
+    query = q_ref[0]
+
+    def key_step(block, masked):
+        rows = pl.ds(pl.multiple_of(block * width, width), width)
+        scores = jnp.dot(k_ref[rows, :], query, preferred_element_type=jnp.float32)
+        if masked:
+            key_pos = block * width + lax.broadcasted_iota(jnp.int32, (width, width), 0)
+            query_pos = query_block * width + lax.broadcasted_iota(jnp.int32, (width, width), 1)
+            scores = jnp.where(
+                (key_pos >= start_ref[...]) & (key_pos <= query_pos), scores, -1e30
+            )
+        old_top = top_ref[...]
+        new_top = jnp.maximum(old_top, jnp.max(scores, axis=0, keepdims=True))
+        shifted = jnp.exp(scores - new_top)
+        scale = jnp.exp(old_top - new_top)
+        top_ref[...] = new_top
+        total_ref[...] = total_ref[...] * scale + jnp.sum(shifted, axis=0, keepdims=True)
+        acc_ref[...] = acc_ref[...] * scale + jnp.dot(
+            v_ref[:, rows], shifted.astype(jnp.bfloat16), preferred_element_type=jnp.float32
+        )
+
+    top_ref[...] = jnp.full_like(top_ref, -1e30)
+    total_ref[...] = jnp.zeros_like(total_ref)
+    acc_ref[...] = jnp.zeros_like(acc_ref)
+    key_step(query_block, True)
+    low, mid = low_ref[query_block], jnp.minimum(mid_ref[query_block], query_block)
+    pl.loop(low, mid)(lambda block: key_step(block, True))
+    pl.loop(mid, query_block)(lambda block: key_step(block, False))
+    out_ref[...] = (acc_ref[...] / total_ref[...]).astype(out_ref.dtype)
+    lse_ref[0] = top_ref[...] + jnp.log(total_ref[...])
+
+
+def attend(query_t, key_rows, value_t, start_row, low, mid, width):
+    heads, double, length = query_t.shape
+    size = HEAD_SIZE
+    group = heads // (value_t.shape[0] // size)
+    blocks = length // width
+    return pl.pallas_call(
+        attend_kernel,
+        grid_spec=pltpu.PrefetchScalarGridSpec(
+            num_scalar_prefetch=2,
+            grid=(heads, blocks),
+            in_specs=[
+                pl.BlockSpec((1, double, width), lambda h, i, *_: (h, 0, i)),
+                pl.BlockSpec((length, double), lambda h, i, *_: (0, 0)),
+                pl.BlockSpec((size, length), lambda h, i, *_: (h // group, 0)),
+                pl.BlockSpec((1, width), lambda h, i, *_: (0, i)),
+            ],
+            out_specs=[
+                pl.BlockSpec((size, width), lambda h, i, *_: (h, i)),
+                pl.BlockSpec((1, 1, width), lambda h, i, *_: (h, 0, i)),
+            ],
+            scratch_shapes=[
+                pltpu.VMEM((1, width), jnp.float32),
+                pltpu.VMEM((1, width), jnp.float32),
+                pltpu.VMEM((size, width), jnp.float32),
+            ],
+        ),
+        out_shape=[
+            jax.ShapeDtypeStruct((heads * size, length), jnp.bfloat16),
+            jax.ShapeDtypeStruct((heads, 1, length), jnp.float32),
+        ],
+        compiler_params=pltpu.CompilerParams(vmem_limit_bytes=VMEM_BYTES),
+        cost_estimate=pl.CostEstimate(
+            flops=4 * heads * length * length * double,
+            bytes_accessed=8 * heads * length * double,
+            transcendentals=heads * length * length // 2,
+        ),
+        name="attend",
+    )(low, mid, query_t, key_rows, value_t, start_row)
+
+
+def attend_back_kernel(
+    low_ref,
+    mid_ref,
+    qt_ref,
+    q_ref,
+    gt_ref,
+    g_ref,
+    k_ref,
+    v_ref,
+    kt_ref,
+    start_ref,
+    lse_ref,
+    delta_ref,
+    gq_ref,
+    gk_ref,
+    gv_ref,
+):
+    key_block = pl.program_id(1)
+    width = kt_ref.shape[1]
+    blocks = k_ref.shape[0] // width
+    key_rows = pl.ds(pl.multiple_of(key_block * width, width), width)
+
+    @pl.when((pl.program_id(0) == 0) & (key_block == 0))
+    def _():
+        gk_ref[...] = jnp.zeros_like(gk_ref)
+        gv_ref[...] = jnp.zeros_like(gv_ref)
+
+    @pl.when(key_block == 0)
+    def _():
+        gq_ref[...] = jnp.zeros_like(gq_ref)
+
+    def query_step(block, masked):
+        rows = pl.ds(pl.multiple_of(block * width, width), width)
+        scores = jnp.dot(k_ref[key_rows, :], qt_ref[0, :, rows], preferred_element_type=jnp.float32)
+        if masked:
+            key_pos = key_block * width + lax.broadcasted_iota(jnp.int32, (width, width), 0)
+            query_pos = block * width + lax.broadcasted_iota(jnp.int32, (width, width), 1)
+            scores = jnp.where(
+                (key_pos >= start_ref[:, rows]) & (key_pos <= query_pos), scores, -1e30
+            )
+        prob = jnp.exp(scores - lse_ref[0, :, rows])
+        gv_ref[key_rows, :] += jnp.dot(
+            prob.astype(jnp.bfloat16), g_ref[0, rows, :], preferred_element_type=jnp.float32
+        )
+        grad_prob = jnp.dot(
+            v_ref[key_rows, :], gt_ref[0, :, rows], preferred_element_type=jnp.float32
+        )
+        grad_scores = (prob * (grad_prob - delta_ref[0, :, rows])).astype(jnp.bfloat16)
+        gk_ref[key_rows, :] += jnp.dot(
+            grad_scores, q_ref[0, rows, :], preferred_element_type=jnp.float32
+        )
+        gq_ref[:, rows] += jnp.dot(kt_ref[...], grad_scores, preferred_element_type=jnp.float32)
+
+    query_step(key_block, True)
+
+    @pl.loop(key_block + 1, blocks)
+    def _(block):
+        @pl.when((low_ref[block] <= key_block) & (mid_ref[block] > key_block))
+        def _():
+            query_step(block, True)
+
+        @pl.when(mid_ref[block] <= key_block)
+        def _():
+            query_step(block, False)
+
+
+def attend_back(
+    query_t, query, grad_t, grad, key_rows, value_rows, key_t, start_row, lse, delta, low, mid, width
+):
+    heads, double, length = query_t.shape
+    size = HEAD_SIZE
+    group = heads // (key_t.shape[0] // size)
+    blocks = length // width
+    row_spec = pl.BlockSpec((1, 1, length), lambda h, j, *_: (h, 0, 0))
+    turned = pl.BlockSpec((1, double, length), lambda h, j, *_: (h, 0, 0))
+    straight = pl.BlockSpec((1, length, double), lambda h, j, *_: (h, 0, 0))
+    whole = pl.BlockSpec((length, double), lambda h, j, *_: (0, 0))
+    return pl.pallas_call(
+        attend_back_kernel,
+        grid_spec=pltpu.PrefetchScalarGridSpec(
+            num_scalar_prefetch=2,
+            grid=(heads, blocks),
+            in_specs=[
+                turned,
+                straight,
+                turned,
+                straight,
+                whole,
+                whole,
+                pl.BlockSpec((size, width), lambda h, j, *_: (h // group, j)),
+                pl.BlockSpec((1, length), lambda h, j, *_: (0, 0)),
+                row_spec,
+                row_spec,
+            ],
+            out_specs=[
+                pl.BlockSpec((size, length), lambda h, j, *_: (h, 0)),
+                whole,
+                whole,
+            ],
+        ),
+        out_shape=[
+            jax.ShapeDtypeStruct((heads * size, length), jnp.float32),
+            jax.ShapeDtypeStruct((length, double), jnp.float32),
+            jax.ShapeDtypeStruct((length, double), jnp.float32),
+        ],
+        compiler_params=pltpu.CompilerParams(vmem_limit_bytes=VMEM_BYTES),
+        cost_estimate=pl.CostEstimate(
+            flops=10 * heads * length * length * double,
+            bytes_accessed=16 * heads * length * double,
+            transcendentals=heads * length * length // 2,
+        ),
+        name="attend_back",
+    )(
+        low,
+        mid,
+        query_t,
+        query,
+        grad_t,
+        grad,
+        key_rows,
+        value_rows,
+        key_t,
+        start_row,
+        lse,
+        delta,
+    )
+
+
+def expert_kernel(me_ref, x_ref, g_ref, own_ref, other_ref, spread_ref, gather_ref, *refs):
+    out_ref, gx_ref, h_ref, dg_ref, du_ref, out_acc, gx_acc, gg_acc = refs[-8:]
+    step = pl.program_id(0)
+    me = me_ref[0]
+    model_width = g_ref.shape[-1]
+    rows = x_ref.shape[0]
+    half = own_ref.shape[2]
+    piece = math.gcd(rows, 256)
+
+    @pl.when(step == 0)
+    def _():
+        out_acc[...] = jnp.zeros_like(out_acc)
+        gx_acc[...] = jnp.zeros_like(gx_acc)
+        gg_acc[...] = jnp.zeros_like(gg_acc)
+
+    def block(number):
+        return pl.ds(pl.multiple_of(number * half, half), half)
+
+    near, far = block(me), block(1 - me)
+    for first in range(0, rows, piece):
+        part = slice(first, first + piece)
+        near_x, far_x = x_ref[part, near], x_ref[part, far]
+        gates = x_ref[part, model_width:]
+        grads = g_ref[0, part, :]
+        for place, number, w_ref in ((near, me, own_ref), (far, 1 - me, other_ref)):
+            down_w = w_ref[0, 2]
+            share = matrix_multiply(gates, spread_ref[number])
+            gate_val = matrix_multiply(near_x, own_ref[0, 0, :, place]) + matrix_multiply(
+                far_x, other_ref[0, 0, :, place]
+            )
+            up_val = matrix_multiply(near_x, own_ref[0, 1, :, place]) + matrix_multiply(
+                far_x, other_ref[0, 1, :, place]
+            )
+            grad_val = contract_last(grads, down_w)
+            sig = jax.nn.sigmoid(gate_val)
+            swish = gate_val * sig
+            plain = swish * up_val
+            active = (plain * share).astype(jnp.bfloat16)
+            grad_share = grad_val * share
+            grad_up = (grad_share * swish).astype(jnp.bfloat16)
+            grad_gate = (grad_share * up_val * (sig + swish * (1.0 - sig))).astype(jnp.bfloat16)
+            product = (plain * grad_val).astype(jnp.bfloat16)
+            h_ref[0, part, place] = active
+            dg_ref[0, part, place] = grad_gate
+            du_ref[0, part, place] = grad_up
+            gg_acc[part, :] += matrix_multiply(product, gather_ref[number])
+            out_acc[part, :] += matrix_multiply(active, down_w)
+            for columns, from_ref in ((near, own_ref), (far, other_ref)):
+                gx_acc[part, columns] += contract_last(
+                    grad_gate, from_ref[0, 0, :, place]
+                ) + contract_last(grad_up, from_ref[0, 1, :, place])
+
+    @pl.when(step == pl.num_programs(0) - 1)
+    def _():
+        out_ref[...] = out_acc[...].astype(jnp.bfloat16)
+        gx_ref[:, :model_width] = gx_acc[...].astype(jnp.bfloat16)
+        gx_ref[:, model_width:] = gg_acc[...].astype(jnp.bfloat16)
+
+
+def expert_chunk(index, me, tokens, grads, own, other, spread, gather, kept):
+    rows, wide = tokens.shape
+    chunks, _, model_width = grads.shape
+    parts, kinds, half, inner = own.shape
+    extra = wide - model_width
+    saved = jax.ShapeDtypeStruct((chunks, rows, parts * inner), jnp.bfloat16)
+    saved_spec = pl.BlockSpec((1, rows, inner), lambda s, *_: (index, 0, s))
+    weight_spec = pl.BlockSpec((1, kinds, half, inner), lambda s, *_: (s, 0, 0, 0))
+    extra_in = [] if kept is None else list(kept)
+    return pl.pallas_call(
+        expert_kernel,
+        grid_spec=pltpu.PrefetchScalarGridSpec(
+            num_scalar_prefetch=1,
+            grid=(parts,),
+            in_specs=[
+                pl.BlockSpec((rows, wide), lambda s, *_: (0, 0)),
+                pl.BlockSpec((1, rows, model_width), lambda s, *_: (index, 0, 0)),
+                weight_spec,
+                weight_spec,
+                pl.BlockSpec(spread.shape, lambda s, *_: (0, 0, 0)),
+                pl.BlockSpec(gather.shape, lambda s, *_: (0, 0, 0)),
+            ]
+            + [pl.BlockSpec(memory_space=pl.ANY)] * len(extra_in),
+            out_specs=[
+                pl.BlockSpec((rows, model_width), lambda s, *_: (0, 0)),
+                pl.BlockSpec((rows, wide), lambda s, *_: (0, 0)),
+                saved_spec,
+                saved_spec,
+                saved_spec,
+            ],
+            scratch_shapes=[
+                pltpu.VMEM((rows, model_width), jnp.float32),
+                pltpu.VMEM((rows, model_width), jnp.float32),
+                pltpu.VMEM((rows, extra), jnp.float32),
+            ],
+        ),
+        out_shape=[
+            jax.ShapeDtypeStruct((rows, model_width), jnp.bfloat16),
+            jax.ShapeDtypeStruct((rows, wide), jnp.bfloat16),
+            saved,
+            saved,
+            saved,
+        ],
+        input_output_aliases={7 + n: 2 + n for n in range(len(extra_in))},
+        compiler_params=pltpu.CompilerParams(vmem_limit_bytes=VMEM_BYTES),
+        cost_estimate=pl.CostEstimate(
+            flops=12 * rows * model_width * parts * inner,
+            bytes_accessed=6 * model_width * parts * inner + 6 * rows * parts * inner,
+            transcendentals=rows * parts * inner,
+        ),
+        name="expert_chunk",
+    )(me, tokens, grads, own, other, spread, gather, *extra_in)
+
+
+def turned_heads(values, cosine, sine):
+    halfway = cosine.shape[0]
+    pieces = []
+    for first in range(0, values.shape[0], 2 * halfway):
+        front = values[first : first + halfway]
+        back = values[first + halfway : first + 2 * halfway]
+        pieces += [front * cosine - back * sine, back * cosine + front * sine]
+    return pieces
+
+
+def join_pieces(me, pieces, rows_ref):
+    quarter, half = pieces[0].shape
+    for number, piece in enumerate(pieces):
+        place = pl.multiple_of((me ^ (number // 2)) * quarter, quarter)
+        columns = slice(number % 2 * half, (number % 2 + 1) * half)
+        rows_ref[pl.ds(place, quarter), columns] = piece[...]
+
+
+def split_pieces(me, rows_ref, pieces):
+    quarter, half = pieces[0].shape
+    for number, piece in enumerate(pieces):
+        place = pl.multiple_of((me ^ (number // 2)) * quarter, quarter)
+        columns = slice(number % 2 * half, (number % 2 + 1) * half)
+        piece[...] = rows_ref[pl.ds(place, quarter), columns]
+
+
+def piece_specs(pieces, quarter, half):
+    return [pl.BlockSpec((quarter, half), lambda i, *_: (i, 0))] * pieces
+
+
+def project_kernel(me_ref, wt_ref, cos_ref, sin_ref, *refs):
+    pieces, (qt_ref, q_ref, kt_ref, k_ref, vt_ref, v_ref, rows_ref) = refs[:-7], refs[-7:]
+    heads, kv_width, width = qt_ref.shape
+    group = heads * HEAD_SIZE // kv_width
+    query_width = heads * HEAD_SIZE
+    join_pieces(me_ref[0], pieces, rows_ref)
+    lin = contract_last(wt_ref[...], rows_ref[...])
+    cosine, sine = cos_ref[...], sin_ref[...]
+    scale = HEAD_SIZE ** (-0.5)
+    for head in range(heads):
+        base = head * HEAD_SIZE
+        own = jnp.concatenate(
+            turned_heads(lin[base : base + HEAD_SIZE], cosine * scale, sine * scale), axis=0
+        )
+        empty = jnp.zeros_like(own)
+        padded = jnp.concatenate(
+            [own if part == head // group else empty for part in range(kv_width // HEAD_SIZE)],
+            axis=0,
+        )
+        qt_ref[head] = padded.astype(jnp.bfloat16)
+        q_ref[head] = padded.T.astype(jnp.bfloat16)
+    keys = jnp.concatenate(
+        turned_heads(lin[query_width : query_width + kv_width], cosine, sine), axis=0
+    )
+    kt_ref[...] = keys.astype(jnp.bfloat16)
+    k_ref[...] = keys.T.astype(jnp.bfloat16)
+    values = lin[query_width + kv_width :]
+    vt_ref[...] = values.astype(jnp.bfloat16)
+    v_ref[...] = values.T.astype(jnp.bfloat16)
+
+
+def project(me, pieces, weights_t, cosine, sine, heads, kv_width, quarter):
+    rows, half = pieces[0].shape
+    model_width = weights_t.shape[1]
+    width = len(pieces) // 2 * quarter
+    blocks = rows // quarter
+    length = blocks * width
+    halfway = cosine.shape[0]
+    bf16 = jnp.bfloat16
+    along = pl.BlockSpec((kv_width, width), lambda i, *_: (0, i))
+    down = pl.BlockSpec((width, kv_width), lambda i, *_: (i, 0))
+    table = pl.BlockSpec((halfway, width), lambda i, *_: (0, i))
+    return pl.pallas_call(
+        project_kernel,
+        grid_spec=pltpu.PrefetchScalarGridSpec(
+        num_scalar_prefetch=1,
+        grid=(blocks,),
+        in_specs=[
+            pl.BlockSpec(weights_t.shape, lambda i, *_: (0, 0)),
+            table,
+            table,
+        ] + piece_specs(len(pieces), quarter, half),
+        out_specs=[
+            pl.BlockSpec((heads, kv_width, width), lambda i, *_: (0, 0, i)),
+            pl.BlockSpec((heads, width, kv_width), lambda i, *_: (0, i, 0)),
+            along,
+            down,
+            along,
+            down,
+        ],
+        scratch_shapes=[pltpu.VMEM((width, model_width), bf16)],
+        ),
+        out_shape=[
+            jax.ShapeDtypeStruct((heads, kv_width, length), bf16),
+            jax.ShapeDtypeStruct((heads, length, kv_width), bf16),
+            jax.ShapeDtypeStruct((kv_width, length), bf16),
+            jax.ShapeDtypeStruct((length, kv_width), bf16),
+            jax.ShapeDtypeStruct((kv_width, length), bf16),
+            jax.ShapeDtypeStruct((length, kv_width), bf16),
+        ],
+        compiler_params=pltpu.CompilerParams(vmem_limit_bytes=VMEM_BYTES),
+        cost_estimate=pl.CostEstimate(
+            flops=2 * length * model_width * weights_t.shape[0],
+            bytes_accessed=2 * length * (model_width + 12 * kv_width),
+            transcendentals=0,
+        ),
+        name="project",
+    )(me, weights_t, cosine, sine, *pieces)
+
+
+def mix_kernel(me_ref, attn_ref, w_ref, *refs):
+    pieces, rows_ref = refs[:-1], refs[-1]
+    rows = attn_ref[...].astype(jnp.float32).T.astype(jnp.bfloat16)
+    rows_ref[...] = matrix_multiply(rows, w_ref[...]).astype(jnp.bfloat16)
+    split_pieces(me_ref[0], rows_ref, pieces)
+
+
+def mix_heads(me, attn_t, w_out, parts, quarter):
+    query_width, length = attn_t.shape
+    model_width = w_out.shape[1]
+    width = parts * quarter
+    blocks = length // width
+    half = model_width // 2
+    return pl.pallas_call(
+        mix_kernel,
+        grid_spec=pltpu.PrefetchScalarGridSpec(
+            num_scalar_prefetch=1,
+            grid=(blocks,),
+            in_specs=[
+                pl.BlockSpec((query_width, width), lambda i, *_: (0, i)),
+                pl.BlockSpec((query_width, model_width), lambda i, *_: (0, 0)),
+            ],
+            out_specs=piece_specs(2 * parts, quarter, half),
+            scratch_shapes=[pltpu.VMEM((width, model_width), jnp.bfloat16)],
+        ),
+        out_shape=[jax.ShapeDtypeStruct((blocks * quarter, half), jnp.bfloat16)] * (2 * parts),
+        compiler_params=pltpu.CompilerParams(vmem_limit_bytes=VMEM_BYTES),
+        cost_estimate=pl.CostEstimate(
+            flops=2 * length * model_width * query_width,
+            bytes_accessed=2 * length * (model_width + query_width),
+            transcendentals=0,
+        ),
+        name="mix_heads",
+    )(me, attn_t, w_out)
+
+
+def unmix_kernel(me_ref, w_ref, attn_ref, *refs):
+    pieces, (gt_ref, g_ref, delta_ref, gw_ref, rows_ref) = refs[:-5], refs[-5:]
+    heads, kv_width, width = gt_ref.shape
+    group = heads * HEAD_SIZE // kv_width
+    join_pieces(me_ref[0], pieces, rows_ref)
+    rows = rows_ref[...]
+    attn = attn_ref[...]
+
+    @pl.when(pl.program_id(0) == 0)
+    def _():
+        gw_ref[...] = jnp.zeros_like(gw_ref)
+
+    gw_ref[...] += matrix_multiply(attn, rows)
+    vec = contract_last(w_ref[...], rows).astype(jnp.bfloat16).astype(jnp.float32)
+    product = vec * attn.astype(jnp.float32)
+    for head in range(heads):
+        base = head * HEAD_SIZE
+        own = vec[base : base + HEAD_SIZE]
+        delta_ref[head] = jnp.sum(product[base : base + HEAD_SIZE], axis=0, keepdims=True)
+        empty = jnp.zeros_like(own)
+        padded = jnp.concatenate(
+            [own if part == head // group else empty for part in range(kv_width // HEAD_SIZE)],
+            axis=0,
+        )
+        gt_ref[head] = padded.astype(jnp.bfloat16)
+        g_ref[head] = padded.T.astype(jnp.bfloat16)
+
+
+def unmix_heads(me, pieces, w_out, attn_t, kv_width, quarter):
+    rows, half = pieces[0].shape
+    query_width, length = attn_t.shape
+    model_width = w_out.shape[1]
+    heads = query_width // HEAD_SIZE
+    width = len(pieces) // 2 * quarter
+    return pl.pallas_call(
+        unmix_kernel,
+        grid_spec=pltpu.PrefetchScalarGridSpec(
+        num_scalar_prefetch=1,
+        grid=(length // width,),
+        in_specs=[
+            pl.BlockSpec((query_width, model_width), lambda i, *_: (0, 0)),
+            pl.BlockSpec((query_width, width), lambda i, *_: (0, i)),
+        ] + piece_specs(len(pieces), quarter, half),
+        out_specs=[
+            pl.BlockSpec((heads, kv_width, width), lambda i, *_: (0, 0, i)),
+            pl.BlockSpec((heads, width, kv_width), lambda i, *_: (0, i, 0)),
+            pl.BlockSpec((heads, 1, width), lambda i, *_: (0, 0, i)),
+            pl.BlockSpec((query_width, model_width), lambda i, *_: (0, 0)),
+        ],
+        scratch_shapes=[pltpu.VMEM((width, model_width), jnp.bfloat16)],
+        ),
+        out_shape=[
+            jax.ShapeDtypeStruct((heads, kv_width, length), jnp.bfloat16),
+            jax.ShapeDtypeStruct((heads, length, kv_width), jnp.bfloat16),
+            jax.ShapeDtypeStruct((heads, 1, length), jnp.float32),
+            jax.ShapeDtypeStruct((query_width, model_width), jnp.float32),
+        ],
+        compiler_params=pltpu.CompilerParams(vmem_limit_bytes=VMEM_BYTES),
+        cost_estimate=pl.CostEstimate(
+            flops=4 * length * model_width * query_width,
+            bytes_accessed=2 * length * (model_width + 5 * query_width),
+            transcendentals=0,
+        ),
+        name="unmix_heads",
+    )(me, w_out, attn_t, *pieces)
+
+
+def unproject_kernel(me_ref, gq_ref, gk_ref, gv_ref, cos_ref, sin_ref, wt_ref, *refs):
+    count = (len(refs) - 2) // 2
+    pieces, gw_ref, results, rows_ref = refs[:count], refs[count], refs[count + 1 : -1], refs[-1]
+    width = gq_ref.shape[1]
+    cosine, sine = cos_ref[...], -sin_ref[...]
+    scale = HEAD_SIZE ** (-0.5)
+    grads = jnp.concatenate(
+        turned_heads(gq_ref[...], cosine * scale, sine * scale)
+        + turned_heads(gk_ref[...].T, cosine, sine)
+        + [gv_ref[...].T],
+        axis=0,
+    )
+    join_pieces(me_ref[0], pieces, rows_ref)
+
+    @pl.when(pl.program_id(0) == 0)
+    def _():
+        gw_ref[...] = jnp.zeros_like(gw_ref)
+
+    gw_ref[...] += matrix_multiply(grads.astype(jnp.bfloat16), rows_ref[...])
+    out = matrix_multiply(grads.T.astype(jnp.bfloat16), wt_ref[...])
+    rows_ref[...] = out.astype(jnp.bfloat16)
+    split_pieces(me_ref[0], rows_ref, results)
+
+
+def unproject(me, grad_query_t, grad_key, grad_value, cosine, sine, pieces, weights_t, quarter):
+    rows, half = pieces[0].shape
+    model_width = weights_t.shape[1]
+    query_width, length = grad_query_t.shape
+    kv_width = grad_key.shape[1]
+    width = len(pieces) // 2 * quarter
+    halfway = cosine.shape[0]
+    table = pl.BlockSpec((halfway, width), lambda i, *_: (0, i))
+    down = pl.BlockSpec((width, kv_width), lambda i, *_: (i, 0))
+    parts = piece_specs(len(pieces), quarter, half)
+    whole = pl.BlockSpec(weights_t.shape, lambda i, *_: (0, 0))
+    return pl.pallas_call(
+        unproject_kernel,
+        grid_spec=pltpu.PrefetchScalarGridSpec(
+        num_scalar_prefetch=1,
+        grid=(length // width,),
+        in_specs=[
+            pl.BlockSpec((query_width, width), lambda i, *_: (0, i)),
+            down,
+            down,
+            table,
+            table,
+            whole,
+        ] + parts,
+        out_specs=[whole] + parts,
+        scratch_shapes=[pltpu.VMEM((width, model_width), jnp.bfloat16)],
+        ),
+        out_shape=[jax.ShapeDtypeStruct(weights_t.shape, jnp.float32)]
+        + [jax.ShapeDtypeStruct((rows, half), jnp.bfloat16)] * len(pieces),
+        compiler_params=pltpu.CompilerParams(vmem_limit_bytes=VMEM_BYTES),
+        cost_estimate=pl.CostEstimate(
+            flops=4 * length * model_width * weights_t.shape[0],
+            bytes_accessed=4 * length * model_width + 4 * length * weights_t.shape[0],
+            transcendentals=0,
+        ),
+        name="unproject",
+    )(me, grad_query_t, grad_key, grad_value, cosine, sine, weights_t, *pieces)
+
+
+def swap(values, axis_name, distance):
+    count = lax.axis_size(axis_name)
+    return lax.ppermute(values, axis_name, [(source, source ^ distance) for source in range(count)])
+
+
+def after(values, *earlier):
+    return lax.optimization_barrier((values, *earlier))[0]
+
+
+def gather_halves(first, second):
+    first_1, second_2 = swap(first, "tp", 1), swap(second, "tp", 2)
+    first_2, second_1 = swap(first, "tp", 2), swap(second, "tp", 1)
+    first_3, second_3 = swap(first_1, "tp", 2), swap(second_2, "tp", 1)
+    return [first, second, first_1, second_1, first_2, second_2, first_3, second_3]
+
+
+def add_low(left_side, right_side):
+    return (left_side.astype(jnp.float32) + right_side.astype(jnp.float32)).astype(jnp.bfloat16)
+
+
+def reduce_halves(pieces):
+    first, second = pieces[0::2], pieces[1::2]
+    first_3, second_3 = swap(first[3], "tp", 1), swap(second[3], "tp", 2)
+    first_1, second_2 = swap(first[1], "tp", 1), swap(second[2], "tp", 2)
+    first_2 = swap(add_low(first[2], first_3), "tp", 2)
+    second_1 = swap(add_low(second[1], second_3), "tp", 1)
+    return [
+        sum(part.astype(jnp.float32) for part in parts)
+        for parts in ((first[0], first_1, first_2), (second[0], second_2, second_1))
+    ]
+
+
+def exchange_parts(values, axis_name):
+    me, count = lax.axis_index(axis_name), lax.axis_size(axis_name)
+    return [
+        shift_by(
+            lax.dynamic_index_in_dim(values, (me + distance) % count, 0, False), axis_name, distance
+        )
+        if distance
+        else lax.dynamic_index_in_dim(values, me, 0, False)
+        for distance in range(count)
+    ]
+
+
+def in_order(parts, axis_name):
+    me, count = lax.axis_index(axis_name), lax.axis_size(axis_name)
+    stacked = jnp.stack(parts)
+    return jnp.stack(
+        [
+            lax.dynamic_index_in_dim(stacked, (me - index) % count, 0, False)
+            for index in range(count)
+        ]
+    )
+
+
+def per_device_by_sequence(
+    hidden_in,
+    cotangent,
+    segment_ids,
+    expert_routes,
+    attn_gain,
+    w_query,
+    key_projection_weight,
+    value_projection_weight,
+    w_out,
+    moe_gain,
+    w_router,
+    w_gate,
+    w_up,
+    w_down,
+):
+    seq_count, slice_rows, model_width = hidden_in.shape
+    top_count = expert_routes.shape[2]
+    expert_count = w_router.shape[1]
+    seq_length = segment_ids.shape[1]
+    query_width, kv_width = w_query.shape[1], key_projection_weight.shape[1]
+    heads = query_width // HEAD_SIZE
+    ep_count, tp_count = lax.axis_size("ep"), lax.axis_size("tp")
+    dp_index, ep_index, tp_index = (lax.axis_index(name) for name in ("dp", "ep", "tp"))
+    quarter = slice_rows // tp_count
+    mine = ep_count * quarter
+    experts_here, _, hidden_here = w_gate.shape
+    inner = experts_here * hidden_here
+    halfway = HEAD_SIZE // 2
+    half = model_width // 2
+    tp_me, dp_me = tp_index.reshape(1), dp_index.reshape(1)
+
+    hidden_parts = exchange_parts(take_part(hidden_in, tp_index, quarter, 1), "ep")
+    hidden_mine = in_order(hidden_parts, "ep").reshape(mine, model_width)
+    routes_mine = in_order(
+        exchange_parts(take_part(expert_routes, tp_index, quarter, 1), "ep"), "ep"
+    ).reshape(mine, top_count)
+
+    hidden = hidden_mine.astype(jnp.float32)
+    gain_first = attn_gain.astype(jnp.float32)
+    factor_first = inverse_rms(hidden)
+    normed_first = hidden * factor_first
+    first_mine = (normed_first * gain_first).astype(jnp.bfloat16)
+    first_rows = gather_halves(first_mine[:, :half], first_mine[:, half:])
+
+    gathered = []
+    for number, weight in enumerate(
+        (
+            jnp.transpose(w_gate, (1, 0, 2)).reshape(model_width, inner),
+            jnp.transpose(w_up, (1, 0, 2)).reshape(model_width, inner),
+            w_down.reshape(inner, model_width),
+        )
+    ):
+        part = take_part(weight, dp_index, half, 0)
+        if number:
+            part = after(part, first_rows[6], first_rows[7])
+        pieces = gather_halves(part[:, : inner // 2], part[:, inner // 2 :])
+        gathered.append(
+            jnp.stack(
+                [jnp.concatenate(pieces[2 * n : 2 * n + 2], axis=1) for n in range(tp_count)]
+            )
+        )
+    own_weights = jnp.stack(gathered, axis=1)
+    other_weights = swap(own_weights, "dp", 1)
+
+    grads_mine_all = after(take_part(cotangent, tp_index, quarter, 1), hidden_mine)
+    grads_all = in_order(
+        [grads_mine_all]
+        + [shift_by(grads_mine_all, "ep", distance) for distance in range(1, ep_count)],
+        "ep",
+    )
+    chunk_grads = jnp.stack(
+        [
+            lax.dynamic_index_in_dim(grads_all, (ep_index + step) % ep_count, 1, False)
+            for step in range(ep_count)
+        ]
+    ).reshape(ep_count, mine, model_width)
+
+    weights_t = jnp.concatenate([w_query, key_projection_weight, value_projection_weight], axis=1).T
+    inverse = 1.0 / 10000.0 ** (jnp.arange(halfway, dtype=jnp.float32) * 2.0 / HEAD_SIZE)
+    angles = inverse[:, None] * jnp.arange(seq_length, dtype=jnp.float32)[None, :]
+    cosine, sine = jnp.cos(angles), jnp.sin(angles)
+    query_t, query, key_t, key_rows, value_t, value_rows = project(
+        tp_me, first_rows, weights_t, cosine, sine, heads, kv_width, quarter
+    )
+
+    block = math.gcd(seq_length, 512)
+    segments = lax.dynamic_index_in_dim(segment_ids, ep_index, 0, False)
+    starts = jnp.sum((segments[None, :] < segments[:, None]).astype(jnp.int32), axis=1)
+    low = starts[::block] // block
+    mid = (starts[block - 1 :: block] + block - 1) // block
+    start_row = starts[None, :]
+    attn_t, lse = attend(query_t, key_rows, value_t, start_row, low, mid, block)
+
+    attn_out = jnp.concatenate(
+        reduce_halves(mix_heads(tp_me, attn_t, w_out, tp_count, quarter)), axis=1
+    )
+    middle = hidden + attn_out
+    gain_second = moe_gain.astype(jnp.float32)
+    factor_second = inverse_rms(middle)
+    normed_second = middle * factor_second
+    second_in = (normed_second * gain_second).astype(jnp.bfloat16)
+    logits = matrix_multiply(second_in, w_router)
+    chosen = (
+        routes_mine[:, :, None] == jnp.arange(expert_count, dtype=jnp.int32)[None, None, :]
+    ).astype(jnp.float32)
+    picked = jnp.sum(chosen * logits[:, None, :], axis=-1)
+    gates = jnp.sum(chosen * jax.nn.softmax(picked, axis=-1)[:, :, None], axis=1)
+    gates_high = lax.reduce_precision(gates, 8, 7)
+    lanes = -(-2 * expert_count // 128) * 128
+    tokens = jnp.concatenate(
+        [
+            second_in,
+            gates_high.astype(jnp.bfloat16),
+            (gates - gates_high).astype(jnp.bfloat16),
+            jnp.zeros((mine, lanes - 2 * expert_count), jnp.bfloat16),
+        ],
+        axis=1,
+    )
+
+    columns = jnp.arange(inner, dtype=jnp.int32).reshape(2, inner // 2)
+    expert_of = ep_index * experts_here + columns // hidden_here
+    lane = jnp.arange(lanes, dtype=jnp.int32)
+    gather = (expert_of[:, :, None] == lane).astype(jnp.bfloat16)
+    spread = (
+        (lane[None, :, None] < 2 * expert_count)
+        & (lane[None, :, None] % expert_count == expert_of[:, None, :])
+    ).astype(jnp.bfloat16)
+    order = [0] + [n for n in range(1, ep_count) if n % 2] + [n for n in range(1, ep_count) if n % 2 == 0]
+    chunk_tokens = {0: tokens}
+    previous = tokens
+    for step in order[1:]:
+        chunk_tokens[step] = previous = shift_by(after(tokens, previous), "ep", -step)
+    kept = None
+    out_parts, grad_parts = [], []
+    for step in order:
+        out_part, grad_part, *kept = expert_chunk(
+            step,
+            dp_me,
+            chunk_tokens[step],
+            chunk_grads,
+            own_weights,
+            other_weights,
+            spread,
+            gather,
+            kept,
+        )
+        out_parts.append(shift_by(out_part, "ep", step) if step else out_part)
+        grad_parts.append(shift_by(grad_part, "ep", step) if step else grad_part)
+    grad_sum = sum(part.astype(jnp.float32) for part in grad_parts)
+
+    active, grad_gate, grad_up = [part.reshape(ep_count * mine, tp_count * inner) for part in kept]
+
+    def token_half(number):
+        return jnp.concatenate(
+            [take_part(chunk_tokens[step], number, half, 1) for step in range(ep_count)], axis=0
+        )
+
+    def grads_half(number):
+        return take_part(chunk_grads.reshape(ep_count * mine, model_width), number, half, 1)
+
+    def low_product(left_side, right_side):
+        return contract_rows(left_side, right_side).astype(jnp.bfloat16)
+
+    far_tokens, far_grads = token_half(1 - dp_index), grads_half(1 - dp_index)
+    far_sums = [
+        swap(part, "dp", 1)
+        for part in (
+            low_product(far_tokens, grad_gate),
+            low_product(far_tokens, grad_up),
+            low_product(active, far_grads),
+        )
+    ]
+    near_tokens, near_grads = token_half(dp_index), grads_half(dp_index)
+    near_sums = [
+        low_product(near_tokens, grad_gate),
+        low_product(near_tokens, grad_up),
+        low_product(active, near_grads),
+    ]
+    gate_sum, up_sum, down_sum = [add_low(*pair) for pair in zip(near_sums, far_sums)]
+    cut = inner // 2
+
+    def columns_home(total):
+        pieces = [total[:, n * cut : (n + 1) * cut] for n in range(2 * tp_count)]
+        home = jnp.concatenate(reduce_halves(pieces), axis=1)
+        return jnp.swapaxes(home.reshape(half, experts_here, hidden_here), 0, 1)
+
+    gate_out, up_out = columns_home(gate_sum), columns_home(up_sum)
+    down_out = jnp.concatenate(
+        reduce_halves([down_sum[n * cut : (n + 1) * cut] for n in range(2 * tp_count)]), axis=0
+    ).reshape(experts_here, hidden_here, half)
+
+    grad_gates = grad_sum[:, model_width : model_width + expert_count]
+    grad_logits = (
+        gates * (grad_gates - jnp.sum(gates * grad_gates, axis=-1, keepdims=True))
+    ).astype(jnp.bfloat16)
+    grad_router = contract_rows(second_in, grad_logits)
+    grad_second = grad_sum[:, :model_width] + contract_last(grad_logits, w_router)
+    grad_moe_gain = jnp.sum(grad_second * normed_second, axis=0)
+    grad_middle = chunk_grads[0].astype(jnp.float32) + norm_back(
+        grad_second, normed_second, factor_second, gain_second
+    )
+    grad_low = grad_middle.astype(jnp.bfloat16)
+    grad_attn = gather_halves(grad_low[:, :half], grad_low[:, half:])
+    grad_vec_t, grad_vec, delta, grad_wo = unmix_heads(
+        tp_me, grad_attn, w_out, attn_t, kv_width, quarter
+    )
+    grad_query_t, grad_key, grad_value = attend_back(
+        query_t,
+        query,
+        grad_vec_t,
+        grad_vec,
+        key_rows,
+        value_rows,
+        key_t,
+        start_row,
+        lse,
+        delta,
+        low,
+        mid,
+        block,
+    )
+    grad_qkv_t, *first_parts = unproject(
+        tp_me, grad_query_t, grad_key, grad_value, cosine, sine, first_rows, weights_t, quarter
+    )
+    grad_first = jnp.concatenate(reduce_halves(first_parts), axis=1)
+    grad_attn_gain = jnp.sum(grad_first * normed_first, axis=0)
+    grad_mine = grad_middle + norm_back(grad_first, normed_first, factor_first, gain_first)
+
+    def rows_home(rows):
+        parts = exchange_parts(rows.astype(jnp.bfloat16).reshape(ep_count, quarter, model_width), "ep")
+        return in_order(parts, "ep")
+
+    def by_quarter(stacked):
+        return [
+            lax.dynamic_index_in_dim(stacked, tp_index ^ index, 0, False)
+            for index in range(tp_count)
+        ]
+
+    home = rows_home(grad_mine)
+    home_pieces = gather_halves(home[..., :half], home[..., half:])
+    grad_in = jnp.concatenate(
+        [
+            jnp.concatenate(by_quarter(jnp.stack(home_pieces[side::2])), axis=1)
+            for side in range(2)
+        ],
+        axis=2,
+    ).astype(jnp.float32)
+
+    out_sum = middle + sum(part.astype(jnp.float32) for part in out_parts)
+    out_home = rows_home(out_sum)
+    column = model_width // tp_count
+    block_out = jnp.concatenate(
+        by_quarter(
+            jnp.stack(
+                [
+                    swap(take_part(out_home, tp_index ^ offset, column, 2), "tp", offset)
+                    if offset
+                    else take_part(out_home, tp_index, column, 2)
+                    for offset in range(tp_count)
+                ]
+            )
+        ),
+        axis=1,
+    ).astype(jnp.float32)
+
+    both = ("dp", "ep")
+    qkv_home = lax.psum_scatter(grad_qkv_t, both, scatter_dimension=1, tiled=True).T
+    wo_home = lax.psum_scatter(grad_wo, both, scatter_dimension=1, tiled=True)
+    small = jnp.concatenate([grad_router, grad_moe_gain[:, None], grad_attn_gain[:, None]], axis=1)
+    small_home = lax.psum_scatter(lax.psum(small, "tp"), both, scatter_dimension=0, tiled=True)
+    return (
+        block_out,
+        grad_in,
+        small_home[:, expert_count + 1],
+        qkv_home[:, :query_width],
+        qkv_home[:, query_width : query_width + kv_width],
+        qkv_home[:, query_width + kv_width :],
+        wo_home,
+        small_home[:, expert_count],
+        small_home[:, :expert_count],
+        gate_out,
+        up_out,
+        down_out,
+    )
+
+
+def block_of_device(*arrays):
+    hidden_in, segment_ids, w_gate = arrays[0], arrays[2], arrays[11]
+    dp_count, ep_count, tp_count = (lax.axis_size(name) for name in ("dp", "ep", "tp"))
+    inner = w_gate.shape[0] * w_gate.shape[2]
+    fits = (
+        hidden_in.shape[0] == ep_count
+        and dp_count == 2
+        and tp_count == 4
+        and hidden_in.shape[1] % (tp_count * 128) == 0
+        and segment_ids.shape[1] % 512 == 0
+        and inner == w_gate.shape[1]
+        and inner % 1024 == 0
+    )
+    return (per_device_by_sequence if fits else per_device)(*arrays)
+
 
 def solution(mesh):
     placed = (
@@ -444,7 +1409,7 @@
         P("ep", "tp", None),
     )
     return jax.shard_map(
-        per_device,
+        block_of_device,
         mesh=mesh,
         in_specs=placed,
         out_specs=(

time: 7660 us -> 1250 us (0.16)
  waiting for transfers between devices: 5300 us -> 544 us
  local copies, waits for them, and re-layouts: 1280 us -> 35.2 us
  matrix products: 546 us -> 87.7 us
  other arithmetic: 396 us -> 68.8 us
  Pallas kernels: 0 us -> 267 us
  starting transfers between devices: 53.3 us -> 192 us
    all_to_all x4 -> x0, waiting for transfers between devices: 4890 us -> none  [the longest x1 1380 us: per_device(): lax.all_to_all(grad_send.reshape(ep_count, experts_here, seq_count * capa...]
    gather x2 -> x0, local copies, waits for them, and re-layouts: 613 us -> none  [the longest x1 307 us: per_device(): grad_inputs.reshape(slots_all, model_width)[place_index]]
    ppermute x0 -> x97, waiting for transfers between devices: none -> 544 us  [the longest x24 276 us: shift_by(): lax.ppermute(values, axis_name, [(source, (source + distance) % count) fo...]
    scatter x3 -> x0, local copies, waits for them, and re-layouts: 512 us -> none  [the longest x2 256 us: per_device(): send_rows = jnp.zeros((slots_all, model_width), jnp.bfloat16).at[place_in...]
    dot_general x15 -> x0, matrix products: 495 us -> none  [the longest x1 69.1 us: expert_backward(): jnp.einsum('secf,edf->secd', grad_up_val, up_w, preferred_element_type=jn...]
    pallas_call x0 -> x10, Pallas kernels: none -> 267 us  [the longest x4 160 us: expert_chunk(): pl.pallas_call(expert_kernel, grid_spec=pltpu.PrefetchScalarGridSpec(num_...]
    psum x3 -> x0, waiting for transfers between devices: 246 us -> none  [the longest x1 99.8 us: per_device(): lax.psum(first_part.astype(jnp.bfloat16), 'tp').astype(jnp.float32)]
    ppermute x0 -> x97, starting transfers between devices: none -> 192 us  [the longest x24 122 us: shift_by(): lax.ppermute(values, axis_name, [(source, (source + distance) % count) fo...]
  transfers between devices with their start and end apart: 18 -> 100, of which waited for: 13 -> 45; matrix products, arithmetic and copies ran while one was open for 16% -> 14% of each run, Pallas kernels for 0% -> 13%
where the time goes in v1:
time: 1250 us; the launch traced here: 1230 us
  waiting for transfers between devices  544 us (44%)
  Pallas kernels  267 us (21%)
  starting transfers between devices  192 us (15%)
  matrix products  87.7 us (7%)
  other arithmetic  68.8 us (6%)
  local copies, waits for them, and re-layouts  35.2 us (3%)
  blocking collectives  20.8 us (2%)
  between operations  15.4 us (1%)
    ppermute x24, waiting for transfers between devices, shift_by(): lax.ppermute(values, axis_name, [(source, (source + distance) % count) fo...  276 us
    ppermute x73, waiting for transfers between devices, swap(): lax.ppermute(values, axis_name, [(source, source ^ distance) for source i...  268 us
    pallas_call x4, Pallas kernels, expert_chunk(): pl.pallas_call(expert_kernel, grid_spec=pltpu.PrefetchScalarGridSpec(num_...  160 us
    ppermute x24, starting transfers between devices, shift_by(): lax.ppermute(values, axis_name, [(source, (source + distance) % count) fo...  122 us
    dot_general x7, matrix products, contract_rows(): lax.dot_general(left_side, right_side, (((0,), (0,)), ((), ())), preferre...  86.4 us
    ppermute x73, starting transfers between devices, swap(): lax.ppermute(values, axis_name, [(source, source ^ distance) for source i...  70.6 us
    pallas_call x1, Pallas kernels, attend_back(): pl.pallas_call(attend_back_kernel, grid_spec=pltpu.PrefetchScalarGridSpec...  43.9 us
    pallas_call x1, Pallas kernels, attend(): pl.pallas_call(attend_kernel, grid_spec=pltpu.PrefetchScalarGridSpec(num_...  31.5 us
  transfers between devices with their start and end apart: 100, of which 45 were waited for; matrix products, arithmetic and copies ran while one was open for 14% of the time, Pallas kernels for 13%

profile of v1, /device:TPU:0, one launch (start us, length us, event | category | flops | bytes accessed | tf_op | source)
XLA Modules:
  0.0 1231.3 jit_solution(3278862311335850943)
XLA Ops:
  109.5 11.2 collective-permute-done.30
  199.0 31.5 %attend.1 = (bf16[256,2048]{1,0:T(8,128)(2,1)}, f32[4,1,2048]{2,1,0:T(1,128)}) custom-call(s32[4]{0:T(128)} %get-tuple-element.293.low_ref, s32[4]{0:T(128)} %get-tuple-element.292.mid_ref, bf16[4,128,2048]{2,1,0:T(8,128)(2,1)} %get-tuple-element.70.q_ref.qt_ref, bf16[2048,128]{1,0:T(8,128)(2,1)} %get-tuple-element.71.k_ref, ...), custom_call_target="tpu_custom_call" | custom-call | flops 8589934592 | bytes 8388608 | tf_op jit(solution)/shard_map/attend/pallas_call | solution.py:484
  299.0 39.1 %collective-permute-done.19 = bf16[4,128,1024]{2,1,0:T(8,128)(2,1)} collective-permute-done((bf16[4,128,1024]{2,1,0:T(8,128)(2,1)}, bf16[4,128,1024]{2,1,0:T(8,128)(2,1)}, u32[]{:S(2)}, u32[]{:S(2)}) %collective-permute-start.19) | collective-permute-done | bytes 1048608 | tf_op jit(solution)/shard_map/ppermute | solution.py:437
  342.1 20.2 %collective-permute-done.40.x_ref = bf16[512,1152]{1,0:T(8,128)(2,1)} collective-permute-done((bf16[512,1152]{1,0:T(8,128)(2,1)}, bf16[512,1152]{1,0:T(8,128)(2,1)}, u32[]{:S(2)}, u32[]{:S(2)}) %collective-permute-start.40) | collective-permute-done | bytes 1179680 | tf_op jit(solution)/shard_map/ppermute | solution.py:437
  362.3 48.4 %collective-permute-start.42 = (bf16[512,1152]{1,0:T(8,128)(2,1)S(1)}, bf16[512,1152]{1,0:T(8,128)(2,1)S(1)}, u32[]{:S(2)}, u32[]{:S(2)}) collective-permute-start(bf16[512,1152]{1,0:T(8,128)(2,1)S(1)} %copy-done.10), channel_id=1, source_target_pairs={{0,4},{4,8},{8,12},{12,0},{1,5},{5,9},{9,13},{13,1},{2,6},{6,10},{... | collective-permute-start | bytes 3538952 | tf_op jit(solution)/shard_map/ppermute | solution.py:437
  415.8 19.3 %collective-permute-done.42.x_ref = bf16[512,1152]{1,0:T(8,128)(2,1)S(1)} collective-permute-done((bf16[512,1152]{1,0:T(8,128)(2,1)S(1)}, bf16[512,1152]{1,0:T(8,128)(2,1)S(1)}, u32[]{:S(2)}, u32[]{:S(2)}) %collective-permute-start.42) | collective-permute-done | bytes 1179680 | tf_op jit(solution)/shard_map/ppermute | solution.py:437
  437.4 39.9 %expert_chunk.4 = (bf16[512,1024]{1,0:T(8,128)(2,1)}, bf16[512,1152]{1,0:T(8,128)(2,1)}, bf16[4,512,4096]{2,1,0:T(8,128)(2,1)}, bf16[4,512,4096]{2,1,0:T(8,128)(2,1)}, bf16[4,512,4096]{2,1,0:T(8,128)(2,1)}) custom-call(s32[1]{0:T(128)} %bitcast.12.me_ref, bf16[512,1152]{1,0:T(8,128)(2,1)} %concatenate.93.x_ref, ...), custom_call_target="tpu_custom_call" | custom-call | flops 25769803776 | bytes 37748736 | tf_op jit(solution)/shard_map/expert_chunk/pallas_call | solution.py:715
  477.3 40.3 %expert_chunk.5 = (bf16[512,1024]{1,0:T(8,128)(2,1)}, bf16[512,1152]{1,0:T(8,128)(2,1)}, bf16[4,512,4096]{2,1,0:T(8,128)(2,1)}, bf16[4,512,4096]{2,1,0:T(8,128)(2,1)}, bf16[4,512,4096]{2,1,0:T(8,128)(2,1)}) custom-call(s32[1]{0:T(128)} %bitcast.12.me_ref, ...), custom_call_target="tpu_custom_call", output_to_operand_aliasing={{2}: (7, {}), {3}: (8, {}), {4}: (9, {})} | custom-call | flops 25769803776 | bytes 37748736 | tf_op jit(solution)/shard_map/expert_chunk/pallas_call | solution.py:715
  517.6 40.1 %expert_chunk.6 = (bf16[512,1024]{1,0:T(8,128)(2,1)}, bf16[512,1152]{1,0:T(8,128)(2,1)}, bf16[4,512,4096]{2,1,0:T(8,128)(2,1)}, bf16[4,512,4096]{2,1,0:T(8,128)(2,1)}, bf16[4,512,4096]{2,1,0:T(8,128)(2,1)}) custom-call(s32[1]{0:T(128)} %bitcast.12.me_ref, bf16[512,1152]{1,0:T(8,128)(2,1)} %copy-done.20, ...), custom_call_target="tpu_custom_call", output_to_operand_aliasing={{2}: (7, {}), {3}: (8, {}), {4}: (9, {})} | custom-call | flops 25769803776 | bytes 37748736 | tf_op jit(solution)/shard_map/expert_chunk/pallas_call | solution.py:715
  558.8 40.1 %expert_chunk.7 = (bf16[512,1024]{1,0:T(8,128)(2,1)}, bf16[512,1152]{1,0:T(8,128)(2,1)}, bf16[4,512,4096]{2,1,0:T(8,128)(2,1)}, bf16[4,512,4096]{2,1,0:T(8,128)(2,1)}, bf16[4,512,4096]{2,1,0:T(8,128)(2,1)}) custom-call(s32[1]{0:T(128)} %bitcast.12.me_ref, bf16[512,1152]{1,0:T(8,128)(2,1)} %copy-done.22, ...), custom_call_target="tpu_custom_call", output_to_operand_aliasing={{2}: (7, {}), {3}: (8, {}), {4}: (9, {})} | custom-call | flops 25769803776 | bytes 37748736 | tf_op jit(solution)/shard_map/expert_chunk/pallas_call | solution.py:715
  609.3 88.2 %collective-permute-done.54 = bf16[512,1152]{1,0:T(8,128)(2,1)} collective-permute-done((bf16[512,1152]{1,0:T(8,128)(2,1)}, bf16[512,1152]{1,0:T(8,128)(2,1)}, u32[]{:S(2)}, u32[]{:S(2)}) %collective-permute-start.54) | collective-permute-done | bytes 1179680 | tf_op jit(solution)/shard_map/ppermute | solution.py:437
  701.2 69.1 %collective-permute-done.45 = bf16[512,1024]{1,0:T(8,128)(2,1)S(1)} collective-permute-done((bf16[512,1024]{1,0:T(8,128)(2,1)S(1)}, bf16[512,1024]{1,0:T(8,128)(2,1)S(1)}, u32[]{:S(2)}, u32[]{:S(2)}) %collective-permute-start.45) | collective-permute-done | bytes 1048608 | tf_op jit(solution)/shard_map/ppermute | solution.py:437
  794.1 13.9 %convolution_convert_fusion.5 = bf16[4096,512]{1,0:T(8,128)(2,1)} fusion(bf16[2048,4096]{1,0:T(8,128)(2,1)} %bitcast.243, bf16[2048,1024]{1,0:T(8,128)(2,1)S(1)} %bitcast.219, s32[]{:T(128)S(6)} %select_n.276), kind=kOutput, calls=%fused_computation.10 | convolution fusion | flops 8592031744 | bytes 23068676 | tf_op jit(solution)/shard_map/dot_general | solution.py:22
  820.6 43.9 %attend_back.1 = (f32[256,2048]{1,0:T(8,128)}, f32[2048,128]{1,0:T(8,128)}, f32[2048,128]{1,0:T(8,128)}) custom-call(s32[4]{0:T(128)} %get-tuple-element.293.low_ref, s32[4]{0:T(128)} %get-tuple-element.292.mid_ref, bf16[4,128,2048]{2,1,0:T(8,128)(2,1)} %get-tuple-element.70.q_ref.qt_ref, bf16[4,2048,128]{2,1,0:T(8,128)(2,1)} %get-tuple-element.105.q_ref, ...), custom_call_target="tpu_custom_call" | custom-call | flops 21474836480 | bytes 16777216 | tf_op jit(solution)/shard_map/attend_back/pallas_call | solution.py:596
  874.9 14.6 %convolution_convert_fusion.4 = bf16[4096,512]{1,0:T(8,128)(2,1)} fusion(bf16[2048,4096]{1,0:T(8,128)(2,1)} %bitcast.244, bf16[2048,1024]{1,0:T(8,128)(2,1)} %bitcast.220, s32[]{:T(128)S(6)} %select_n.289), kind=kOutput, calls=%fused_computation.9 | convolution fusion | flops 8592031744 | bytes 23068676 | tf_op jit(solution)/shard_map/dot_general | solution.py:22
  893.6 14.1 %convolution_convert_fusion = bf16[512,4096]{1,0:T(8,128)(2,1)} fusion(bf16[2048,4096]{1,0:T(8,128)(2,1)} %bitcast.247, bf16[512,512]{1,0:T(8,128)(2,1)S(1)} %get-tuple-element.232, bf16[512,512]{1,0:T(8,128)(2,1)S(1)} %get-tuple-element.230, bf16[512,512]{1,0:T(8,128)(2,1)S(1)} %get-tuple-element.228, bf16[512,512]{1,0:T(8,128)(2,1)S(1)} %get-tuple-element.226), kind=kOutput, calls=%fused_computation.5 | convolution fusion | flops 8600420352 | bytes 23068672 | tf_op jit(solution)/shard_map/dot_general | solution.py:22
  929.4 15.0 %convolution_convert_fusion.2 = bf16[512,4096]{1,0:T(8,128)(2,1)} fusion(bf16[2048,4096]{1,0:T(8,128)(2,1)} %bitcast.245, bf16[512,512]{1,0:T(8,128)(2,1)} %copy-done.40, bf16[512,512]{1,0:T(8,128)(2,1)} %copy-done.41, bf16[512,512]{1,0:T(8,128)(2,1)} %copy-done.39, bf16[512,512]{1,0:T(8,128)(2,1)} %copy-done.38), kind=kOutput, calls=%fused_computation.7 | convolution fusion | flops 8600420352 | bytes 23068672 | tf_op jit(solution)/shard_map/dot_general | solution.py:22
  945.3 23.0 %collective-permute-start.46 = (bf16[128,1024]{1,0:T(8,128)(2,1)}, bf16[128,1024]{1,0:T(8,128)(2,1)}, u32[]{:S(2)}, u32[]{:S(2)}) collective-permute-start(bf16[128,1024]{1,0:T(8,128)(2,1)} %get-tuple-element.262), channel_id=1, source_target_pairs={{0,4},{4,8},{8,12},{12,0},{1,5},{5,9},{9,13},{13,1},{2,6},{6,10},{... | collective-permute-start | bytes 786440 | tf_op jit(solution)/shard_map/ppermute | solution.py:437
  973.0 14.6 %convolution_convert_fusion.1 = bf16[512,4096]{1,0:T(8,128)(2,1)} fusion(bf16[2048,4096]{1,0:T(8,128)(2,1)} %bitcast.248, bf16[512,512]{1,0:T(8,128)(2,1)} %get-tuple-element.231, bf16[512,512]{1,0:T(8,128)(2,1)} %get-tuple-element.229, bf16[512,512]{1,0:T(8,128)(2,1)} %get-tuple-element.227, bf16[512,512]{1,0:T(8,128)(2,1)} %get-tuple-element.225), kind=kOutput, calls=%fused_computation.6 | convolution fusion | flops 8600420352 | bytes 23068672 | tf_op jit(solution)/shard_map/dot_general | solution.py:22
  1004.5 13.9 %convolution_convert_fusion.3 = bf16[512,4096]{1,0:T(8,128)(2,1)} fusion(bf16[2048,4096]{1,0:T(8,128)(2,1)} %bitcast.246, bf16[512,512]{1,0:T(8,128)(2,1)S(1)} %copy-done.36, bf16[512,512]{1,0:T(8,128)(2,1)S(1)} %copy-done.37, bf16[512,512]{1,0:T(8,128)(2,1)S(1)} %copy-done.35, bf16[512,512]{1,0:T(8,128)(2,1)S(1)} %copy-done.34), kind=kOutput, calls=%fused_computation.8 | convolution fusion | flops 8600420352 | bytes 23068672 | tf_op jit(solution)/shard_map/dot_general | solution.py:22
  1028.1 16.4 %collective-permute-done.68 = bf16[128,1024]{1,0:T(8,128)(2,1)S(1)} collective-permute-done((bf16[128,1024]{1,0:T(8,128)(2,1)S(1)}, bf16[128,1024]{1,0:T(8,128)(2,1)S(1)}, u32[]{:S(2)}, u32[]{:S(2)}) %collective-permute-start.68) | collective-permute-done | bytes 262176 | tf_op jit(solution)/shard_map/ppermute | solution.py:437
  1049.2 20.8 %psum.8 = f32[128,34]{0,1:T(8,128)S(1)} all-reduce(f32[128,34]{0,1:T(8,128)} %reduce-scatter.8.cloned.1.call-done), channel_id=1, replica_groups=mesh['dp'=2,'ep'=4,'tp'=4] {'tp'}, use_global_device_ids=true, to_apply=%region_12.13 | all-reduce | flops 4352 | bytes 34816 | tf_op jit(solution)/shard_map/psum | solution.py:1361
  1114.7 21.9 %collective-permute-done.85 = bf16[512,512]{1,0:T(8,128)(2,1)S(1)} collective-permute-done((bf16[512,512]{1,0:T(8,128)(2,1)S(1)}, bf16[512,512]{1,0:T(8,128)(2,1)S(1)}, u32[]{:S(2)}, u32[]{:S(2)}) %collective-permute-start.85) | collective-permute-done | bytes 524320 | tf_op jit(solution)/shard_map/ppermute | solution.py:1038
  1138.9 16.8 %collective-permute-done.78 = bf16[512,512]{1,0:T(8,128)(2,1)S(1)} collective-permute-done((bf16[512,512]{1,0:T(8,128)(2,1)S(1)}, bf16[512,512]{1,0:T(8,128)(2,1)S(1)}, u32[]{:S(2)}, u32[]{:S(2)}) %collective-permute-start.78) | collective-permute-done | bytes 524320 | tf_op jit(solution)/shard_map/ppermute | solution.py:1038
  (496 shorter events, 499.4 us)
Async XLA Ops:
  7.2 1042.0 %reduce-scatter.8.cloned.1.call-start = ((), (), s32[]{:S(2)}) async-start(), calls=%async_computation.5 | async-start | bytes 184320 | tf_op jit(solution)/shard_map/reduce_scatter | solution.py:1361
  170.5 266.8 %collective-permute-start.39 = (bf16[4,3,512,1024]{3,2,1,0:T(8,128)(2,1)}, bf16[4,3,512,1024]{3,2,1,0:T(8,128)(2,1)}, u32[]{:S(2)}, u32[]{:S(2)}) collective-permute-start(bf16[4,3,512,1024]{3,2,1,0:T(8,128)(2,1)} %pad_maximum_fusion.own_ref), channel_id=1, source_target_pairs={{0,16},{16,0},{1,17},{17,1},{2,18},{18,2},{3,19},{19,3},{4,20},{20... | collective-permute-start | bytes 37748744 | tf_op jit(solution)/shard_map/ppermute | solution.py:1038
  271.9 66.2 %collective-permute-start.19 = (bf16[4,128,1024]{2,1,0:T(8,128)(2,1)}, bf16[4,128,1024]{2,1,0:T(8,128)(2,1)}, u32[]{:S(2)}, u32[]{:S(2)}) collective-permute-start(bf16[4,128,1024]{2,1,0:T(8,128)(2,1)} %constant_dynamic-slice_fusion.32), channel_id=1, source_target_pairs={{0,8},{4,12},{8,0},{12,4},{1,9},{5,13},{9,1},{13,5},{2,10},{6,14},... | collective-permute-start | bytes 3145736 | tf_op jit(solution)/shard_map/ppermute | solution.py:437
  280.0 59.6 %collective-permute-start.20 = (bf16[4,128,1024]{2,1,0:T(8,128)(2,1)}, bf16[4,128,1024]{2,1,0:T(8,128)(2,1)}, u32[]{:S(2)}, u32[]{:S(2)}) collective-permute-start(bf16[4,128,1024]{2,1,0:T(8,128)(2,1)} %constant_dynamic-slice_fusion.32), channel_id=1, source_target_pairs={{0,12},{4,0},{8,4},{12,8},{1,13},{5,1},{9,5},{13,9},{2,14},{6,2},{... | collective-permute-start | bytes 3145736 | tf_op jit(solution)/shard_map/ppermute | solution.py:437
  288.7 73.6 %collective-permute-start.40 = (bf16[512,1152]{1,0:T(8,128)(2,1)}, bf16[512,1152]{1,0:T(8,128)(2,1)}, u32[]{:S(2)}, u32[]{:S(2)}) collective-permute-start(bf16[512,1152]{1,0:T(8,128)(2,1)} %concatenate.93.x_ref), channel_id=1, source_target_pairs={{0,12},{4,0},{8,4},{12,8},{1,13},{5,1},{9,5},{13,9},{2,14},{6,2},{... | collective-permute-start | bytes 3538952 | tf_op jit(solution)/shard_map/ppermute | solution.py:437
  362.3 72.9 %collective-permute-start.42 = (bf16[512,1152]{1,0:T(8,128)(2,1)S(1)}, bf16[512,1152]{1,0:T(8,128)(2,1)S(1)}, u32[]{:S(2)}, u32[]{:S(2)}) collective-permute-start(bf16[512,1152]{1,0:T(8,128)(2,1)S(1)} %copy-done.10), channel_id=1, source_target_pairs={{0,4},{4,8},{8,12},{12,0},{1,5},{5,9},{9,13},{13,1},{2,6},{6,10},{... | collective-permute-start | bytes 3538952 | tf_op jit(solution)/shard_map/ppermute | solution.py:437
  435.1 122.6 %collective-permute-start.44 = (bf16[512,1152]{1,0:T(8,128)(2,1)S(1)}, bf16[512,1152]{1,0:T(8,128)(2,1)S(1)}, u32[]{:S(2)}, u32[]{:S(2)}) collective-permute-start(bf16[512,1152]{1,0:T(8,128)(2,1)S(1)} %copy-done.10), channel_id=1, source_target_pairs={{0,8},{4,12},{8,0},{12,4},{1,9},{5,13},{9,1},{13,5},{2,10},{6,14},... | collective-permute-start | bytes 3538952 | tf_op jit(solution)/shard_map/ppermute | solution.py:437
  598.9 98.6 %collective-permute-start.54 = (bf16[512,1152]{1,0:T(8,128)(2,1)}, bf16[512,1152]{1,0:T(8,128)(2,1)}, u32[]{:S(2)}, u32[]{:S(2)}) collective-permute-start(bf16[512,1152]{1,0:T(8,128)(2,1)} %get-tuple-element.104), channel_id=1, source_target_pairs={{0,8},{4,12},{8,0},{12,4},{1,9},{5,13},{9,1},{13,5},{2,10},{6,14},... | collective-permute-start | bytes 3538952 | tf_op jit(solution)/shard_map/ppermute | solution.py:437
  600.0 97.5 %collective-permute-start.53 = (bf16[512,1152]{1,0:T(8,128)(2,1)}, bf16[512,1152]{1,0:T(8,128)(2,1)}, u32[]{:S(2)}, u32[]{:S(2)}) collective-permute-start(bf16[512,1152]{1,0:T(8,128)(2,1)} %get-tuple-element.103), channel_id=1, source_target_pairs={{0,12},{4,0},{8,4},{12,8},{1,13},{5,1},{9,5},{13,9},{2,14},{6,2},{... | collective-permute-start | bytes 3538952 | tf_op jit(solution)/shard_map/ppermute | solution.py:437
  602.6 94.8 %collective-permute-start.52 = (bf16[512,1152]{1,0:T(8,128)(2,1)}, bf16[512,1152]{1,0:T(8,128)(2,1)}, u32[]{:S(2)}, u32[]{:S(2)}) collective-permute-start(bf16[512,1152]{1,0:T(8,128)(2,1)} %get-tuple-element.102), channel_id=1, source_target_pairs={{0,4},{4,8},{8,12},{12,0},{1,5},{5,9},{9,13},{13,1},{2,6},{6,10},{... | collective-permute-start | bytes 3538952 | tf_op jit(solution)/shard_map/ppermute | solution.py:437
  605.3 165.0 %collective-permute-start.45 = (bf16[512,1024]{1,0:T(8,128)(2,1)S(1)}, bf16[512,1024]{1,0:T(8,128)(2,1)S(1)}, u32[]{:S(2)}, u32[]{:S(2)}) collective-permute-start(bf16[512,1024]{1,0:T(8,128)(2,1)S(1)} %copy-done.65), channel_id=1, source_target_pairs={{0,8},{4,12},{8,0},{12,4},{1,9},{5,13},{9,1},{13,5},{2,10},{6,14},... | collective-permute-start | bytes 3145736 | tf_op jit(solution)/shard_map/ppermute | solution.py:437
  606.5 163.8 %collective-permute-start.43 = (bf16[512,1024]{1,0:T(8,128)(2,1)S(1)}, bf16[512,1024]{1,0:T(8,128)(2,1)S(1)}, u32[]{:S(2)}, u32[]{:S(2)}) collective-permute-start(bf16[512,1024]{1,0:T(8,128)(2,1)S(1)} %copy-done.64), channel_id=1, source_target_pairs={{0,12},{4,0},{8,4},{12,8},{1,13},{5,1},{9,5},{13,9},{2,14},{6,2},{... | collective-permute-start | bytes 3145736 | tf_op jit(solution)/shard_map/ppermute | solution.py:437
  697.4 72.9 %collective-permute-start.41 = (bf16[512,1024]{1,0:T(8,128)(2,1)S(1)}, bf16[512,1024]{1,0:T(8,128)(2,1)S(1)}, u32[]{:S(2)}, u32[]{:S(2)}) collective-permute-start(bf16[512,1024]{1,0:T(8,128)(2,1)S(1)} %copy-done.63), channel_id=1, source_target_pairs={{0,4},{4,8},{8,12},{12,0},{1,5},{5,9},{9,13},{13,1},{2,6},{6,10},{... | collective-permute-start | bytes 3145736 | tf_op jit(solution)/shard_map/ppermute | solution.py:437
  889.6 181.6 %collective-permute-start.90 = (bf16[4096,512]{1,0:T(8,128)(2,1)}, bf16[4096,512]{1,0:T(8,128)(2,1)}, u32[]{:S(2)}, u32[]{:S(2)}) collective-permute-start(bf16[4096,512]{1,0:T(8,128)(2,1)} %convolution_convert_fusion.4), channel_id=1, source_target_pairs={{0,16},{16,0},{1,17},{17,1},{2,18},{18,2},{3,19},{19,3},{4,20},{20... | collective-permute-start | bytes 12582920 | tf_op jit(solution)/shard_map/ppermute | solution.py:1038
  910.1 174.2 %collective-permute-start.83 = (bf16[512,4096]{1,0:T(8,128)(2,1)}, bf16[512,4096]{1,0:T(8,128)(2,1)}, u32[]{:S(2)}, u32[]{:S(2)}) collective-permute-start(bf16[512,4096]{1,0:T(8,128)(2,1)} %convolution_convert_fusion), channel_id=1, source_target_pairs={{0,16},{16,0},{1,17},{17,1},{2,18},{18,2},{3,19},{19,3},{4,20},{20... | collective-permute-start | bytes 12582920 | tf_op jit(solution)/shard_map/ppermute | solution.py:1038
  929.4 291.2 %reduce-scatter.4.cloned.1.call-start = ((), (), s32[]{:S(2)}) async-start(), calls=%async_computation.3 | async-start | bytes 2359296 | tf_op jit(solution)/shard_map/reduce_scatter | solution.py:1358
  972.9 251.7 %reduce-scatter.6.cloned.1.call-start = ((), (), s32[]{:S(2)}) async-start(), calls=%async_computation.4 | async-start | bytes 1179648 | tf_op jit(solution)/shard_map/reduce_scatter | solution.py:1359
  987.5 100.8 %collective-permute-start.76 = (bf16[512,4096]{1,0:T(8,128)(2,1)}, bf16[512,4096]{1,0:T(8,128)(2,1)}, u32[]{:S(2)}, u32[]{:S(2)}) collective-permute-start(bf16[512,4096]{1,0:T(8,128)(2,1)} %convolution_convert_fusion.2), channel_id=1, source_target_pairs={{0,16},{16,0},{1,17},{17,1},{2,18},{18,2},{3,19},{19,3},{4,20},{20... | collective-permute-start | bytes 12582920 | tf_op jit(solution)/shard_map/ppermute | solution.py:1038
  1048.9 45.6 %collective-permute-start.71 = (bf16[4,128,512]{2,1,0:T(8,128)(2,1)S(1)}, bf16[4,128,512]{2,1,0:T(8,128)(2,1)S(1)}, u32[]{:S(2)}, u32[]{:S(2)}) collective-permute-start(bf16[4,128,512]{2,1,0:T(8,128)(2,1)S(1)} %get-tuple-element.236), channel_id=1, source_target_pairs={{0,2},{1,3},{2,0},{3,1},{4,6},{5,7},{6,4},{7,5},{8,10},{9,11},{10,... | collective-permute-start | bytes 1572872 | tf_op jit(solution)/shard_map/ppermute | solution.py:1038
  1094.6 43.8 %collective-permute-start.91 = (bf16[512,512]{1,0:T(8,128)(2,1)S(1)}, bf16[512,512]{1,0:T(8,128)(2,1)S(1)}, u32[]{:S(2)}, u32[]{:S(2)}) collective-permute-start(bf16[512,512]{1,0:T(8,128)(2,1)S(1)} %get-tuple-element.186), channel_id=1, source_target_pairs={{0,1},{1,0},{2,3},{3,2},{4,5},{5,4},{6,7},{7,6},{8,9},{9,8},{10,11... | collective-permute-start | bytes 1572872 | tf_op jit(solution)/shard_map/ppermute | solution.py:1038
  1098.1 58.5 %collective-permute-start.95 = (bf16[512,512]{1,0:T(8,128)(2,1)S(1)}, bf16[512,512]{1,0:T(8,128)(2,1)S(1)}, u32[]{:S(2)}, u32[]{:S(2)}) collective-permute-start(bf16[512,512]{1,0:T(8,128)(2,1)S(1)} %get-tuple-element.187), channel_id=1, source_target_pairs={{0,2},{1,3},{2,0},{3,1},{4,6},{5,7},{6,4},{7,5},{8,10},{9,11},{10,... | collective-permute-start | bytes 1572872 | tf_op jit(solution)/shard_map/ppermute | solution.py:1038
  1103.1 54.8 %collective-permute-start.84 = (bf16[512,512]{1,0:T(8,128)(2,1)S(1)}, bf16[512,512]{1,0:T(8,128)(2,1)S(1)}, u32[]{:S(2)}, u32[]{:S(2)}) collective-permute-start(bf16[512,512]{1,0:T(8,128)(2,1)S(1)} %get-tuple-element.192), channel_id=1, source_target_pairs={{0,1},{1,0},{2,3},{3,2},{4,5},{5,4},{6,7},{7,6},{8,9},{9,8},{10,11... | collective-permute-start | bytes 1572872 | tf_op jit(solution)/shard_map/ppermute | solution.py:1038
  1160.2 44.1 %collective-permute-start.94 = (bf16[512,512]{1,0:T(8,128)(2,1)S(1)}, bf16[512,512]{1,0:T(8,128)(2,1)S(1)}, u32[]{:S(2)}, u32[]{:S(2)}) collective-permute-start(bf16[512,512]{1,0:T(8,128)(2,1)S(1)} %get-tuple-element.188), channel_id=1, source_target_pairs={{0,2},{1,3},{2,0},{3,1},{4,6},{5,7},{6,4},{7,5},{8,10},{9,11},{10,... | collective-permute-start | bytes 1572872 | tf_op jit(solution)/shard_map/ppermute | solution.py:1038
  1171.0 42.3 %collective-permute-start.87 = (bf16[512,512]{1,0:T(8,128)(2,1)S(1)}, bf16[512,512]{1,0:T(8,128)(2,1)S(1)}, u32[]{:S(2)}, u32[]{:S(2)}) collective-permute-start(bf16[512,512]{1,0:T(8,128)(2,1)S(1)} %get-tuple-element.194), channel_id=1, source_target_pairs={{0,2},{1,3},{2,0},{3,1},{4,6},{5,7},{6,4},{7,5},{8,10},{9,11},{10,... | collective-permute-start | bytes 1572872 | tf_op jit(solution)/shard_map/ppermute | solution.py:1038
  (157 other events, 3341.9 us)
Sparse Core Ops, SparseCore 0:
  929.5 53.0 reduce-scatter.7
  985.0 82.0 reduce-scatter.3
  1070.1 33.8 reduce-scatter.5

commit v2 on v1

--- a/solution.py
+++ b/solution.py
@@ -645,17 +645,18 @@
 
 
 def expert_kernel(me_ref, x_ref, g_ref, own_ref, other_ref, spread_ref, gather_ref, *refs):
-    out_ref, gx_ref, h_ref, dg_ref, du_ref, out_acc, gx_acc, gg_acc = refs[-8:]
+    gx_ref, out_ref, h_ref, dg_ref, du_ref, out_acc, gx_acc, gg_acc = refs[-8:]
+    base_ref = refs[0] if len(refs) == 9 else None
     step = pl.program_id(0)
     me = me_ref[0]
     model_width = g_ref.shape[-1]
     rows = x_ref.shape[0]
     half = own_ref.shape[2]
-    piece = math.gcd(rows, 256)
+    piece = math.gcd(rows, 512)
 
     @pl.when(step == 0)
     def _():
-        out_acc[...] = jnp.zeros_like(out_acc)
+        out_acc[...] = jnp.zeros_like(out_acc) if base_ref is None else base_ref[...]
         gx_acc[...] = jnp.zeros_like(gx_acc)
         gg_acc[...] = jnp.zeros_like(gg_acc)
 
@@ -698,12 +699,12 @@
 
     @pl.when(step == pl.num_programs(0) - 1)
     def _():
-        out_ref[...] = out_acc[...].astype(jnp.bfloat16)
+        out_ref[...] = out_acc[...].astype(jnp.bfloat16).reshape(out_ref.shape)
         gx_ref[:, :model_width] = gx_acc[...].astype(jnp.bfloat16)
         gx_ref[:, model_width:] = gg_acc[...].astype(jnp.bfloat16)
 
 
-def expert_chunk(index, me, tokens, grads, own, other, spread, gather, kept):
+def expert_chunk(index, me, tokens, grads, own, other, spread, gather, kept, base):
     rows, wide = tokens.shape
     chunks, _, model_width = grads.shape
     parts, kinds, half, inner = own.shape
@@ -711,7 +712,13 @@
     saved = jax.ShapeDtypeStruct((chunks, rows, parts * inner), jnp.bfloat16)
     saved_spec = pl.BlockSpec((1, rows, inner), lambda s, *_: (index, 0, s))
     weight_spec = pl.BlockSpec((1, kinds, half, inner), lambda s, *_: (s, 0, 0, 0))
-    extra_in = [] if kept is None else list(kept)
+    extra_in = [base] if kept is None else list(kept)
+    extra_spec = (
+        [pl.BlockSpec((rows, model_width), lambda s, *_: (0, 0))]
+        if kept is None
+        else [pl.BlockSpec(memory_space=pl.ANY)] * len(extra_in)
+    )
+    aliases = {} if kept is None else {7 + n: 1 + n for n in range(len(extra_in))}
     return pl.pallas_call(
         expert_kernel,
         grid_spec=pltpu.PrefetchScalarGridSpec(
@@ -725,10 +732,10 @@
                 pl.BlockSpec(spread.shape, lambda s, *_: (0, 0, 0)),
                 pl.BlockSpec(gather.shape, lambda s, *_: (0, 0, 0)),
             ]
-            + [pl.BlockSpec(memory_space=pl.ANY)] * len(extra_in),
+            + extra_spec,
             out_specs=[
-                pl.BlockSpec((rows, model_width), lambda s, *_: (0, 0)),
                 pl.BlockSpec((rows, wide), lambda s, *_: (0, 0)),
+                pl.BlockSpec((chunks, 1, rows // chunks, model_width), lambda s, me: (0, me[1], 0, 0)),
                 saved_spec,
                 saved_spec,
                 saved_spec,
@@ -740,13 +747,13 @@
             ],
         ),
         out_shape=[
-            jax.ShapeDtypeStruct((rows, model_width), jnp.bfloat16),
             jax.ShapeDtypeStruct((rows, wide), jnp.bfloat16),
+            jax.ShapeDtypeStruct((chunks, chunks, rows // chunks, model_width), jnp.bfloat16),
             saved,
             saved,
             saved,
         ],
-        input_output_aliases={7 + n: 2 + n for n in range(len(extra_in))},
+        input_output_aliases=aliases,
         compiler_params=pltpu.CompilerParams(vmem_limit_bytes=VMEM_BYTES),
         cost_estimate=pl.CostEstimate(
             flops=12 * rows * model_width * parts * inner,
@@ -1059,10 +1066,11 @@
     first_1, second_2 = swap(first[1], "tp", 1), swap(second[2], "tp", 2)
     first_2 = swap(add_low(first[2], first_3), "tp", 2)
     second_1 = swap(add_low(second[1], second_3), "tp", 1)
-    return [
+    sums = [
         sum(part.astype(jnp.float32) for part in parts)
         for parts in ((first[0], first_1, first_2), (second[0], second_2, second_1))
     ]
+    return sums
 
 
 def exchange_parts(values, axis_name):
@@ -1120,11 +1128,16 @@
     half = model_width // 2
     tp_me, dp_me = tp_index.reshape(1), dp_index.reshape(1)
 
-    hidden_parts = exchange_parts(take_part(hidden_in, tp_index, quarter, 1), "ep")
-    hidden_mine = in_order(hidden_parts, "ep").reshape(mine, model_width)
-    routes_mine = in_order(
-        exchange_parts(take_part(expert_routes, tp_index, quarter, 1), "ep"), "ep"
-    ).reshape(mine, top_count)
+    wide_hidden = jnp.concatenate(
+        [
+            take_part(hidden_in, tp_index, quarter, 1),
+            take_part(expert_routes, tp_index, quarter, 1).astype(jnp.bfloat16),
+        ],
+        axis=2,
+    )
+    wide_mine = in_order(exchange_parts(wide_hidden, "ep"), "ep").reshape(mine, -1)
+    hidden_mine = wide_mine[:, :model_width]
+    routes_mine = wide_mine[:, model_width:].astype(jnp.int32)
 
     hidden = hidden_mine.astype(jnp.float32)
     gain_first = attn_gain.astype(jnp.float32)
@@ -1133,38 +1146,22 @@
     first_mine = (normed_first * gain_first).astype(jnp.bfloat16)
     first_rows = gather_halves(first_mine[:, :half], first_mine[:, half:])
 
-    gathered = []
-    for number, weight in enumerate(
-        (
-            jnp.transpose(w_gate, (1, 0, 2)).reshape(model_width, inner),
-            jnp.transpose(w_up, (1, 0, 2)).reshape(model_width, inner),
-            w_down.reshape(inner, model_width),
-        )
-    ):
-        part = take_part(weight, dp_index, half, 0)
-        if number:
-            part = after(part, first_rows[6], first_rows[7])
-        pieces = gather_halves(part[:, : inner // 2], part[:, inner // 2 :])
-        gathered.append(
-            jnp.stack(
-                [jnp.concatenate(pieces[2 * n : 2 * n + 2], axis=1) for n in range(tp_count)]
+    weights_here = jnp.stack(
+        [
+            take_part(weight, dp_index, half, 0)
+            for weight in (
+                jnp.transpose(after(w_gate, wide_hidden), (1, 0, 2)).reshape(model_width, inner),
+                jnp.transpose(after(w_up, wide_hidden), (1, 0, 2)).reshape(model_width, inner),
+                after(w_down, wide_hidden).reshape(inner, model_width),
             )
-        )
-    own_weights = jnp.stack(gathered, axis=1)
-    other_weights = swap(own_weights, "dp", 1)
-
-    grads_mine_all = after(take_part(cotangent, tp_index, quarter, 1), hidden_mine)
-    grads_all = in_order(
-        [grads_mine_all]
-        + [shift_by(grads_mine_all, "ep", distance) for distance in range(1, ep_count)],
-        "ep",
-    )
-    chunk_grads = jnp.stack(
-        [
-            lax.dynamic_index_in_dim(grads_all, (ep_index + step) % ep_count, 1, False)
-            for step in range(ep_count)
         ]
-    ).reshape(ep_count, mine, model_width)
+    )
+    own_weights = lax.all_gather(weights_here, "tp")
+
+    grads_mine_all = after(take_part(cotangent, tp_index, quarter, 1), first_rows[7])
+    grads_parts = [grads_mine_all] + [
+        shift_by(grads_mine_all, "ep", distance) for distance in range(1, ep_count)
+    ]
 
     weights_t = jnp.concatenate([w_query, key_projection_weight, value_projection_weight], axis=1).T
     inverse = 1.0 / 10000.0 ** (jnp.arange(halfway, dtype=jnp.float32) * 2.0 / HEAD_SIZE)
@@ -1182,9 +1179,18 @@
     start_row = starts[None, :]
     attn_t, lse = attend(query_t, key_rows, value_t, start_row, low, mid, block)
 
-    attn_out = jnp.concatenate(
-        reduce_halves(mix_heads(tp_me, attn_t, w_out, tp_count, quarter)), axis=1
-    )
+    grads_parts = [after(part, attn_t) for part in grads_parts]
+    mixed = mix_heads(tp_me, after(attn_t, *grads_parts), w_out, tp_count, quarter)
+    own_weights = after(own_weights, mixed[0])
+    grads_all = in_order([after(part, mixed[0]) for part in grads_parts], "ep")
+    other_weights = swap(own_weights, "dp", 1)
+    chunk_grads = jnp.stack(
+        [
+            lax.dynamic_index_in_dim(grads_all, (ep_index + step) % ep_count, 1, False)
+            for step in range(ep_count)
+        ]
+    ).reshape(ep_count, mine, model_width)
+    attn_out = jnp.concatenate(reduce_halves(mixed), axis=1)
     middle = hidden + attn_out
     gain_second = moe_gain.astype(jnp.float32)
     factor_second = inverse_rms(middle)
@@ -1216,17 +1222,21 @@
         (lane[None, :, None] < 2 * expert_count)
         & (lane[None, :, None] % expert_count == expert_of[:, None, :])
     ).astype(jnp.bfloat16)
-    order = [0] + [n for n in range(1, ep_count) if n % 2] + [n for n in range(1, ep_count) if n % 2 == 0]
-    chunk_tokens = {0: tokens}
-    previous = tokens
-    for step in order[1:]:
-        chunk_tokens[step] = previous = shift_by(after(tokens, previous), "ep", -step)
-    kept = None
-    out_parts, grad_parts = [], []
-    for step in order:
-        out_part, grad_part, *kept = expert_chunk(
+    order = [0, *range(1, ep_count, 2), *range(2, ep_count, 2)]
+    turns = len(order)
+    chunk_tokens, grad_parts = {0: tokens}, {}
+    kept, last = None, tokens
+    for turn_number, step in enumerate(order):
+        incoming = []
+        if turn_number == 0:
+            incoming = [n for n in order if n % 2]
+        elif turn_number == 1:
+            incoming = [n for n in order if n and n % 2 == 0]
+        for n in incoming:
+            chunk_tokens[n] = shift_by(after(tokens, last), "ep", -n)
+        grad_part, *kept = expert_chunk(
             step,
-            dp_me,
+            jnp.stack([dp_index, (ep_index + step) % ep_count]),
             chunk_tokens[step],
             chunk_grads,
             own_weights,
@@ -1234,12 +1244,21 @@
             spread,
             gather,
             kept,
-        )
-        out_parts.append(shift_by(out_part, "ep", step) if step else out_part)
-        grad_parts.append(shift_by(grad_part, "ep", step) if step else grad_part)
-    grad_sum = sum(part.astype(jnp.float32) for part in grad_parts)
-
+            None if step else middle,
+        )
+        last = grad_part
+        for n in order[turn_number + 1 : turn_number + 3]:
+            if n in chunk_tokens:
+                chunk_tokens[n] = after(chunk_tokens[n], last)
+        for n in order[1:turn_number]:
+            grad_parts[n] = after(grad_parts[n], last)
+        grad_parts[step] = shift_by(grad_part, "ep", step) if step else grad_part
+
+    out_all = kept.pop(0)
     active, grad_gate, grad_up = [part.reshape(ep_count * mine, tp_count * inner) for part in kept]
+    out_home = lax.psum_scatter(
+        out_all.reshape(ep_count * mine, model_width), "ep", scatter_dimension=0, tiled=True
+    ).reshape(seq_count, quarter, model_width)
 
     def token_half(number):
         return jnp.concatenate(
@@ -1252,49 +1271,50 @@
     def low_product(left_side, right_side):
         return contract_rows(left_side, right_side).astype(jnp.bfloat16)
 
-    far_tokens, far_grads = token_half(1 - dp_index), grads_half(1 - dp_index)
-    far_sums = [
-        swap(part, "dp", 1)
-        for part in (
-            low_product(far_tokens, grad_gate),
-            low_product(far_tokens, grad_up),
-            low_product(active, far_grads),
-        )
-    ]
-    near_tokens, near_grads = token_half(dp_index), grads_half(dp_index)
-    near_sums = [
-        low_product(near_tokens, grad_gate),
-        low_product(near_tokens, grad_up),
-        low_product(active, near_grads),
-    ]
-    gate_sum, up_sum, down_sum = [add_low(*pair) for pair in zip(near_sums, far_sums)]
-    cut = inner // 2
-
-    def columns_home(total):
-        pieces = [total[:, n * cut : (n + 1) * cut] for n in range(2 * tp_count)]
-        home = jnp.concatenate(reduce_halves(pieces), axis=1)
-        return jnp.swapaxes(home.reshape(half, experts_here, hidden_here), 0, 1)
-
-    gate_out, up_out = columns_home(gate_sum), columns_home(up_sum)
-    down_out = jnp.concatenate(
-        reduce_halves([down_sum[n * cut : (n + 1) * cut] for n in range(2 * tp_count)]), axis=0
-    ).reshape(experts_here, hidden_here, half)
+    def weight_products(number, *earlier):
+        tokens_part, grads_part = after(token_half(number), *earlier), grads_half(number)
+        return [
+            low_product(tokens_part, grad_gate),
+            low_product(tokens_part, grad_up),
+            low_product(active, after(grads_part, *earlier)),
+        ]
+
+    far_sums = weight_products(1 - dp_index)
+    final = order[-1]
+    grad_parts[final] = after(grad_parts[final], *far_sums)
+    grad_sum = sum(grad_parts[step].astype(jnp.float32) for step in range(ep_count))
+    far_sums = [swap(part, "dp", 1) for part in far_sums]
 
     grad_gates = grad_sum[:, model_width : model_width + expert_count]
     grad_logits = (
         gates * (grad_gates - jnp.sum(gates * grad_gates, axis=-1, keepdims=True))
     ).astype(jnp.bfloat16)
-    grad_router = contract_rows(second_in, grad_logits)
     grad_second = grad_sum[:, :model_width] + contract_last(grad_logits, w_router)
-    grad_moe_gain = jnp.sum(grad_second * normed_second, axis=0)
     grad_middle = chunk_grads[0].astype(jnp.float32) + norm_back(
         grad_second, normed_second, factor_second, gain_second
     )
     grad_low = grad_middle.astype(jnp.bfloat16)
     grad_attn = gather_halves(grad_low[:, :half], grad_low[:, half:])
+    near_sums = weight_products(dp_index, grad_low)
+    grad_attn[6:] = [after(piece, *near_sums) for piece in grad_attn[6:]]
     grad_vec_t, grad_vec, delta, grad_wo = unmix_heads(
         tp_me, grad_attn, w_out, attn_t, kv_width, quarter
     )
+    cut = inner // 2
+    sums = [add_low(*pair) for pair in zip(near_sums, far_sums)]
+
+    def sum_piece(offset, side):
+        place = tp_index ^ offset
+        columns = [
+            lax.dynamic_slice_in_dim(total, place * inner + side * cut, cut, 1) for total in sums[:2]
+        ]
+        return jnp.concatenate(
+            columns + [lax.dynamic_slice_in_dim(sums[2], place * inner + side * cut, cut, 0)], axis=0
+        )
+
+    first, second = [[sum_piece(offset, side) for offset in range(tp_count)] for side in range(2)]
+    first_3, second_3 = swap(first[3], "tp", 1), swap(second[3], "tp", 2)
+    first_1, second_2 = swap(first[1], "tp", 1), swap(second[2], "tp", 2)
     grad_query_t, grad_key, grad_value = attend_back(
         query_t,
         query,
@@ -1310,12 +1330,47 @@
         mid,
         block,
     )
+    first_3, second_3, first_1, second_2 = [
+        after(part, grad_query_t) for part in (first_3, second_3, first_1, second_2)
+    ]
+    grad_query_t = after(grad_query_t, first_3, second_3, first_1, second_2)
     grad_qkv_t, *first_parts = unproject(
         tp_me, grad_query_t, grad_key, grad_value, cosine, sine, first_rows, weights_t, quarter
     )
-    grad_first = jnp.concatenate(reduce_halves(first_parts), axis=1)
-    grad_attn_gain = jnp.sum(grad_first * normed_first, axis=0)
+    def dp_half(rows):
+        share = rows.shape[1] // 2
+        return take_part(rows, dp_index, share, 1) + swap(
+            take_part(rows, 1 - dp_index, share, 1), "dp", 1
+        )
+
+    def ep_part(rows):
+        share = rows.shape[1] // ep_count
+        return sum(
+            shift_by(take_part(rows, (ep_index + step) % ep_count, share, 1), "ep", step)
+            if step
+            else take_part(rows, ep_index, share, 1)
+            for step in range(ep_count)
+        )
+
+    dense_half = dp_half(jnp.concatenate([grad_qkv_t, grad_wo], axis=0))
+    grad_first = after(jnp.concatenate(reduce_halves(first_parts), axis=1), dense_half)
     grad_mine = grad_middle + norm_back(grad_first, normed_first, factor_first, gain_first)
+    first_2 = swap(after(add_low(first[2], first_3), grad_mine), "tp", 2)
+    second_1 = swap(after(add_low(second[1], second_3), grad_mine), "tp", 1)
+    home_sides = [
+        sum(part.astype(jnp.float32) for part in parts)
+        for parts in ((first[0], first_1, first_2), (second[0], second_2, second_1))
+    ]
+
+    def columns_home(number):
+        rows = slice(number * half, (number + 1) * half)
+        home = jnp.concatenate([side[rows] for side in home_sides], axis=1)
+        return jnp.swapaxes(home.reshape(half, experts_here, hidden_here), 0, 1)
+
+    gate_out, up_out = columns_home(0), columns_home(1)
+    down_out = jnp.concatenate([side[2 * half :] for side in home_sides], axis=0).reshape(
+        experts_here, hidden_here, half
+    )
 
     def rows_home(rows):
         parts = exchange_parts(rows.astype(jnp.bfloat16).reshape(ep_count, quarter, model_width), "ep")
@@ -1327,7 +1382,7 @@
             for index in range(tp_count)
         ]
 
-    home = rows_home(grad_mine)
+    home = after(rows_home(grad_mine), first_2, second_1)
     home_pieces = gather_halves(home[..., :half], home[..., half:])
     grad_in = jnp.concatenate(
         [
@@ -1337,8 +1392,7 @@
         axis=2,
     ).astype(jnp.float32)
 
-    out_sum = middle + sum(part.astype(jnp.float32) for part in out_parts)
-    out_home = rows_home(out_sum)
+    out_home = after(out_home, grad_mine)
     column = model_width // tp_count
     block_out = jnp.concatenate(
         by_quarter(
@@ -1354,21 +1408,36 @@
         axis=1,
     ).astype(jnp.float32)
 
-    both = ("dp", "ep")
-    qkv_home = lax.psum_scatter(grad_qkv_t, both, scatter_dimension=1, tiled=True).T
-    wo_home = lax.psum_scatter(grad_wo, both, scatter_dimension=1, tiled=True)
-    small = jnp.concatenate([grad_router, grad_moe_gain[:, None], grad_attn_gain[:, None]], axis=1)
-    small_home = lax.psum_scatter(lax.psum(small, "tp"), both, scatter_dimension=0, tiled=True)
+    def tp_total(rows):
+        rows = rows + swap(rows, "tp", 1)
+        return rows + swap(rows, "tp", 2)
+
+    grad_router = contract_rows(after(second_in, grad_vec_t), grad_logits)
+    grad_moe_gain = jnp.sum(after(grad_second, grad_vec_t) * normed_second, axis=0)
+    grad_attn_gain = jnp.sum(after(grad_first, home_pieces[2]) * normed_first, axis=0)
+    dense_home = ep_part(after(dense_half, home_pieces[2]))
+    qkv_home = dense_home[: query_width + 2 * kv_width].T
+    wo_home = dense_home[query_width + 2 * kv_width :]
+    small = jnp.concatenate(
+        [
+            grad_router.T,
+            grad_moe_gain[None, :],
+            grad_attn_gain[None, :],
+            jnp.zeros((6, model_width), jnp.float32),
+        ],
+        axis=0,
+    )
+    small_home = ep_part(dp_half(tp_total(small)))
     return (
         block_out,
         grad_in,
-        small_home[:, expert_count + 1],
+        small_home[expert_count + 1],
         qkv_home[:, :query_width],
         qkv_home[:, query_width : query_width + kv_width],
         qkv_home[:, query_width + kv_width :],
         wo_home,
-        small_home[:, expert_count],
-        small_home[:, :expert_count],
+        small_home[expert_count],
+        small_home[:expert_count].T,
         gate_out,
         up_out,
         down_out,

time: 1250 us -> 870 us (0.70)
  waiting for transfers between devices: 544 us -> 259 us
  starting transfers between devices: 192 us -> 116 us
  blocking collectives: 20.8 us -> 0 us
  local copies, waits for them, and re-layouts: 35.2 us -> 52.4 us
    ppermute x73 -> x47, waiting for transfers between devices: 268 us -> 123 us  [swap(): lax.ppermute(values, axis_name, [(source, source ^ distance) for source i...]
    ppermute x24 -> x21, waiting for transfers between devices: 276 us -> 136 us  [shift_by(): lax.ppermute(values, axis_name, [(source, (source + distance) % count) fo...]
    ppermute x24 -> x21, starting transfers between devices: 122 us -> 74 us  [shift_by(): lax.ppermute(values, axis_name, [(source, (source + distance) % count) fo...]
    ppermute x73 -> x47, starting transfers between devices: 70.6 us -> 42.3 us  [swap(): lax.ppermute(values, axis_name, [(source, source ^ distance) for source i...]
    psum x1 -> x0, blocking collectives: 20.8 us -> none  [per_device_by_sequence(): lax.psum(small, 'tp')]
  transfers between devices with their start and end apart: 100 -> 70, of which waited for: 45 -> 24; matrix products, arithmetic and copies ran while one was open for 14% -> 20% of each run, Pallas kernels for 13% -> 31%
where the time goes in v2:
time: 870 us; the launch traced here: 863 us
  Pallas kernels  264 us (30%)
  waiting for transfers between devices  259 us (30%)
  starting transfers between devices  116 us (13%)
  matrix products  83.4 us (10%)
  other arithmetic  71.8 us (8%)
  local copies, waits for them, and re-layouts  52.4 us (6%)
  between operations  16 us (2%)
    pallas_call x4, Pallas kernels, expert_chunk(): pl.pallas_call(expert_kernel, grid_spec=pltpu.PrefetchScalarGridSpec(num_...  157 us
    ppermute x21, waiting for transfers between devices, shift_by(): lax.ppermute(values, axis_name, [(source, (source + distance) % count) fo...  136 us
    ppermute x47, waiting for transfers between devices, swap(): lax.ppermute(values, axis_name, [(source, source ^ distance) for source i...  123 us
    dot_general x7, matrix products, contract_rows(): lax.dot_general(left_side, right_side, (((0,), (0,)), ((), ())), preferre...  82.3 us
    ppermute x21, starting transfers between devices, shift_by(): lax.ppermute(values, axis_name, [(source, (source + distance) % count) fo...  74 us
    pallas_call x1, Pallas kernels, attend_back(): pl.pallas_call(attend_back_kernel, grid_spec=pltpu.PrefetchScalarGridSpec...  44.1 us
    ppermute x47, starting transfers between devices, swap(): lax.ppermute(values, axis_name, [(source, source ^ distance) for source i...  42.3 us
    pallas_call x1, Pallas kernels, attend(): pl.pallas_call(attend_kernel, grid_spec=pltpu.PrefetchScalarGridSpec(num_...  31.5 us
  transfers between devices with their start and end apart: 70, of which 24 were waited for; matrix products, arithmetic and copies ran while one was open for 20% of the time, Pallas kernels for 31%

profile of v2, /device:TPU:0, one launch (start us, length us, event | category | flops | bytes accessed | tf_op | source)
XLA Modules:
  0.0 862.7 jit_solution(10952747761354445286)
XLA Ops:
  39.8 17.7 %collective-permute-done.1 = bf16[128,1032]{1,0:T(8,128)(2,1)S(1)} collective-permute-done((bf16[128,1032]{1,0:T(8,128)(2,1)S(1)}, bf16[128,1032]{1,0:T(8,128)(2,1)S(1)}, u32[]{:S(2)}, u32[]{:S(2)}) %collective-permute-start.1) | collective-permute-done | bytes 264224 | tf_op jit(solution)/shard_map/ppermute | solution.py:437
  67.7 19.1 %collective-permute-done.6.refs_5_ = bf16[512,512]{1,0:T(8,128)(2,1)} collective-permute-done((bf16[512,512]{1,0:T(8,128)(2,1)}, bf16[512,512]{1,0:T(8,128)(2,1)}, u32[]{:S(2)}, u32[]{:S(2)}) %collective-permute-start.6) | collective-permute-done | bytes 524320 | tf_op jit(solution)/shard_map/ppermute | solution.py:1045
  91.1 25.6 %collective-permute-done.8.refs_7_ = bf16[512,512]{1,0:T(8,128)(2,1)S(1)} collective-permute-done((bf16[512,512]{1,0:T(8,128)(2,1)}, bf16[512,512]{1,0:T(8,128)(2,1)S(1)}, u32[]{:S(2)}, u32[]{:S(2)}) %collective-permute-start.8) | collective-permute-done | bytes 524320 | tf_op jit(solution)/shard_map/ppermute | solution.py:1045
  131.6 31.5 %attend.1 = (bf16[256,2048]{1,0:T(8,128)(2,1)}, f32[4,1,2048]{2,1,0:T(1,128)}) custom-call(s32[4]{0:T(128)} %get-tuple-element.381.low_ref, s32[4]{0:T(128)} %get-tuple-element.380.mid_ref, bf16[4,128,2048]{2,1,0:T(8,128)(2,1)} %get-tuple-element.107.q_ref.qt_ref, bf16[2048,128]{1,0:T(8,128)(2,1)} %get-tuple-element.108.k_ref, ...), custom_call_target="tpu_custom_call" | custom-call | flops 8589934592 | bytes 8388608 | tf_op jit(solution)/shard_map/attend/pallas_call | solution.py:484
  163.1 23.8 %collective-permute-done.10 = bf16[4,128,1024]{2,1,0:T(8,128)(2,1)S(1)} collective-permute-done((bf16[4,128,1024]{2,1,0:T(8,128)(2,1)S(1)}, bf16[4,128,1024]{2,1,0:T(8,128)(2,1)S(1)}, u32[]{:S(2)}, u32[]{:S(2)}) %collective-permute-start.10) | collective-permute-done | bytes 1048608 | tf_op jit(solution)/shard_map/ppermute | solution.py:437
  240.1 24.2 %collective-permute-start.20 = (bf16[512,1152]{1,0:T(8,128)(2,1)S(1)}, bf16[512,1152]{1,0:T(8,128)(2,1)S(1)}, u32[]{:S(2)}, u32[]{:S(2)}) collective-permute-start(bf16[512,1152]{1,0:T(8,128)(2,1)S(1)} %concatenate.76.x_ref), channel_id=1, source_target_pairs={{0,12},{4,0},{8,4},{12,8},{1,13},{5,1},{9,5},{13,9},{2,14},{6,2},{... | collective-permute-start | bytes 3538952 | tf_op jit(solution)/shard_map/ppermute | solution.py:437
  265.3 39.6 %expert_chunk.4 = (bf16[512,1152]{1,0:T(8,128)(2,1)}, bf16[4,4,128,1024]{3,2,1,0:T(8,128)(2,1)}, bf16[4,512,4096]{2,1,0:T(8,128)(2,1)}, bf16[4,512,4096]{2,1,0:T(8,128)(2,1)}, bf16[4,512,4096]{2,1,0:T(8,128)(2,1)}) custom-call(s32[2]{0:T(128)} %pad_add_fusion.1.me_ref, bf16[512,1152]{1,0:T(8,128)(2,1)} %copy-done.15, ...), custom_call_target="tpu_custom_call" | custom-call | flops 25769803776 | bytes 37748736 | tf_op jit(solution)/shard_map/expert_chunk/pallas_call | solution.py:722
  305.5 11.0 %collective-permute-done.21.x_ref = bf16[512,1152]{1,0:T(8,128)(2,1)} collective-permute-done((bf16[512,1152]{1,0:T(8,128)(2,1)S(1)}, bf16[512,1152]{1,0:T(8,128)(2,1)}, u32[]{:S(2)}, u32[]{:S(2)}) %collective-permute-start.21) | collective-permute-done | bytes 1179680 | tf_op jit(solution)/shard_map/ppermute | solution.py:437
  316.6 39.1 %expert_chunk.5 = (bf16[512,1152]{1,0:T(8,128)(2,1)}, bf16[4,4,128,1024]{3,2,1,0:T(8,128)(2,1)}, bf16[4,512,4096]{2,1,0:T(8,128)(2,1)}, bf16[4,512,4096]{2,1,0:T(8,128)(2,1)}, bf16[4,512,4096]{2,1,0:T(8,128)(2,1)}) custom-call(s32[2]{0:T(128)} %get-tuple-element.383.me_ref, ...), custom_call_target="tpu_custom_call", output_to_operand_aliasing={{1}: (7, {}), {2}: (8, {}), {3}: (9, {}), {4}: (10, {})} | custom-call | flops 25769803776 | bytes 37748736 | tf_op jit(solution)/shard_map/expert_chunk/pallas_call | solution.py:722
  357.6 39.0 %expert_chunk.6 = (bf16[512,1152]{1,0:T(8,128)(2,1)}, bf16[4,4,128,1024]{3,2,1,0:T(8,128)(2,1)}, bf16[4,512,4096]{2,1,0:T(8,128)(2,1)}, bf16[4,512,4096]{2,1,0:T(8,128)(2,1)}, bf16[4,512,4096]{2,1,0:T(8,128)(2,1)}) custom-call(s32[2]{0:T(128)} %pad_add_fusion.3.me_ref, ...), custom_call_target="tpu_custom_call", output_to_operand_aliasing={{1}: (7, {}), {2}: (8, {}), {3}: (9, {}), {4}: (10, {})} | custom-call | flops 25769803776 | bytes 37748736 | tf_op jit(solution)/shard_map/expert_chunk/pallas_call | solution.py:722
  401.3 39.3 %expert_chunk.7 = (bf16[512,1152]{1,0:T(8,128)(2,1)}, bf16[4,4,128,1024]{3,2,1,0:T(8,128)(2,1)}, bf16[4,512,4096]{2,1,0:T(8,128)(2,1)}, bf16[4,512,4096]{2,1,0:T(8,128)(2,1)}, bf16[4,512,4096]{2,1,0:T(8,128)(2,1)}) custom-call(s32[2]{0:T(128)} %get-tuple-element.382.me_ref, ...), custom_call_target="tpu_custom_call", output_to_operand_aliasing={{1}: (7, {}), {2}: (8, {}), {3}: (9, {}), {4}: (10, {})} | custom-call | flops 25769803776 | bytes 37748736 | tf_op jit(solution)/shard_map/expert_chunk/pallas_call | solution.py:722
  440.7 24.3 %collective-permute-start.23 = (bf16[512,1152]{1,0:T(8,128)(2,1)}, bf16[512,1152]{1,0:T(8,128)(2,1)S(1)}, u32[]{:S(2)}, u32[]{:S(2)}) collective-permute-start(bf16[512,1152]{1,0:T(8,128)(2,1)} %get-tuple-element.157), channel_id=1, source_target_pairs={{0,8},{4,12},{8,0},{12,4},{1,9},{5,13},{9,1},{13,5},{2,10},{6,14},... | collective-permute-start | bytes 3538952 | tf_op jit(solution)/shard_map/ppermute | solution.py:437
  466.4 14.9 %convolution_convert_fusion.3 = bf16[512,4096]{1,0:T(8,128)(2,1)} fusion(bf16[2048,512]{1,0:T(8,128)(2,1)S(1)} %pad_maximum_fusion.6, bf16[2048,4096]{1,0:T(8,128)(2,1)} %bitcast.204), kind=kOutput, calls=%fused_computation.7 | convolution fusion | flops 8592031744 | bytes 23068672 | tf_op jit(solution)/shard_map/dot_general | solution.py:22
  481.3 10.7 %convolution_convert_fusion.5 = bf16[4096,512]{1,0:T(8,128)(2,1)} fusion(bf16[2048,4096]{1,0:T(8,128)(2,1)S(1)} %bitcast.203, bf16[2048,512]{1,0:T(8,128)(2,1)S(1)} %copy-done.22), kind=kOutput, calls=%fused_computation.9 | convolution fusion | flops 8592031744 | bytes 23068672 | tf_op jit(solution)/shard_map/dot_general | solution.py:22
  492.0 14.1 %convolution_convert_fusion.2 = bf16[512,4096]{1,0:T(8,128)(2,1)} fusion(bf16[2048,512]{1,0:T(8,128)(2,1)S(1)} %pad_maximum_fusion.6, bf16[2048,4096]{1,0:T(8,128)(2,1)} %bitcast.206), kind=kOutput, calls=%fused_computation.6 | convolution fusion | flops 8592031744 | bytes 23068672 | tf_op jit(solution)/shard_map/dot_general | solution.py:22
  507.0 41.4 %collective-permute-done.23 = bf16[512,1152]{1,0:T(8,128)(2,1)S(1)} collective-permute-done((bf16[512,1152]{1,0:T(8,128)(2,1)}, bf16[512,1152]{1,0:T(8,128)(2,1)S(1)}, u32[]{:S(2)}, u32[]{:S(2)}) %collective-permute-start.23) | collective-permute-done | bytes 1179680 | tf_op jit(solution)/shard_map/ppermute | solution.py:437
  555.1 14.0 %convolution_convert_fusion.4 = bf16[4096,512]{1,0:T(8,128)(2,1)} fusion(bf16[2048,4096]{1,0:T(8,128)(2,1)} %bitcast.200, bf16[2048,512]{1,0:T(8,128)(2,1)S(1)} %copy-done.21), kind=kOutput, calls=%fused_computation.8 | convolution fusion | flops 8592031744 | bytes 23068672 | tf_op jit(solution)/shard_map/dot_general | solution.py:22
  571.1 14.0 %convolution_convert_fusion.1 = bf16[512,4096]{1,0:T(8,128)(2,1)} fusion(bf16[2048,512]{1,0:T(8,128)(2,1)S(1)} %pad_maximum_fusion.7, bf16[2048,4096]{1,0:T(8,128)(2,1)} %bitcast.205), kind=kOutput, calls=%fused_computation.5 | convolution fusion | flops 8592031744 | bytes 23068672 | tf_op jit(solution)/shard_map/dot_general | solution.py:22
  587.3 14.3 %convolution_convert_fusion = bf16[512,4096]{1,0:T(8,128)(2,1)} fusion(bf16[2048,512]{1,0:T(8,128)(2,1)S(1)} %pad_maximum_fusion.7, bf16[2048,4096]{1,0:T(8,128)(2,1)} %bitcast.207), kind=kOutput, calls=%fused_computation.4 | convolution fusion | flops 8592031744 | bytes 23068672 | tf_op jit(solution)/shard_map/dot_general | solution.py:22
  638.5 44.1 %attend_back.1 = (f32[256,2048]{1,0:T(8,128)}, f32[2048,128]{1,0:T(8,128)}, f32[2048,128]{1,0:T(8,128)}) custom-call(s32[4]{0:T(128)} %get-tuple-element.381.low_ref, s32[4]{0:T(128)} %get-tuple-element.380.mid_ref, bf16[4,128,2048]{2,1,0:T(8,128)(2,1)} %get-tuple-element.107.q_ref.qt_ref, bf16[4,2048,128]{2,1,0:T(8,128)(2,1)} %get-tuple-element.164.q_ref, ...), custom_call_target="tpu_custom_call" | custom-call | flops 21474836480 | bytes 16777216 | tf_op jit(solution)/shard_map/attend_back/pallas_call | solution.py:596
  708.7 12.3 %collective-permute-done.43 = bf16[512,512]{1,0:T(8,128)(2,1)S(1)} collective-permute-done((bf16[512,512]{1,0:T(8,128)(2,1)S(1)}, bf16[512,512]{1,0:T(8,128)(2,1)S(1)}, u32[]{:S(2)}, u32[]{:S(2)}) %collective-permute-start.43) | collective-permute-done | bytes 524320 | tf_op jit(solution)/shard_map/ppermute | solution.py:1045
  753.5 16.2 %collective-permute-done.47 = bf16[4,128,256]{2,1,0:T(8,128)(2,1)S(1)} collective-permute-done((bf16[4,128,256]{2,1,0:T(8,128)(2,1)S(1)}, bf16[4,128,256]{2,1,0:T(8,128)(2,1)S(1)}, u32[]{:S(2)}, u32[]{:S(2)}) %collective-permute-start.47) | collective-permute-done | bytes 262176 | tf_op jit(solution)/shard_map/ppermute | solution.py:1045
  803.5 15.7 %collective-permute-done.66 = f32[768,128]{1,0:T(8,128)S(1)} collective-permute-done((f32[768,128]{1,0:T(8,128)S(1)}, f32[768,128]{1,0:T(8,128)S(1)}, u32[]{:S(2)}, u32[]{:S(2)}) %collective-permute-start.66) | collective-permute-done | bytes 393248 | tf_op jit(solution)/shard_map/ppermute | solution.py:437
  830.7 11.0 %collective-permute-done.58 = bf16[4,128,512]{2,1,0:T(8,128)(2,1)S(1)} collective-permute-done((bf16[4,128,512]{2,1,0:T(8,128)(2,1)}, bf16[4,128,512]{2,1,0:T(8,128)(2,1)S(1)}, u32[]{:S(2)}, u32[]{:S(2)}) %collective-permute-start.58) | collective-permute-done | bytes 524320 | tf_op jit(solution)/shard_map/ppermute | solution.py:1045
  (454 shorter events, 289.8 us)
Async XLA Ops:
  7.2 185.8 %all-gather.3.cloned.1.call-start = ((), (), s32[]{:S(2)}) async-start(), calls=%async_computation.2 | async-start | bytes 15728640 | tf_op jit(solution)/shard_map/all_gather | solution.py:1159
  27.0 721.4 %reduce-scatter.2.cloned.1.call-start = ((), (), s32[]{:S(2)}) async-start(), calls=%async_computation.1 | async-start | bytes 5242880 | tf_op jit(solution)/shard_map/reduce_scatter | solution.py:1259
  67.1 53.7 %collective-permute-start.4 = (bf16[512,512]{1,0:T(8,128)(2,1)}, bf16[512,512]{1,0:T(8,128)(2,1)S(1)}, u32[]{:S(2)}, u32[]{:S(2)}) collective-permute-start(bf16[512,512]{1,0:T(8,128)(2,1)} %get-tuple-element.365.refs_1_), channel_id=1, source_target_pairs={{0,1},{1,0},{2,3},{3,2},{4,5},{5,4},{6,7},{7,6},{8,9},{9,8},{10,11... | collective-permute-start | bytes 1572872 | tf_op jit(solution)/shard_map/ppermute | solution.py:1045
  87.3 36.3 %collective-permute-start.5 = (bf16[512,512]{1,0:T(8,128)(2,1)}, bf16[512,512]{1,0:T(8,128)(2,1)}, u32[]{:S(2)}, u32[]{:S(2)}) collective-permute-start(bf16[512,512]{1,0:T(8,128)(2,1)} %get-tuple-element.366.refs_0_), channel_id=1, source_target_pairs={{0,2},{1,3},{2,0},{3,1},{4,6},{5,7},{6,4},{7,5},{8,10},{9,11},{10,... | collective-permute-start | bytes 1572872 | tf_op jit(solution)/shard_map/ppermute | solution.py:1045
  116.7 46.4 %collective-permute-start.9 = (bf16[4,128,1024]{2,1,0:T(8,128)(2,1)S(1)}, bf16[4,128,1024]{2,1,0:T(8,128)(2,1)S(1)}, u32[]{:S(2)}, u32[]{:S(2)}) collective-permute-start(bf16[4,128,1024]{2,1,0:T(8,128)(2,1)S(1)} %constant_dynamic-slice_fusion.61), channel_id=1, source_target_pairs={{0,4},{4,8},{8,12},{12,0},{1,5},{5,9},{9,13},{13,1},{2,6},{6,10},{... | collective-permute-start | bytes 3145736 | tf_op jit(solution)/shard_map/ppermute | solution.py:437
  118.1 68.8 %collective-permute-start.10 = (bf16[4,128,1024]{2,1,0:T(8,128)(2,1)S(1)}, bf16[4,128,1024]{2,1,0:T(8,128)(2,1)S(1)}, u32[]{:S(2)}, u32[]{:S(2)}) collective-permute-start(bf16[4,128,1024]{2,1,0:T(8,128)(2,1)S(1)} %constant_dynamic-slice_fusion.61), channel_id=1, source_target_pairs={{0,8},{4,12},{8,0},{12,4},{1,9},{5,13},{9,1},{13,5},{2,10},{6,14},... | collective-permute-start | bytes 3145736 | tf_op jit(solution)/shard_map/ppermute | solution.py:437
  120.8 66.1 %collective-permute-start.11 = (bf16[4,128,1024]{2,1,0:T(8,128)(2,1)S(1)}, bf16[4,128,1024]{2,1,0:T(8,128)(2,1)}, u32[]{:S(2)}, u32[]{:S(2)}) collective-permute-start(bf16[4,128,1024]{2,1,0:T(8,128)(2,1)S(1)} %constant_dynamic-slice_fusion.61), channel_id=1, source_target_pairs={{0,12},{4,0},{8,4},{12,8},{1,13},{5,1},{9,5},{13,9},{2,14},{6,2},{... | collective-permute-start | bytes 3145736 | tf_op jit(solution)/shard_map/ppermute | solution.py:437
  193.0 72.3 %collective-permute-start.18 = (bf16[4,3,512,1024]{3,2,1,0:T(8,128)(2,1)}, bf16[4,3,512,1024]{3,2,1,0:T(8,128)(2,1)}, u32[]{:S(2)}, u32[]{:S(2)}) collective-permute-start(bf16[4,3,512,1024]{3,2,1,0:T(8,128)(2,1)} %bitcast.195), channel_id=1, source_target_pairs={{0,16},{16,0},{1,17},{17,1},{2,18},{18,2},{3,19},{19,3},{4,20},{20... | collective-permute-start | bytes 37748744 | tf_op jit(solution)/shard_map/ppermute | solution.py:1045
  240.1 65.5 %collective-permute-start.20 = (bf16[512,1152]{1,0:T(8,128)(2,1)S(1)}, bf16[512,1152]{1,0:T(8,128)(2,1)S(1)}, u32[]{:S(2)}, u32[]{:S(2)}) collective-permute-start(bf16[512,1152]{1,0:T(8,128)(2,1)S(1)} %concatenate.76.x_ref), channel_id=1, source_target_pairs={{0,12},{4,0},{8,4},{12,8},{1,13},{5,1},{9,5},{13,9},{2,14},{6,2},{... | collective-permute-start | bytes 3538952 | tf_op jit(solution)/shard_map/ppermute | solution.py:437
  264.2 52.4 %collective-permute-start.21 = (bf16[512,1152]{1,0:T(8,128)(2,1)S(1)}, bf16[512,1152]{1,0:T(8,128)(2,1)}, u32[]{:S(2)}, u32[]{:S(2)}) collective-permute-start(bf16[512,1152]{1,0:T(8,128)(2,1)S(1)} %concatenate.76.x_ref), channel_id=1, source_target_pairs={{0,4},{4,8},{8,12},{12,0},{1,5},{5,9},{9,13},{13,1},{2,6},{6,10},{... | collective-permute-start | bytes 3538952 | tf_op jit(solution)/shard_map/ppermute | solution.py:437
  304.9 95.1 %collective-permute-start.19 = (bf16[512,1152]{1,0:T(8,128)(2,1)}, bf16[512,1152]{1,0:T(8,128)(2,1)S(1)}, u32[]{:S(2)}, u32[]{:S(2)}) collective-permute-start(bf16[512,1152]{1,0:T(8,128)(2,1)} %copy-done.15), channel_id=1, source_target_pairs={{0,8},{4,12},{8,0},{12,4},{1,9},{5,13},{9,1},{13,5},{2,10},{6,14},... | collective-permute-start | bytes 3538952 | tf_op jit(solution)/shard_map/ppermute | solution.py:437
  355.7 150.5 %collective-permute-start.22 = (bf16[512,1152]{1,0:T(8,128)(2,1)}, bf16[512,1152]{1,0:T(8,128)(2,1)}, u32[]{:S(2)}, u32[]{:S(2)}) collective-permute-start(bf16[512,1152]{1,0:T(8,128)(2,1)} %get-tuple-element.141), channel_id=1, source_target_pairs={{0,4},{4,8},{8,12},{12,0},{1,5},{5,9},{9,13},{13,1},{2,6},{6,10},{... | collective-permute-start | bytes 3538952 | tf_op jit(solution)/shard_map/ppermute | solution.py:437
  396.7 109.5 %collective-permute-start.24 = (bf16[512,1152]{1,0:T(8,128)(2,1)}, bf16[512,1152]{1,0:T(8,128)(2,1)}, u32[]{:S(2)}, u32[]{:S(2)}) collective-permute-start(bf16[512,1152]{1,0:T(8,128)(2,1)} %get-tuple-element.149), channel_id=1, source_target_pairs={{0,12},{4,0},{8,4},{12,8},{1,13},{5,1},{9,5},{13,9},{2,14},{6,2},{... | collective-permute-start | bytes 3538952 | tf_op jit(solution)/shard_map/ppermute | solution.py:437
  440.7 107.7 %collective-permute-start.23 = (bf16[512,1152]{1,0:T(8,128)(2,1)}, bf16[512,1152]{1,0:T(8,128)(2,1)S(1)}, u32[]{:S(2)}, u32[]{:S(2)}) collective-permute-start(bf16[512,1152]{1,0:T(8,128)(2,1)} %get-tuple-element.157), channel_id=1, source_target_pairs={{0,8},{4,12},{8,0},{12,4},{1,9},{5,13},{9,1},{13,5},{2,10},{6,14},... | collective-permute-start | bytes 3538952 | tf_op jit(solution)/shard_map/ppermute | solution.py:437
  506.1 104.1 %collective-permute-start.33 = (bf16[4096,512]{1,0:T(8,128)(2,1)}, bf16[4096,512]{1,0:T(8,128)(2,1)}, u32[]{:S(2)}, u32[]{:S(2)}) collective-permute-start(bf16[4096,512]{1,0:T(8,128)(2,1)} %convolution_convert_fusion.5), channel_id=1, source_target_pairs={{0,16},{16,0},{1,17},{17,1},{2,18},{18,2},{3,19},{19,3},{4,20},{20... | collective-permute-start | bytes 12582920 | tf_op jit(solution)/shard_map/ppermute | solution.py:1045
  506.2 110.0 %collective-permute-start.32 = (bf16[512,4096]{1,0:T(8,128)(2,1)}, bf16[512,4096]{1,0:T(8,128)(2,1)}, u32[]{:S(2)}, u32[]{:S(2)}) collective-permute-start(bf16[512,4096]{1,0:T(8,128)(2,1)} %convolution_convert_fusion.2), channel_id=1, source_target_pairs={{0,16},{16,0},{1,17},{17,1},{2,18},{18,2},{3,19},{19,3},{4,20},{20... | collective-permute-start | bytes 12582920 | tf_op jit(solution)/shard_map/ppermute | solution.py:1045
  506.7 116.0 %collective-permute-start.31 = (bf16[512,4096]{1,0:T(8,128)(2,1)}, bf16[512,4096]{1,0:T(8,128)(2,1)}, u32[]{:S(2)}, u32[]{:S(2)}) collective-permute-start(bf16[512,4096]{1,0:T(8,128)(2,1)} %convolution_convert_fusion.3), channel_id=1, source_target_pairs={{0,16},{16,0},{1,17},{17,1},{2,18},{18,2},{3,19},{19,3},{4,20},{20... | collective-permute-start | bytes 12582920 | tf_op jit(solution)/shard_map/ppermute | solution.py:1045
  630.6 52.0 %collective-permute-start.34 = (bf16[1536,512]{1,0:T(8,128)(2,1)}, bf16[1536,512]{1,0:T(8,128)(2,1)}, u32[]{:S(2)}, u32[]{:S(2)}) collective-permute-start(bf16[1536,512]{1,0:T(8,128)(2,1)} %pad_maximum_fusion.12), channel_id=1, source_target_pairs={{0,1},{1,0},{2,3},{3,2},{4,5},{5,4},{6,7},{7,6},{8,9},{9,8},{10,11... | collective-permute-start | bytes 4718600 | tf_op jit(solution)/shard_map/ppermute | solution.py:1045
  633.4 49.2 %collective-permute-start.35 = (bf16[1536,512]{1,0:T(8,128)(2,1)}, bf16[1536,512]{1,0:T(8,128)(2,1)}, u32[]{:S(2)}, u32[]{:S(2)}) collective-permute-start(bf16[1536,512]{1,0:T(8,128)(2,1)} %pad_maximum_fusion.13), channel_id=1, source_target_pairs={{0,2},{1,3},{2,0},{3,1},{4,6},{5,7},{6,4},{7,5},{8,10},{9,11},{10,... | collective-permute-start | bytes 4718600 | tf_op jit(solution)/shard_map/ppermute | solution.py:1045
  635.2 47.4 %collective-permute-start.36 = (bf16[1536,512]{1,0:T(8,128)(2,1)}, bf16[1536,512]{1,0:T(8,128)(2,1)}, u32[]{:S(2)}, u32[]{:S(2)}) collective-permute-start(bf16[1536,512]{1,0:T(8,128)(2,1)} %pad_maximum_fusion.14), channel_id=1, source_target_pairs={{0,1},{1,0},{2,3},{3,2},{4,5},{5,4},{6,7},{7,6},{8,9},{9,8},{10,11... | collective-permute-start | bytes 4718600 | tf_op jit(solution)/shard_map/ppermute | solution.py:1045
  637.8 44.8 %collective-permute-start.37 = (bf16[1536,512]{1,0:T(8,128)(2,1)}, bf16[1536,512]{1,0:T(8,128)(2,1)}, u32[]{:S(2)}, u32[]{:S(2)}) collective-permute-start(bf16[1536,512]{1,0:T(8,128)(2,1)} %pad_maximum_fusion.15), channel_id=1, source_target_pairs={{0,2},{1,3},{2,0},{3,1},{4,6},{5,7},{6,4},{7,5},{8,10},{9,11},{10,... | collective-permute-start | bytes 4718600 | tf_op jit(solution)/shard_map/ppermute | solution.py:1045
  726.4 46.9 %collective-permute-start.51 = (bf16[1536,512]{1,0:T(8,128)(2,1)}, bf16[1536,512]{1,0:T(8,128)(2,1)}, u32[]{:S(2)}, u32[]{:S(2)}) collective-permute-start(bf16[1536,512]{1,0:T(8,128)(2,1)} %add_convert_fusion.4), channel_id=1, source_target_pairs={{0,2},{1,3},{2,0},{3,1},{4,6},{5,7},{6,4},{7,5},{8,10},{9,11},{10,... | collective-permute-start | bytes 4718600 | tf_op jit(solution)/shard_map/ppermute | solution.py:1045
  727.8 45.6 %collective-permute-start.52 = (bf16[1536,512]{1,0:T(8,128)(2,1)}, bf16[1536,512]{1,0:T(8,128)(2,1)}, u32[]{:S(2)}, u32[]{:S(2)}) collective-permute-start(bf16[1536,512]{1,0:T(8,128)(2,1)} %add_convert_fusion.3), channel_id=1, source_target_pairs={{0,1},{1,0},{2,3},{3,2},{4,5},{5,4},{6,7},{7,6},{8,9},{9,8},{10,11... | collective-permute-start | bytes 4718600 | tf_op jit(solution)/shard_map/ppermute | solution.py:1045
  774.7 52.4 %collective-permute-start.57 = (bf16[4,128,512]{2,1,0:T(8,128)(2,1)}, bf16[4,128,512]{2,1,0:T(8,128)(2,1)}, u32[]{:S(2)}, u32[]{:S(2)}) collective-permute-start(bf16[4,128,512]{2,1,0:T(8,128)(2,1)} %get-tuple-element.345), channel_id=1, source_target_pairs={{0,2},{1,3},{2,0},{3,1},{4,6},{5,7},{6,4},{7,5},{8,10},{9,11},{10,... | collective-permute-start | bytes 1572872 | tf_op jit(solution)/shard_map/ppermute | solution.py:1045
  (131 other events, 1991.0 us)
Sparse Core Ops, SparseCore 0:
  27.1 151.2 all-gather.2
  440.8 113.3 reduce-scatter.1

commit v3 on v2

--- a/solution.py
+++ b/solution.py
@@ -1135,7 +1135,16 @@
         ],
         axis=2,
     )
-    wide_mine = in_order(exchange_parts(wide_hidden, "ep"), "ep").reshape(mine, -1)
+    gate_part, up_part = [
+        jnp.transpose(take_part(weight, dp_index, half, 1), (1, 0, 2)).reshape(half, inner)
+        for weight in (after(w_gate, wide_hidden), after(w_up, wide_hidden))
+    ]
+    down_part = take_part(after(w_down, wide_hidden).reshape(inner, model_width), dp_index, half, 0)
+    weights_here = jnp.stack([gate_part, up_part, down_part])
+    own_weights = lax.all_gather(weights_here, "tp")
+
+    wide_parts = [after(part, weights_here) for part in exchange_parts(wide_hidden, "ep")]
+    wide_mine = in_order(wide_parts, "ep").reshape(mine, -1)
     hidden_mine = wide_mine[:, :model_width]
     routes_mine = wide_mine[:, model_width:].astype(jnp.int32)
 
@@ -1146,22 +1155,13 @@
     first_mine = (normed_first * gain_first).astype(jnp.bfloat16)
     first_rows = gather_halves(first_mine[:, :half], first_mine[:, half:])
 
-    weights_here = jnp.stack(
-        [
-            take_part(weight, dp_index, half, 0)
-            for weight in (
-                jnp.transpose(after(w_gate, wide_hidden), (1, 0, 2)).reshape(model_width, inner),
-                jnp.transpose(after(w_up, wide_hidden), (1, 0, 2)).reshape(model_width, inner),
-                after(w_down, wide_hidden).reshape(inner, model_width),
-            )
-        ]
-    )
-    own_weights = lax.all_gather(weights_here, "tp")
-
-    grads_mine_all = after(take_part(cotangent, tp_index, quarter, 1), first_rows[7])
-    grads_parts = [grads_mine_all] + [
-        shift_by(grads_mine_all, "ep", distance) for distance in range(1, ep_count)
-    ]
+    grads_parts = [take_part(cotangent, tp_index, quarter, 1)]
+    sent = after(grads_parts[0], hidden_mine)
+    grads_parts.append(shift_by(sent, "ep", 1))
+    first_rows[7] = after(first_rows[7], grads_parts[1])
+    for distance in range(3, ep_count, 2):
+        sent = after(sent, grads_parts[1])
+        grads_parts.append(shift_by(sent, "ep", distance))
 
     weights_t = jnp.concatenate([w_query, key_projection_weight, value_projection_weight], axis=1).T
     inverse = 1.0 / 10000.0 ** (jnp.arange(halfway, dtype=jnp.float32) * 2.0 / HEAD_SIZE)
@@ -1179,10 +1179,14 @@
     start_row = starts[None, :]
     attn_t, lse = attend(query_t, key_rows, value_t, start_row, low, mid, block)
 
-    grads_parts = [after(part, attn_t) for part in grads_parts]
-    mixed = mix_heads(tp_me, after(attn_t, *grads_parts), w_out, tp_count, quarter)
+    grads_parts[2:] = [after(part, attn_t) for part in grads_parts[2:]]
+    attn_t = after(attn_t, *grads_parts[2:])
+    mixed = mix_heads(tp_me, attn_t, w_out, tp_count, quarter)
+    for distance in range(2, ep_count, 2):
+        part = shift_by(after(sent, attn_t), "ep", distance)
+        grads_parts.insert(distance, after(part, mixed[0]))
     own_weights = after(own_weights, mixed[0])
-    grads_all = in_order([after(part, mixed[0]) for part in grads_parts], "ep")
+    grads_all = in_order(grads_parts, "ep")
     other_weights = swap(own_weights, "dp", 1)
     chunk_grads = jnp.stack(
         [
@@ -1256,10 +1260,6 @@
 
     out_all = kept.pop(0)
     active, grad_gate, grad_up = [part.reshape(ep_count * mine, tp_count * inner) for part in kept]
-    out_home = lax.psum_scatter(
-        out_all.reshape(ep_count * mine, model_width), "ep", scatter_dimension=0, tiled=True
-    ).reshape(seq_count, quarter, model_width)
-
     def token_half(number):
         return jnp.concatenate(
             [take_part(chunk_tokens[step], number, half, 1) for step in range(ep_count)], axis=0
@@ -1295,22 +1295,34 @@
     )
     grad_low = grad_middle.astype(jnp.bfloat16)
     grad_attn = gather_halves(grad_low[:, :half], grad_low[:, half:])
+    out_home = lax.psum_scatter(
+        after(out_all, grad_low).reshape(ep_count * mine, model_width),
+        "ep",
+        scatter_dimension=0,
+        tiled=True,
+    ).reshape(seq_count, quarter, model_width)
     near_sums = weight_products(dp_index, grad_low)
     grad_attn[6:] = [after(piece, *near_sums) for piece in grad_attn[6:]]
     grad_vec_t, grad_vec, delta, grad_wo = unmix_heads(
         tp_me, grad_attn, w_out, attn_t, kv_width, quarter
     )
     cut = inner // 2
-    sums = [add_low(*pair) for pair in zip(near_sums, far_sums)]
 
     def sum_piece(offset, side):
         place = tp_index ^ offset
-        columns = [
-            lax.dynamic_slice_in_dim(total, place * inner + side * cut, cut, 1) for total in sums[:2]
-        ]
-        return jnp.concatenate(
-            columns + [lax.dynamic_slice_in_dim(sums[2], place * inner + side * cut, cut, 0)], axis=0
-        )
+        pieces = []
+        for number, pair in enumerate(zip(near_sums, far_sums)):
+            pieces.append(
+                add_low(
+                    *(
+                        lax.dynamic_slice_in_dim(
+                            part, place * inner + side * cut, cut, 0 if number == 2 else 1
+                        )
+                        for part in pair
+                    )
+                )
+            )
+        return jnp.concatenate(pieces, axis=0)
 
     first, second = [[sum_piece(offset, side) for offset in range(tp_count)] for side in range(2)]
     first_3, second_3 = swap(first[3], "tp", 1), swap(second[3], "tp", 2)
@@ -1353,7 +1365,17 @@
         )
 
     dense_half = dp_half(jnp.concatenate([grad_qkv_t, grad_wo], axis=0))
-    grad_first = after(jnp.concatenate(reduce_halves(first_parts), axis=1), dense_half)
+    column = model_width // tp_count
+    out_home = after(out_home, grad_qkv_t)
+    out_pieces = [
+        swap(take_part(out_home, tp_index ^ offset, column, 2), "tp", offset)
+        if offset
+        else take_part(out_home, tp_index, column, 2)
+        for offset in range(tp_count)
+    ]
+    grad_first = after(
+        jnp.concatenate(reduce_halves(first_parts), axis=1), dense_half, *out_pieces
+    )
     grad_mine = grad_middle + norm_back(grad_first, normed_first, factor_first, gain_first)
     first_2 = swap(after(add_low(first[2], first_3), grad_mine), "tp", 2)
     second_1 = swap(after(add_low(second[1], second_3), grad_mine), "tp", 1)
@@ -1392,29 +1414,11 @@
         axis=2,
     ).astype(jnp.float32)
 
-    out_home = after(out_home, grad_mine)
-    column = model_width // tp_count
-    block_out = jnp.concatenate(
-        by_quarter(
-            jnp.stack(
-                [
-                    swap(take_part(out_home, tp_index ^ offset, column, 2), "tp", offset)
-                    if offset
-                    else take_part(out_home, tp_index, column, 2)
-                    for offset in range(tp_count)
-                ]
-            )
-        ),
-        axis=1,
-    ).astype(jnp.float32)
-
-    def tp_total(rows):
-        rows = rows + swap(rows, "tp", 1)
-        return rows + swap(rows, "tp", 2)
+    block_out = jnp.concatenate(by_quarter(jnp.stack(out_pieces)), axis=1).astype(jnp.float32)
 
     grad_router = contract_rows(after(second_in, grad_vec_t), grad_logits)
     grad_moe_gain = jnp.sum(after(grad_second, grad_vec_t) * normed_second, axis=0)
-    grad_attn_gain = jnp.sum(after(grad_first, home_pieces[2]) * normed_first, axis=0)
+    grad_attn_gain = jnp.sum(grad_first * normed_first, axis=0)
     dense_home = ep_part(after(dense_half, home_pieces[2]))
     qkv_home = dense_home[: query_width + 2 * kv_width].T
     wo_home = dense_home[query_width + 2 * kv_width :]
@@ -1427,7 +1431,10 @@
         ],
         axis=0,
     )
-    small_home = ep_part(dp_half(tp_total(small)))
+    share = model_width // (2 * ep_count)
+    small_home = take_part(
+        after(lax.psum(small, ("dp", "ep", "tp")), home_pieces[6]), dp_index * ep_count + ep_index, share, 1
+    )
     return (
         block_out,
         grad_in,

time: 870 us -> 851 us (0.978)
  starting transfers between devices: 116 us -> 67.3 us
  waiting for transfers between devices: 259 us -> 277 us
  other arithmetic: 71.8 us -> 81.5 us
    ppermute x21 -> x18, starting transfers between devices: 74 us -> 24.5 us  [shift_by(): lax.ppermute(values, axis_name, [(source, (source + distance) % count) fo...]
    psum x0 -> x1, waiting for transfers between devices: none -> 39 us  [per_device_by_sequence(): lax.psum(small, ('dp', 'ep', 'tp'))]
    ppermute x21 -> x18, waiting for transfers between devices: 136 us -> 115 us  [shift_by(): lax.ppermute(values, axis_name, [(source, (source + distance) % count) fo...]
    ppermute x47 -> x44, waiting for transfers between devices: 123 us -> 121 us  [swap(): lax.ppermute(values, axis_name, [(source, source ^ distance) for source i...]
    ppermute x47 -> x44, starting transfers between devices: 42.3 us -> 42.7 us  [swap(): lax.ppermute(values, axis_name, [(source, source ^ distance) for source i...]
  transfers between devices with their start and end apart: 70 -> 65, of which waited for: 24 -> 30; matrix products, arithmetic and copies ran while one was open for 20% -> 22% of each run, Pallas kernels for 31% -> 31%
where the time goes in v3:
time: 851 us; the launch traced here: 842 us
  waiting for transfers between devices  277 us (33%)
  Pallas kernels  265 us (31%)
  matrix products  83.8 us (10%)
  other arithmetic  81.5 us (10%)
  starting transfers between devices  67.3 us (8%)
  local copies, waits for them, and re-layouts  52.7 us (6%)
  between operations  15.6 us (2%)
    pallas_call x4, Pallas kernels, expert_chunk(): pl.pallas_call(expert_kernel, grid_spec=pltpu.PrefetchScalarGridSpec(num_...  159 us
    ppermute x44, waiting for transfers between devices, swap(): lax.ppermute(values, axis_name, [(source, source ^ distance) for source i...  121 us
    ppermute x18, waiting for transfers between devices, shift_by(): lax.ppermute(values, axis_name, [(source, (source + distance) % count) fo...  115 us
    dot_general x7, matrix products, contract_rows(): lax.dot_general(left_side, right_side, (((0,), (0,)), ((), ())), preferre...  82.8 us
    pallas_call x1, Pallas kernels, attend_back(): pl.pallas_call(attend_back_kernel, grid_spec=pltpu.PrefetchScalarGridSpec...  44.1 us
    ppermute x44, starting transfers between devices, swap(): lax.ppermute(values, axis_name, [(source, source ^ distance) for source i...  42.7 us
    psum x1, waiting for transfers between devices, per_device_by_sequence(): lax.psum(small, ('dp', 'ep', 'tp'))  39 us
    pallas_call x1, Pallas kernels, attend(): pl.pallas_call(attend_kernel, grid_spec=pltpu.PrefetchScalarGridSpec(num_...  31.5 us
  transfers between devices with their start and end apart: 65, of which 30 were waited for; matrix products, arithmetic and copies ran while one was open for 22% of the time, Pallas kernels for 31%

profile of v3, /device:TPU:0, one launch (start us, length us, event | category | flops | bytes accessed | tf_op | source)
XLA Modules:
  0.0 842.5 jit_solution(2106189341521774399)
XLA Ops:
  39.3 40.0 %collective-permute-done.1 = bf16[128,1032]{1,0:T(8,128)(2,1)S(1)} collective-permute-done((bf16[128,1032]{1,0:T(8,128)(2,1)S(1)}, bf16[128,1032]{1,0:T(8,128)(2,1)S(1)}, u32[]{:S(2)}, u32[]{:S(2)}) %collective-permute-start.1) | collective-permute-done | bytes 264224 | tf_op jit(solution)/shard_map/ppermute | solution.py:437
  102.9 32.8 %collective-permute-done.8.refs_7_ = bf16[512,512]{1,0:T(8,128)(2,1)S(1)} collective-permute-done((bf16[512,512]{1,0:T(8,128)(2,1)}, bf16[512,512]{1,0:T(8,128)(2,1)S(1)}, u32[]{:S(2)}, u32[]{:S(2)}) %collective-permute-start.8) | collective-permute-done | bytes 524320 | tf_op jit(solution)/shard_map/ppermute | solution.py:1045
  147.3 31.5 %attend.1 = (bf16[256,2048]{1,0:T(8,128)(2,1)}, f32[4,1,2048]{2,1,0:T(1,128)}) custom-call(s32[4]{0:T(128)} %get-tuple-element.372.low_ref, s32[4]{0:T(128)} %get-tuple-element.371.mid_ref, bf16[4,128,2048]{2,1,0:T(8,128)(2,1)} %get-tuple-element.118.q_ref.qt_ref, bf16[2048,128]{1,0:T(8,128)(2,1)} %get-tuple-element.119.k_ref, ...), custom_call_target="tpu_custom_call" | custom-call | flops 8589934592 | bytes 8388608 | tf_op jit(solution)/shard_map/attend/pallas_call | solution.py:484
  193.1 9.8 %collective-permute-done.15 = bf16[512,512]{1,0:T(8,128)(2,1)} collective-permute-done((bf16[512,512]{1,0:T(8,128)(2,1)}, bf16[512,512]{1,0:T(8,128)(2,1)}, u32[]{:S(2)}, u32[]{:S(2)}) %collective-permute-start.15) | collective-permute-done | bytes 524320 | tf_op jit(solution)/shard_map/ppermute | solution.py:1045
  207.5 20.9 %collective-permute-done.17 = bf16[4,128,1024]{2,1,0:T(8,128)(2,1)} collective-permute-done((bf16[4,128,1024]{2,1,0:T(8,128)(2,1)S(1)}, bf16[4,128,1024]{2,1,0:T(8,128)(2,1)}, u32[]{:S(2)}, u32[]{:S(2)}) %collective-permute-start.17) | collective-permute-done | bytes 1048608 | tf_op jit(solution)/shard_map/ppermute | solution.py:437
  249.4 39.5 %expert_chunk.4 = (bf16[512,1152]{1,0:T(8,128)(2,1)}, bf16[4,4,128,1024]{3,2,1,0:T(8,128)(2,1)}, bf16[4,512,4096]{2,1,0:T(8,128)(2,1)}, bf16[4,512,4096]{2,1,0:T(8,128)(2,1)}, bf16[4,512,4096]{2,1,0:T(8,128)(2,1)}) custom-call(s32[2]{0:T(128)} %pad_add_fusion.1.me_ref, bf16[512,1152]{1,0:T(8,128)(2,1)} %copy-done.14, ...), custom_call_target="tpu_custom_call" | custom-call | flops 25769803776 | bytes 37748736 | tf_op jit(solution)/shard_map/expert_chunk/pallas_call | solution.py:722
  301.0 39.3 %expert_chunk.5 = (bf16[512,1152]{1,0:T(8,128)(2,1)}, bf16[4,4,128,1024]{3,2,1,0:T(8,128)(2,1)}, bf16[4,512,4096]{2,1,0:T(8,128)(2,1)}, bf16[4,512,4096]{2,1,0:T(8,128)(2,1)}, bf16[4,512,4096]{2,1,0:T(8,128)(2,1)}) custom-call(s32[2]{0:T(128)} %get-tuple-element.374.me_ref, ...), custom_call_target="tpu_custom_call", output_to_operand_aliasing={{1}: (7, {}), {2}: (8, {}), {3}: (9, {}), {4}: (10, {})} | custom-call | flops 25769803776 | bytes 37748736 | tf_op jit(solution)/shard_map/expert_chunk/pallas_call | solution.py:722
  342.3 40.8 %expert_chunk.6 = (bf16[512,1152]{1,0:T(8,128)(2,1)}, bf16[4,4,128,1024]{3,2,1,0:T(8,128)(2,1)}, bf16[4,512,4096]{2,1,0:T(8,128)(2,1)}, bf16[4,512,4096]{2,1,0:T(8,128)(2,1)}, bf16[4,512,4096]{2,1,0:T(8,128)(2,1)}) custom-call(s32[2]{0:T(128)} %pad_add_fusion.3.me_ref, ...), custom_call_target="tpu_custom_call", output_to_operand_aliasing={{1}: (7, {}), {2}: (8, {}), {3}: (9, {}), {4}: (10, {})} | custom-call | flops 25769803776 | bytes 37748736 | tf_op jit(solution)/shard_map/expert_chunk/pallas_call | solution.py:722
  386.5 39.0 %expert_chunk.7 = (bf16[512,1152]{1,0:T(8,128)(2,1)}, bf16[4,4,128,1024]{3,2,1,0:T(8,128)(2,1)}, bf16[4,512,4096]{2,1,0:T(8,128)(2,1)}, bf16[4,512,4096]{2,1,0:T(8,128)(2,1)}, bf16[4,512,4096]{2,1,0:T(8,128)(2,1)}) custom-call(s32[2]{0:T(128)} %get-tuple-element.373.me_ref, ...), custom_call_target="tpu_custom_call", output_to_operand_aliasing={{1}: (7, {}), {2}: (8, {}), {3}: (9, {}), {4}: (10, {})} | custom-call | flops 25769803776 | bytes 37748736 | tf_op jit(solution)/shard_map/expert_chunk/pallas_call | solution.py:722
  426.9 14.0 %convolution_convert_fusion.3 = bf16[512,4096]{1,0:T(8,128)(2,1)} fusion(bf16[2048,512]{1,0:T(8,128)(2,1)S(1)} %pad_maximum_fusion.6, bf16[2048,4096]{1,0:T(8,128)(2,1)} %bitcast.196), kind=kOutput, calls=%fused_computation.4 | convolution fusion | flops 8592031744 | bytes 23068672 | tf_op jit(solution)/shard_map/dot_general | solution.py:22
  440.9 14.2 %convolution_convert_fusion.5 = bf16[4096,512]{1,0:T(8,128)(2,1)} fusion(bf16[2048,4096]{1,0:T(8,128)(2,1)} %bitcast.194, bf16[2048,512]{1,0:T(8,128)(2,1)S(1)} %copy-done.23), kind=kOutput, calls=%fused_computation.6 | convolution fusion | flops 8592031744 | bytes 23068672 | tf_op jit(solution)/shard_map/dot_general | solution.py:22
  455.1 13.9 %convolution_convert_fusion.2 = bf16[512,4096]{1,0:T(8,128)(2,1)} fusion(bf16[2048,512]{1,0:T(8,128)(2,1)S(1)} %pad_maximum_fusion.6, bf16[2048,4096]{1,0:T(8,128)(2,1)} %bitcast.198), kind=kOutput, calls=%fused_computation.3 | convolution fusion | flops 8592031744 | bytes 23068672 | tf_op jit(solution)/shard_map/dot_general | solution.py:22
  485.2 15.5 %convolution_convert_fusion.4 = bf16[4096,512]{1,0:T(8,128)(2,1)} fusion(bf16[2048,4096]{1,0:T(8,128)(2,1)} %bitcast.195, bf16[2048,512]{1,0:T(8,128)(2,1)} %get-tuple-element.170), kind=kOutput, calls=%fused_computation.5 | convolution fusion | flops 8592031744 | bytes 23068672 | tf_op jit(solution)/shard_map/dot_general | solution.py:22
  501.6 14.1 %convolution_convert_fusion.1 = bf16[512,4096]{1,0:T(8,128)(2,1)} fusion(bf16[2048,512]{1,0:T(8,128)(2,1)S(1)} %copy-done.25, bf16[2048,4096]{1,0:T(8,128)(2,1)} %bitcast.197), kind=kOutput, calls=%fused_computation.2 | convolution fusion | flops 8592031744 | bytes 23068672 | tf_op jit(solution)/shard_map/dot_general | solution.py:22
  519.0 10.7 %convolution_convert_fusion = bf16[512,4096]{1,0:T(8,128)(2,1)} fusion(bf16[2048,512]{1,0:T(8,128)(2,1)S(1)} %copy-done.25, bf16[2048,4096]{1,0:T(8,128)(2,1)S(1)} %bitcast.201), kind=kOutput, calls=%fused_computation.1 | convolution fusion | flops 8592031744 | bytes 23068672 | tf_op jit(solution)/shard_map/dot_general | solution.py:22
  564.2 44.1 %attend_back.1 = (f32[256,2048]{1,0:T(8,128)}, f32[2048,128]{1,0:T(8,128)}, f32[2048,128]{1,0:T(8,128)}) custom-call(s32[4]{0:T(128)} %get-tuple-element.372.low_ref, s32[4]{0:T(128)} %get-tuple-element.371.mid_ref, bf16[4,128,2048]{2,1,0:T(8,128)(2,1)} %get-tuple-element.118.q_ref.qt_ref, bf16[4,2048,128]{2,1,0:T(8,128)(2,1)} %get-tuple-element.168.q_ref, ...), custom_call_target="tpu_custom_call" | custom-call | flops 21474836480 | bytes 16777216 | tf_op jit(solution)/shard_map/attend_back/pallas_call | solution.py:596
  608.3 13.8 %collective-permute-done.36 = bf16[1536,512]{1,0:T(8,128)(2,1)} collective-permute-done((bf16[1536,512]{1,0:T(8,128)(2,1)}, bf16[1536,512]{1,0:T(8,128)(2,1)}, u32[]{:S(2)}, u32[]{:S(2)}) %collective-permute-start.36) | collective-permute-done | bytes 1572896 | tf_op jit(solution)/shard_map/ppermute | solution.py:1045
  624.0 10.0 %unproject.1 = (f32[512,1024]{1,0:T(8,128)}, bf16[512,512]{1,0:T(8,128)(2,1)}, bf16[512,512]{1,0:T(8,128)(2,1)}, bf16[512,512]{1,0:T(8,128)(2,1)}, bf16[512,512]...) custom-call(s32[1]{0:T(128)} %bitcast.17.me_ref, ...), custom_call_target="tpu_custom_call" | custom-call | flops 4294967296 | bytes 12582912 | tf_op jit(solution)/shard_map/unproject/pallas_call | solution.py:1015
  656.0 11.0 %collective-permute-done.46 = bf16[512,512]{1,0:T(8,128)(2,1)S(1)} collective-permute-done((bf16[512,512]{1,0:T(8,128)(2,1)S(1)}, bf16[512,512]{1,0:T(8,128)(2,1)S(1)}, u32[]{:S(2)}, u32[]{:S(2)}) %collective-permute-start.46) | collective-permute-done | bytes 524320 | tf_op jit(solution)/shard_map/ppermute | solution.py:1045
  697.8 10.2 %collective-permute-done.49 = bf16[128,1024]{1,0:T(8,128)(2,1)S(1)} collective-permute-done((bf16[128,1024]{1,0:T(8,128)(2,1)S(1)}, bf16[128,1024]{1,0:T(8,128)(2,1)S(1)}, u32[]{:S(2)}, u32[]{:S(2)}) %collective-permute-start.49) | collective-permute-done | bytes 262176 | tf_op jit(solution)/shard_map/ppermute | solution.py:437
  708.4 10.9 %collective-permute-done.51 = bf16[1536,512]{1,0:T(8,128)(2,1)} collective-permute-done((bf16[1536,512]{1,0:T(8,128)(2,1)}, bf16[1536,512]{1,0:T(8,128)(2,1)}, u32[]{:S(2)}, u32[]{:S(2)}) %collective-permute-start.51) | collective-permute-done | bytes 1572896 | tf_op jit(solution)/shard_map/ppermute | solution.py:1045
  729.3 14.3 %collective-permute-done.53 = bf16[4,128,512]{2,1,0:T(8,128)(2,1)} collective-permute-done((bf16[4,128,512]{2,1,0:T(8,128)(2,1)S(1)}, bf16[4,128,512]{2,1,0:T(8,128)(2,1)}, u32[]{:S(2)}, u32[]{:S(2)}) %collective-permute-start.53) | collective-permute-done | bytes 524320 | tf_op jit(solution)/shard_map/ppermute | solution.py:1045
  757.8 15.7 %collective-permute-done.60 = f32[768,128]{1,0:T(8,128)S(1)} collective-permute-done((f32[768,128]{1,0:T(8,128)S(1)}, f32[768,128]{1,0:T(8,128)S(1)}, u32[]{:S(2)}, u32[]{:S(2)}) %collective-permute-start.60) | collective-permute-done | bytes 393248 | tf_op jit(solution)/shard_map/ppermute | solution.py:437
  788.3 39.0 %all-reduce.2.cloned.1.call-done = f32[40,1024]{1,0:T(8,128)} async-done(((f32[40,1024]{1,0:T(8,128)}), f32[40,1024]{1,0:T(8,128)}) %all-reduce.2.cloned.1.call-update) | async-done | bytes 163856 | tf_op jit(solution)/shard_map/psum | solution.py:1436
  (433 shorter events, 281.9 us)
Async XLA Ops:
  7.2 178.8 %all-gather.3.cloned.1.call-start = ((), (), s32[]{:S(2)}) async-start(), calls=%async_computation.3 | async-start | bytes 15728640 | tf_op jit(solution)/shard_map/all_gather | solution.py:1144
  24.5 644.4 %reduce-scatter.2.cloned.1.call-start = ((), (), s32[]{:S(2)}) async-start(), calls=%async_computation.1 | async-start | bytes 5242880 | tf_op jit(solution)/shard_map/reduce_scatter | solution.py:1298
  31.5 47.8 %collective-permute-start.1 = (bf16[128,1032]{1,0:T(8,128)(2,1)S(1)}, bf16[128,1032]{1,0:T(8,128)(2,1)S(1)}, u32[]{:S(2)}, u32[]{:S(2)}) collective-permute-start(bf16[128,1032]{1,0:T(8,128)(2,1)S(1)} %get-tuple-element.335), channel_id=1, source_target_pairs={{0,8},{4,12},{8,0},{12,4},{1,9},{5,13},{9,1},{13,5},{2,10},{6,14},... | collective-permute-start | bytes 792584 | tf_op jit(solution)/shard_map/ppermute | solution.py:437
  31.5 47.8 %collective-permute-start = (bf16[128,1032]{1,0:T(8,128)(2,1)S(1)}, bf16[128,1032]{1,0:T(8,128)(2,1)S(1)}, u32[]{:S(2)}, u32[]{:S(2)}) collective-permute-start(bf16[128,1032]{1,0:T(8,128)(2,1)S(1)} %get-tuple-element.334), channel_id=1, source_target_pairs={{0,4},{4,8},{8,12},{12,0},{1,5},{5,9},{9,13},{13,1},{2,6},{6,10},{... | collective-permute-start | bytes 792584 | tf_op jit(solution)/shard_map/ppermute | solution.py:437
  32.6 69.1 %collective-permute-start.9 = (bf16[4,128,1024]{2,1,0:T(8,128)(2,1)S(1)}, bf16[4,128,1024]{2,1,0:T(8,128)(2,1)}, u32[]{:S(2)}, u32[]{:S(2)}) collective-permute-start(bf16[4,128,1024]{2,1,0:T(8,128)(2,1)S(1)} %copy-done.22), channel_id=1, source_target_pairs={{0,4},{4,8},{8,12},{12,0},{1,5},{5,9},{9,13},{13,1},{2,6},{6,10},{... | collective-permute-start | bytes 3145736 | tf_op jit(solution)/shard_map/ppermute | solution.py:437
  88.7 47.0 %collective-permute-start.4 = (bf16[512,512]{1,0:T(8,128)(2,1)}, bf16[512,512]{1,0:T(8,128)(2,1)S(1)}, u32[]{:S(2)}, u32[]{:S(2)}) collective-permute-start(bf16[512,512]{1,0:T(8,128)(2,1)} %get-tuple-element.359.refs_1_), channel_id=1, source_target_pairs={{0,1},{1,0},{2,3},{3,2},{4,5},{5,4},{6,7},{7,6},{8,9},{9,8},{10,11... | collective-permute-start | bytes 1572872 | tf_op jit(solution)/shard_map/ppermute | solution.py:1045
  101.6 77.3 %collective-permute-start.10 = (bf16[4,128,1024]{2,1,0:T(8,128)(2,1)S(1)}, bf16[4,128,1024]{2,1,0:T(8,128)(2,1)S(1)}, u32[]{:S(2)}, u32[]{:S(2)}) collective-permute-start(bf16[4,128,1024]{2,1,0:T(8,128)(2,1)S(1)} %copy-done.22), channel_id=1, source_target_pairs={{0,12},{4,0},{8,4},{12,8},{1,13},{5,1},{9,5},{13,9},{2,14},{6,2},{... | collective-permute-start | bytes 3145736 | tf_op jit(solution)/shard_map/ppermute | solution.py:437
  186.0 63.3 %collective-permute-start.18 = (bf16[4,3,512,1024]{3,2,1,0:T(8,128)(2,1)}, bf16[4,3,512,1024]{3,2,1,0:T(8,128)(2,1)}, u32[]{:S(2)}, u32[]{:S(2)}) collective-permute-start(bf16[4,3,512,1024]{3,2,1,0:T(8,128)(2,1)} %bitcast.189), channel_id=1, source_target_pairs={{0,16},{16,0},{1,17},{17,1},{2,18},{18,2},{3,19},{19,3},{4,20},{20... | collective-permute-start | bytes 37748744 | tf_op jit(solution)/shard_map/ppermute | solution.py:1045
  192.6 49.9 %collective-permute-start.14 = (bf16[512,512]{1,0:T(8,128)(2,1)}, bf16[512,512]{1,0:T(8,128)(2,1)S(1)}, u32[]{:S(2)}, u32[]{:S(2)}) collective-permute-start(bf16[512,512]{1,0:T(8,128)(2,1)} %get-tuple-element.130), channel_id=1, source_target_pairs={{0,2},{1,3},{2,0},{3,1},{4,6},{5,7},{6,4},{7,5},{8,10},{9,11},{10,... | collective-permute-start | bytes 1572872 | tf_op jit(solution)/shard_map/ppermute | solution.py:1045
  246.9 50.9 %collective-permute-start.20 = (bf16[512,1152]{1,0:T(8,128)(2,1)S(1)}, bf16[512,1152]{1,0:T(8,128)(2,1)S(1)}, u32[]{:S(2)}, u32[]{:S(2)}) collective-permute-start(bf16[512,1152]{1,0:T(8,128)(2,1)S(1)} %concatenate.76.x_ref), channel_id=1, source_target_pairs={{0,12},{4,0},{8,4},{12,8},{1,13},{5,1},{9,5},{13,9},{2,14},{6,2},{... | collective-permute-start | bytes 3538952 | tf_op jit(solution)/shard_map/ppermute | solution.py:437
  248.7 52.3 %collective-permute-start.21 = (bf16[512,1152]{1,0:T(8,128)(2,1)S(1)}, bf16[512,1152]{1,0:T(8,128)(2,1)S(1)}, u32[]{:S(2)}, u32[]{:S(2)}) collective-permute-start(bf16[512,1152]{1,0:T(8,128)(2,1)S(1)} %concatenate.76.x_ref), channel_id=1, source_target_pairs={{0,4},{4,8},{8,12},{12,0},{1,5},{5,9},{9,13},{13,1},{2,6},{6,10},{... | collective-permute-start | bytes 3538952 | tf_op jit(solution)/shard_map/ppermute | solution.py:437
  288.9 96.4 %collective-permute-start.19 = (bf16[512,1152]{1,0:T(8,128)(2,1)}, bf16[512,1152]{1,0:T(8,128)(2,1)}, u32[]{:S(2)}, u32[]{:S(2)}) collective-permute-start(bf16[512,1152]{1,0:T(8,128)(2,1)} %copy-done.14), channel_id=1, source_target_pairs={{0,8},{4,12},{8,0},{12,4},{1,9},{5,13},{9,1},{13,5},{2,10},{6,14},... | collective-permute-start | bytes 3538952 | tf_op jit(solution)/shard_map/ppermute | solution.py:437
  340.3 128.7 %collective-permute-start.22 = (bf16[512,1152]{1,0:T(8,128)(2,1)}, bf16[512,1152]{1,0:T(8,128)(2,1)S(1)}, u32[]{:S(2)}, u32[]{:S(2)}) collective-permute-start(bf16[512,1152]{1,0:T(8,128)(2,1)} %get-tuple-element.144), channel_id=1, source_target_pairs={{0,4},{4,8},{8,12},{12,0},{1,5},{5,9},{9,13},{13,1},{2,6},{6,10},{... | collective-permute-start | bytes 3538952 | tf_op jit(solution)/shard_map/ppermute | solution.py:437
  383.1 85.9 %collective-permute-start.24 = (bf16[512,1152]{1,0:T(8,128)(2,1)}, bf16[512,1152]{1,0:T(8,128)(2,1)}, u32[]{:S(2)}, u32[]{:S(2)}) collective-permute-start(bf16[512,1152]{1,0:T(8,128)(2,1)} %get-tuple-element.152), channel_id=1, source_target_pairs={{0,12},{4,0},{8,4},{12,8},{1,13},{5,1},{9,5},{13,9},{2,14},{6,2},{... | collective-permute-start | bytes 3538952 | tf_op jit(solution)/shard_map/ppermute | solution.py:437
  425.5 51.6 %collective-permute-start.23 = (bf16[512,1152]{1,0:T(8,128)(2,1)}, bf16[512,1152]{1,0:T(8,128)(2,1)S(1)}, u32[]{:S(2)}, u32[]{:S(2)}) collective-permute-start(bf16[512,1152]{1,0:T(8,128)(2,1)} %get-tuple-element.160), channel_id=1, source_target_pairs={{0,8},{4,12},{8,0},{12,4},{1,9},{5,13},{9,1},{13,5},{2,10},{6,14},... | collective-permute-start | bytes 3538952 | tf_op jit(solution)/shard_map/ppermute | solution.py:437
  469.0 70.2 %collective-permute-start.33 = (bf16[4096,512]{1,0:T(8,128)(2,1)}, bf16[4096,512]{1,0:T(8,128)(2,1)}, u32[]{:S(2)}, u32[]{:S(2)}) collective-permute-start(bf16[4096,512]{1,0:T(8,128)(2,1)} %convolution_convert_fusion.5), channel_id=1, source_target_pairs={{0,16},{16,0},{1,17},{17,1},{2,18},{18,2},{3,19},{19,3},{4,20},{20... | collective-permute-start | bytes 12582920 | tf_op jit(solution)/shard_map/ppermute | solution.py:1045
  469.1 76.0 %collective-permute-start.32 = (bf16[512,4096]{1,0:T(8,128)(2,1)}, bf16[512,4096]{1,0:T(8,128)(2,1)}, u32[]{:S(2)}, u32[]{:S(2)}) collective-permute-start(bf16[512,4096]{1,0:T(8,128)(2,1)} %convolution_convert_fusion.2), channel_id=1, source_target_pairs={{0,16},{16,0},{1,17},{17,1},{2,18},{18,2},{3,19},{19,3},{4,20},{20... | collective-permute-start | bytes 12582920 | tf_op jit(solution)/shard_map/ppermute | solution.py:1045
  469.6 80.6 %collective-permute-start.31 = (bf16[512,4096]{1,0:T(8,128)(2,1)}, bf16[512,4096]{1,0:T(8,128)(2,1)}, u32[]{:S(2)}, u32[]{:S(2)}) collective-permute-start(bf16[512,4096]{1,0:T(8,128)(2,1)} %convolution_convert_fusion.3), channel_id=1, source_target_pairs={{0,16},{16,0},{1,17},{17,1},{2,18},{18,2},{3,19},{19,3},{4,20},{20... | collective-permute-start | bytes 12582920 | tf_op jit(solution)/shard_map/ppermute | solution.py:1045
  482.6 344.8 %all-reduce.2.cloned.1.call-start = ((), (), s32[]{:S(2)}) async-start(), calls=%async_computation.2 | async-start | bytes 327680 | tf_op jit(solution)/shard_map/psum | solution.py:1436
  556.3 52.0 %collective-permute-start.34 = (bf16[1536,512]{1,0:T(8,128)(2,1)}, bf16[1536,512]{1,0:T(8,128)(2,1)}, u32[]{:S(2)}, u32[]{:S(2)}) collective-permute-start(bf16[1536,512]{1,0:T(8,128)(2,1)} %pad_maximum_fusion.12), channel_id=1, source_target_pairs={{0,1},{1,0},{2,3},{3,2},{4,5},{5,4},{6,7},{7,6},{8,9},{9,8},{10,11... | collective-permute-start | bytes 4718600 | tf_op jit(solution)/shard_map/ppermute | solution.py:1045
  557.8 50.5 %collective-permute-start.35 = (bf16[1536,512]{1,0:T(8,128)(2,1)}, bf16[1536,512]{1,0:T(8,128)(2,1)}, u32[]{:S(2)}, u32[]{:S(2)}) collective-permute-start(bf16[1536,512]{1,0:T(8,128)(2,1)} %pad_maximum_fusion.13), channel_id=1, source_target_pairs={{0,2},{1,3},{2,0},{3,1},{4,6},{5,7},{6,4},{7,5},{8,10},{9,11},{10,... | collective-permute-start | bytes 4718600 | tf_op jit(solution)/shard_map/ppermute | solution.py:1045
  559.7 62.3 %collective-permute-start.36 = (bf16[1536,512]{1,0:T(8,128)(2,1)}, bf16[1536,512]{1,0:T(8,128)(2,1)}, u32[]{:S(2)}, u32[]{:S(2)}) collective-permute-start(bf16[1536,512]{1,0:T(8,128)(2,1)} %pad_maximum_fusion.14), channel_id=1, source_target_pairs={{0,1},{1,0},{2,3},{3,2},{4,5},{5,4},{6,7},{7,6},{8,9},{9,8},{10,11... | collective-permute-start | bytes 4718600 | tf_op jit(solution)/shard_map/ppermute | solution.py:1045
  562.2 61.8 %collective-permute-start.37 = (bf16[1536,512]{1,0:T(8,128)(2,1)}, bf16[1536,512]{1,0:T(8,128)(2,1)}, u32[]{:S(2)}, u32[]{:S(2)}) collective-permute-start(bf16[1536,512]{1,0:T(8,128)(2,1)} %pad_maximum_fusion.15), channel_id=1, source_target_pairs={{0,2},{1,3},{2,0},{3,1},{4,6},{5,7},{6,4},{7,5},{8,10},{9,11},{10,... | collective-permute-start | bytes 4718600 | tf_op jit(solution)/shard_map/ppermute | solution.py:1045
  721.3 56.6 %collective-permute-start.56 = (bf16[4,128,512]{2,1,0:T(8,128)(2,1)S(1)}, bf16[4,128,512]{2,1,0:T(8,128)(2,1)S(1)}, u32[]{:S(2)}, u32[]{:S(2)}) collective-permute-start(bf16[4,128,512]{2,1,0:T(8,128)(2,1)S(1)} %get-tuple-element.339), channel_id=1, source_target_pairs={{0,1},{1,0},{2,3},{3,2},{4,5},{5,4},{6,7},{7,6},{8,9},{9,8},{10,11... | collective-permute-start | bytes 1572872 | tf_op jit(solution)/shard_map/ppermute | solution.py:1045
  (125 other events, 1860.7 us)
Sparse Core Ops, SparseCore 0:
  24.6 161.3 all-gather.2
  482.7 76.4 reduce-scatter.1
  693.4 133.8 all-reduce.1

commit v4 on v3

--- a/solution.py
+++ b/solution.py
@@ -782,12 +782,30 @@
         rows_ref[pl.ds(place, quarter), columns] = piece[...]
 
 
-def split_pieces(me, rows_ref, pieces):
-    quarter, half = pieces[0].shape
-    for number, piece in enumerate(pieces):
-        place = pl.multiple_of((me ^ (number // 2)) * quarter, quarter)
-        columns = slice(number % 2 * half, (number % 2 + 1) * half)
-        piece[...] = rows_ref[pl.ds(place, quarter), columns]
+def split_pieces(me, rows_ref, results):
+    quarter, half = results[0].shape
+
+    def rows(offset, side):
+        place = pl.multiple_of((me ^ offset) * quarter, quarter)
+        return rows_ref[pl.ds(place, quarter), side * half : (side + 1) * half]
+
+    for result, (offset, side) in zip(results, ((0, 0), (0, 1), (2, 0), (1, 1))):
+        result[...] = rows(offset, side)
+    for number in range(2):
+        results[4][number] = rows((1, 3)[number], 0)
+        results[5][number] = rows((2, 3)[number], 1)
+
+
+def split_specs(quarter, half):
+    return [pl.BlockSpec((quarter, half), lambda i, *_: (i, 0))] * 4 + [
+        pl.BlockSpec((2, quarter, half), lambda i, *_: (0, i, 0))
+    ] * 2
+
+
+def split_shapes(rows, half):
+    return [jax.ShapeDtypeStruct((rows, half), jnp.bfloat16)] * 4 + [
+        jax.ShapeDtypeStruct((2, rows, half), jnp.bfloat16)
+    ] * 2
 
 
 def piece_specs(pieces, quarter, half):
@@ -896,10 +914,10 @@
                 pl.BlockSpec((query_width, width), lambda i, *_: (0, i)),
                 pl.BlockSpec((query_width, model_width), lambda i, *_: (0, 0)),
             ],
-            out_specs=piece_specs(2 * parts, quarter, half),
+            out_specs=split_specs(quarter, half),
             scratch_shapes=[pltpu.VMEM((width, model_width), jnp.bfloat16)],
         ),
-        out_shape=[jax.ShapeDtypeStruct((blocks * quarter, half), jnp.bfloat16)] * (2 * parts),
+        out_shape=split_shapes(blocks * quarter, half),
         compiler_params=pltpu.CompilerParams(vmem_limit_bytes=VMEM_BYTES),
         cost_estimate=pl.CostEstimate(
             flops=2 * length * model_width * query_width,
@@ -978,8 +996,7 @@
 
 
 def unproject_kernel(me_ref, gq_ref, gk_ref, gv_ref, cos_ref, sin_ref, wt_ref, *refs):
-    count = (len(refs) - 2) // 2
-    pieces, gw_ref, results, rows_ref = refs[:count], refs[count], refs[count + 1 : -1], refs[-1]
+    pieces, (gw_ref, gain_ref, *results), rows_ref = refs[:-9], refs[-9:-1], refs[-1]
     width = gq_ref.shape[1]
     cosine, sine = cos_ref[...], -sin_ref[...]
     scale = HEAD_SIZE ** (-0.5)
@@ -994,9 +1011,11 @@
     @pl.when(pl.program_id(0) == 0)
     def _():
         gw_ref[...] = jnp.zeros_like(gw_ref)
+        gain_ref[...] = jnp.zeros_like(gain_ref)
 
     gw_ref[...] += matrix_multiply(grads.astype(jnp.bfloat16), rows_ref[...])
     out = matrix_multiply(grads.T.astype(jnp.bfloat16), wt_ref[...])
+    gain_ref[:1, :] += jnp.sum(out * rows_ref[...].astype(jnp.float32), axis=0, keepdims=True)
     rows_ref[...] = out.astype(jnp.bfloat16)
     split_pieces(me_ref[0], rows_ref, results)
 
@@ -1025,11 +1044,15 @@
             table,
             whole,
         ] + parts,
-        out_specs=[whole] + parts,
+        out_specs=[whole, pl.BlockSpec((8, model_width), lambda i, *_: (0, 0))]
+        + split_specs(quarter, half),
         scratch_shapes=[pltpu.VMEM((width, model_width), jnp.bfloat16)],
         ),
-        out_shape=[jax.ShapeDtypeStruct(weights_t.shape, jnp.float32)]
-        + [jax.ShapeDtypeStruct((rows, half), jnp.bfloat16)] * len(pieces),
+        out_shape=[
+            jax.ShapeDtypeStruct(weights_t.shape, jnp.float32),
+            jax.ShapeDtypeStruct((8, model_width), jnp.float32),
+        ]
+        + split_shapes(rows, half),
         compiler_params=pltpu.CompilerParams(vmem_limit_bytes=VMEM_BYTES),
         cost_estimate=pl.CostEstimate(
             flops=4 * length * model_width * weights_t.shape[0],
@@ -1049,6 +1072,11 @@
     return lax.optimization_barrier((values, *earlier))[0]
 
 
+def zero_of(values):
+    corner = values[(0,) * (values.ndim - 1)][:1]
+    return (corner != corner).astype(jnp.int32)[0]
+
+
 def gather_halves(first, second):
     first_1, second_2 = swap(first, "tp", 1), swap(second, "tp", 2)
     first_2, second_1 = swap(first, "tp", 2), swap(second, "tp", 1)
@@ -1060,17 +1088,14 @@
     return (left_side.astype(jnp.float32) + right_side.astype(jnp.float32)).astype(jnp.bfloat16)
 
 
-def reduce_halves(pieces):
-    first, second = pieces[0::2], pieces[1::2]
-    first_3, second_3 = swap(first[3], "tp", 1), swap(second[3], "tp", 2)
-    first_1, second_2 = swap(first[1], "tp", 1), swap(second[2], "tp", 2)
-    first_2 = swap(add_low(first[2], first_3), "tp", 2)
-    second_1 = swap(add_low(second[1], second_3), "tp", 1)
-    sums = [
+def reduce_halves(first, second, first_2, second_1, over_1, over_2):
+    over_1, over_2 = swap(over_1, "tp", 1), swap(over_2, "tp", 2)
+    first_2 = swap(add_low(first_2, over_1[1]), "tp", 2)
+    second_1 = swap(add_low(second_1, over_2[1]), "tp", 1)
+    return [
         sum(part.astype(jnp.float32) for part in parts)
-        for parts in ((first[0], first_1, first_2), (second[0], second_2, second_1))
+        for parts in ((first, over_1[0], first_2), (second, over_2[0], second_1))
     ]
-    return sums
 
 
 def exchange_parts(values, axis_name):
@@ -1135,15 +1160,20 @@
         ],
         axis=2,
     )
+    wide_parts = exchange_parts(wide_hidden, "ep")
+    half_start = dp_index * half + sum(zero_of(part) for part in wide_parts[1:])
     gate_part, up_part = [
-        jnp.transpose(take_part(weight, dp_index, half, 1), (1, 0, 2)).reshape(half, inner)
-        for weight in (after(w_gate, wide_hidden), after(w_up, wide_hidden))
+        jnp.transpose(
+            lax.dynamic_slice_in_dim(weight, half_start, half, 1), (1, 0, 2)
+        ).reshape(half, inner)
+        for weight in (w_gate, w_up)
     ]
-    down_part = take_part(after(w_down, wide_hidden).reshape(inner, model_width), dp_index, half, 0)
+    down_part = lax.dynamic_slice_in_dim(
+        w_down.reshape(inner, model_width), half_start, half, 0
+    )
     weights_here = jnp.stack([gate_part, up_part, down_part])
     own_weights = lax.all_gather(weights_here, "tp")
 
-    wide_parts = [after(part, weights_here) for part in exchange_parts(wide_hidden, "ep")]
     wide_mine = in_order(wide_parts, "ep").reshape(mine, -1)
     hidden_mine = wide_mine[:, :model_width]
     routes_mine = wide_mine[:, model_width:].astype(jnp.int32)
@@ -1155,13 +1185,15 @@
     first_mine = (normed_first * gain_first).astype(jnp.bfloat16)
     first_rows = gather_halves(first_mine[:, :half], first_mine[:, half:])
 
+    def own_grads(earlier):
+        start = tp_index * quarter + zero_of(earlier)
+        return lax.dynamic_slice_in_dim(cotangent, start, quarter, 1)
+
     grads_parts = [take_part(cotangent, tp_index, quarter, 1)]
-    sent = after(grads_parts[0], hidden_mine)
-    grads_parts.append(shift_by(sent, "ep", 1))
+    grads_parts.append(shift_by(own_grads(hidden_mine), "ep", 1))
     first_rows[7] = after(first_rows[7], grads_parts[1])
     for distance in range(3, ep_count, 2):
-        sent = after(sent, grads_parts[1])
-        grads_parts.append(shift_by(sent, "ep", distance))
+        grads_parts.append(shift_by(own_grads(grads_parts[-1]), "ep", distance))
 
     weights_t = jnp.concatenate([w_query, key_projection_weight, value_projection_weight], axis=1).T
     inverse = 1.0 / 10000.0 ** (jnp.arange(halfway, dtype=jnp.float32) * 2.0 / HEAD_SIZE)
@@ -1183,7 +1215,7 @@
     attn_t = after(attn_t, *grads_parts[2:])
     mixed = mix_heads(tp_me, attn_t, w_out, tp_count, quarter)
     for distance in range(2, ep_count, 2):
-        part = shift_by(after(sent, attn_t), "ep", distance)
+        part = shift_by(own_grads(attn_t), "ep", distance)
         grads_parts.insert(distance, after(part, mixed[0]))
     own_weights = after(own_weights, mixed[0])
     grads_all = in_order(grads_parts, "ep")
@@ -1194,7 +1226,7 @@
             for step in range(ep_count)
         ]
     ).reshape(ep_count, mine, model_width)
-    attn_out = jnp.concatenate(reduce_halves(mixed), axis=1)
+    attn_out = jnp.concatenate(reduce_halves(*mixed), axis=1)
     middle = hidden + attn_out
     gain_second = moe_gain.astype(jnp.float32)
     factor_second = inverse_rms(middle)
@@ -1268,18 +1300,16 @@
     def grads_half(number):
         return take_part(chunk_grads.reshape(ep_count * mine, model_width), number, half, 1)
 
-    def low_product(left_side, right_side):
-        return contract_rows(left_side, right_side).astype(jnp.bfloat16)
-
     def weight_products(number, *earlier):
-        tokens_part, grads_part = after(token_half(number), *earlier), grads_half(number)
+        tokens_part = after(token_half(number), *earlier)
+        grads_part = after(grads_half(number), *earlier)
         return [
-            low_product(tokens_part, grad_gate),
-            low_product(tokens_part, grad_up),
-            low_product(active, after(grads_part, *earlier)),
+            contract_rows(tokens_part, grad_gate),
+            contract_rows(tokens_part, grad_up),
+            contract_rows(active, grads_part),
         ]
 
-    far_sums = weight_products(1 - dp_index)
+    far_sums = [part.astype(jnp.bfloat16) for part in weight_products(1 - dp_index)]
     final = order[-1]
     grad_parts[final] = after(grad_parts[final], *far_sums)
     grad_sum = sum(grad_parts[step].astype(jnp.float32) for step in range(ep_count))
@@ -1301,7 +1331,10 @@
         scatter_dimension=0,
         tiled=True,
     ).reshape(seq_count, quarter, model_width)
-    near_sums = weight_products(dp_index, grad_low)
+    near_sums = [
+        (near + far.astype(jnp.float32)).astype(jnp.bfloat16)
+        for near, far in zip(weight_products(dp_index, grad_low), far_sums)
+    ]
     grad_attn[6:] = [after(piece, *near_sums) for piece in grad_attn[6:]]
     grad_vec_t, grad_vec, delta, grad_wo = unmix_heads(
         tp_me, grad_attn, w_out, attn_t, kv_width, quarter
@@ -1309,20 +1342,14 @@
     cut = inner // 2
 
     def sum_piece(offset, side):
-        place = tp_index ^ offset
-        pieces = []
-        for number, pair in enumerate(zip(near_sums, far_sums)):
-            pieces.append(
-                add_low(
-                    *(
-                        lax.dynamic_slice_in_dim(
-                            part, place * inner + side * cut, cut, 0 if number == 2 else 1
-                        )
-                        for part in pair
-                    )
-                )
-            )
-        return jnp.concatenate(pieces, axis=0)
+        place = (tp_index ^ offset) * inner + side * cut
+        return jnp.concatenate(
+            [
+                lax.dynamic_slice_in_dim(part, place, cut, 0 if number == 2 else 1)
+                for number, part in enumerate(near_sums)
+            ],
+            axis=0,
+        )
 
     first, second = [[sum_piece(offset, side) for offset in range(tp_count)] for side in range(2)]
     first_3, second_3 = swap(first[3], "tp", 1), swap(second[3], "tp", 2)
@@ -1346,7 +1373,7 @@
         after(part, grad_query_t) for part in (first_3, second_3, first_1, second_2)
     ]
     grad_query_t = after(grad_query_t, first_3, second_3, first_1, second_2)
-    grad_qkv_t, *first_parts = unproject(
+    grad_qkv_t, gain_part, *first_parts = unproject(
         tp_me, grad_query_t, grad_key, grad_value, cosine, sine, first_rows, weights_t, quarter
     )
     def dp_half(rows):
@@ -1358,13 +1385,28 @@
     def ep_part(rows):
         share = rows.shape[1] // ep_count
         return sum(
-            shift_by(take_part(rows, (ep_index + step) % ep_count, share, 1), "ep", step)
-            if step
-            else take_part(rows, ep_index, share, 1)
+            (
+                shift_by(take_part(rows, (ep_index + step) % ep_count, share, 1), "ep", step)
+                if step
+                else take_part(rows, ep_index, share, 1)
+            ).astype(jnp.float32)
             for step in range(ep_count)
         )
 
-    dense_half = dp_half(jnp.concatenate([grad_qkv_t, grad_wo], axis=0))
+    grad_router = contract_rows(after(second_in, grad_vec_t), grad_logits)
+    grad_moe_gain = jnp.sum(after(grad_second, grad_vec_t) * normed_second, axis=0)
+    small = jnp.concatenate(
+        [
+            grad_router.T,
+            grad_moe_gain[None, :],
+            gain_part[:1] / gain_first[None, :],
+            jnp.zeros((6, model_width), jnp.float32),
+        ],
+        axis=0,
+    )
+    small = small + swap(small, "tp", 1)
+    small = small + swap(small, "tp", 2)
+    dense_half = dp_half(jnp.concatenate([grad_qkv_t, grad_wo, small], axis=0))
     column = model_width // tp_count
     out_home = after(out_home, grad_qkv_t)
     out_pieces = [
@@ -1374,7 +1416,7 @@
         for offset in range(tp_count)
     ]
     grad_first = after(
-        jnp.concatenate(reduce_halves(first_parts), axis=1), dense_half, *out_pieces
+        jnp.concatenate(reduce_halves(*first_parts), axis=1), dense_half, *out_pieces
     )
     grad_mine = grad_middle + norm_back(grad_first, normed_first, factor_first, gain_first)
     first_2 = swap(after(add_low(first[2], first_3), grad_mine), "tp", 2)
@@ -1416,25 +1458,11 @@
 
     block_out = jnp.concatenate(by_quarter(jnp.stack(out_pieces)), axis=1).astype(jnp.float32)
 
-    grad_router = contract_rows(after(second_in, grad_vec_t), grad_logits)
-    grad_moe_gain = jnp.sum(after(grad_second, grad_vec_t) * normed_second, axis=0)
-    grad_attn_gain = jnp.sum(grad_first * normed_first, axis=0)
-    dense_home = ep_part(after(dense_half, home_pieces[2]))
-    qkv_home = dense_home[: query_width + 2 * kv_width].T
-    wo_home = dense_home[query_width + 2 * kv_width :]
-    small = jnp.concatenate(
-        [
-            grad_router.T,
-            grad_moe_gain[None, :],
-            grad_attn_gain[None, :],
-            jnp.zeros((6, model_width), jnp.float32),
-        ],
-        axis=0,
-    )
-    share = model_width // (2 * ep_count)
-    small_home = take_part(
-        after(lax.psum(small, ("dp", "ep", "tp")), home_pieces[6]), dp_index * ep_count + ep_index, share, 1
-    )
+    dense_home = ep_part(after(dense_half, home).astype(jnp.bfloat16))
+    kept_rows = query_width + 2 * kv_width
+    qkv_home = dense_home[:kept_rows].T
+    wo_home = dense_home[kept_rows : kept_rows + query_width]
+    small_home = dense_home[kept_rows + query_width :]
     return (
         block_out,
         grad_in,

time: 851 us -> 901 us (1.059)
  starting transfers between devices: 67.3 us -> 102 us
  local copies, waits for them, and re-layouts: 52.7 us -> 68.8 us
  other arithmetic: 81.5 us -> 72.1 us
    psum x1 -> x0, waiting for transfers between devices: 39 us -> none  [per_device_by_sequence(): lax.psum(small, ('dp', 'ep', 'tp'))]
    ppermute x18, starting transfers between devices: 24.5 us -> 63.4 us  [shift_by(): lax.ppermute(values, axis_name, [(source, (source + distance) % count) fo...]
    all_gather x1, waiting for transfers between devices: 1.13 us -> 29.6 us  [per_device_by_sequence(): own_weights = lax.all_gather(weights_here, 'tp')]
    convert_element_type x9 -> x6, other arithmetic: 24.7 us -> 9.51 us  [add_low(): (left_side.astype(jnp.float32) + right_side.astype(jnp.float32)).astype(j...]
    dynamic_slice x0 -> x7, local copies, waits for them, and re-layouts: none -> 14.7 us  [the longest x3 7.19 us: sum_piece(): lax.dynamic_slice_in_dim(part, place, cut, 0 if number == 2 else 1)]
    ppermute x18, waiting for transfers between devices: 115 us -> 127 us  [shift_by(): lax.ppermute(values, axis_name, [(source, (source + distance) % count) fo...]
    ppermute x44 -> x42, waiting for transfers between devices: 121 us -> 117 us  [swap(): lax.ppermute(values, axis_name, [(source, source ^ distance) for source i...]
    unnamed x176 -> x179, local copies, waits for them, and re-layouts: 16.5 us -> 20.8 us
  transfers between devices with their start and end apart: 65 -> 62, of which waited for: 30 -> 27; matrix products, arithmetic and copies ran while one was open for 22% -> 21% of each run, Pallas kernels for 31% -> 25%
where the time goes in v4:
time: 901 us; the launch traced here: 892 us
  waiting for transfers between devices  274 us (30%)
  Pallas kernels  264 us (29%)
  starting transfers between devices  102 us (11%)
  matrix products  86.9 us (10%)
  other arithmetic  72.1 us (8%)
  local copies, waits for them, and re-layouts  68.8 us (8%)
  between operations  23.8 us (3%)
    pallas_call x4, Pallas kernels, expert_chunk(): pl.pallas_call(expert_kernel, grid_spec=pltpu.PrefetchScalarGridSpec(num_...  157 us
    ppermute x18, waiting for transfers between devices, shift_by(): lax.ppermute(values, axis_name, [(source, (source + distance) % count) fo...  127 us
    ppermute x42, waiting for transfers between devices, swap(): lax.ppermute(values, axis_name, [(source, source ^ distance) for source i...  117 us
    dot_general x7, matrix products, contract_rows(): lax.dot_general(left_side, right_side, (((0,), (0,)), ((), ())), preferre...  85.8 us
    ppermute x18, starting transfers between devices, shift_by(): lax.ppermute(values, axis_name, [(source, (source + distance) % count) fo...  63.4 us
    pallas_call x1, Pallas kernels, attend_back(): pl.pallas_call(attend_back_kernel, grid_spec=pltpu.PrefetchScalarGridSpec...  43.8 us
    ppermute x42, starting transfers between devices, swap(): lax.ppermute(values, axis_name, [(source, source ^ distance) for source i...  38.8 us
    pallas_call x1, Pallas kernels, attend(): pl.pallas_call(attend_kernel, grid_spec=pltpu.PrefetchScalarGridSpec(num_...  31.6 us
  transfers between devices with their start and end apart: 62, of which 27 were waited for; matrix products, arithmetic and copies ran while one was open for 21% of the time, Pallas kernels for 25%

profile of v4, /device:TPU:0, one launch (start us, length us, event | category | flops | bytes accessed | tf_op | source)
XLA Modules:
  0.0 891.5 jit_solution(10918634308837068207)
XLA Ops:
  75.7 17.7 %collective-permute-done.6.refs_5_ = bf16[512,512]{1,0:T(8,128)(2,1)} collective-permute-done((bf16[512,512]{1,0:T(8,128)(2,1)}, bf16[512,512]{1,0:T(8,128)(2,1)}, u32[]{:S(2)}, u32[]{:S(2)}) %collective-permute-start.6) | collective-permute-done | bytes 524320 | tf_op jit(solution)/shard_map/ppermute | solution.py:1068
  110.0 29.9 %collective-permute-done.8.refs_7_ = bf16[512,512]{1,0:T(8,128)(2,1)} collective-permute-done((bf16[512,512]{1,0:T(8,128)(2,1)}, bf16[512,512]{1,0:T(8,128)(2,1)}, u32[]{:S(2)}, u32[]{:S(2)}) %collective-permute-start.8) | collective-permute-done | bytes 524320 | tf_op jit(solution)/shard_map/ppermute | solution.py:1068
  148.1 31.6 %attend.1 = (bf16[256,2048]{1,0:T(8,128)(2,1)}, f32[4,1,2048]{2,1,0:T(1,128)}) custom-call(s32[4]{0:T(128)} %get-tuple-element.344.low_ref, s32[4]{0:T(128)} %get-tuple-element.343.mid_ref, bf16[4,128,2048]{2,1,0:T(8,128)(2,1)} %get-tuple-element.96.q_ref.qt_ref, bf16[2048,128]{1,0:T(8,128)(2,1)} %get-tuple-element.97.k_ref, ...), custom_call_target="tpu_custom_call" | custom-call | flops 8589934592 | bytes 8388608 | tf_op jit(solution)/shard_map/attend/pallas_call | solution.py:484
  185.7 29.6 %all-gather.3.cloned.1.call-done = bf16[12,512,1024]{2,1,0:T(8,128)(2,1)} async-done(((bf16[3,512,1024]{2,1,0:T(8,128)(2,1)}), bf16[12,512,1024]{2,1,0:T(8,128)(2,1)}) %all-gather.3.cloned.1.call-update) | async-done | bytes 12582928 | tf_op jit(solution)/shard_map/all_gather | solution.py:1175
  229.2 40.5 %collective-permute-done.15 = bf16[4,128,1024]{2,1,0:T(8,128)(2,1)} collective-permute-done((bf16[4,128,1024]{2,1,0:T(8,128)(2,1)}, bf16[4,128,1024]{2,1,0:T(8,128)(2,1)}, u32[]{:S(2)}, u32[]{:S(2)}) %collective-permute-start.15) | collective-permute-done | bytes 1048608 | tf_op jit(solution)/shard_map/ppermute | solution.py:437
  296.2 39.6 %expert_chunk.4 = (bf16[512,1152]{1,0:T(8,128)(2,1)}, bf16[4,4,128,1024]{3,2,1,0:T(8,128)(2,1)}, bf16[4,512,4096]{2,1,0:T(8,128)(2,1)}, bf16[4,512,4096]{2,1,0:T(8,128)(2,1)}, bf16[4,512,4096]{2,1,0:T(8,128)(2,1)}) custom-call(s32[2]{0:T(128)} %pad_add_fusion.1.me_ref, bf16[512,1152]{1,0:T(8,128)(2,1)} %copy-done.15, ...), custom_call_target="tpu_custom_call" | custom-call | flops 25769803776 | bytes 37748736 | tf_op jit(solution)/shard_map/expert_chunk/pallas_call | solution.py:722
  335.7 10.5 %collective-permute-done.19.x_ref = bf16[512,1152]{1,0:T(8,128)(2,1)} collective-permute-done((bf16[512,1152]{1,0:T(8,128)(2,1)S(1)}, bf16[512,1152]{1,0:T(8,128)(2,1)}, u32[]{:S(2)}, u32[]{:S(2)}) %collective-permute-start.19) | collective-permute-done | bytes 1179680 | tf_op jit(solution)/shard_map/ppermute | solution.py:437
  346.2 39.5 %expert_chunk.5 = (bf16[512,1152]{1,0:T(8,128)(2,1)}, bf16[4,4,128,1024]{3,2,1,0:T(8,128)(2,1)}, bf16[4,512,4096]{2,1,0:T(8,128)(2,1)}, bf16[4,512,4096]{2,1,0:T(8,128)(2,1)}, bf16[4,512,4096]{2,1,0:T(8,128)(2,1)}) custom-call(s32[2]{0:T(128)} %get-tuple-element.346.me_ref, ...), custom_call_target="tpu_custom_call", output_to_operand_aliasing={{1}: (7, {}), {2}: (8, {}), {3}: (9, {}), {4}: (10, {})} | custom-call | flops 25769803776 | bytes 37748736 | tf_op jit(solution)/shard_map/expert_chunk/pallas_call | solution.py:722
  388.3 39.0 %expert_chunk.6 = (bf16[512,1152]{1,0:T(8,128)(2,1)}, bf16[4,4,128,1024]{3,2,1,0:T(8,128)(2,1)}, bf16[4,512,4096]{2,1,0:T(8,128)(2,1)}, bf16[4,512,4096]{2,1,0:T(8,128)(2,1)}, bf16[4,512,4096]{2,1,0:T(8,128)(2,1)}) custom-call(s32[2]{0:T(128)} %pad_add_fusion.3.me_ref, ...), custom_call_target="tpu_custom_call", output_to_operand_aliasing={{1}: (7, {}), {2}: (8, {}), {3}: (9, {}), {4}: (10, {})} | custom-call | flops 25769803776 | bytes 37748736 | tf_op jit(solution)/shard_map/expert_chunk/pallas_call | solution.py:722
  430.4 34.2 %collective-permute-done.17.x_ref = bf16[512,1152]{1,0:T(8,128)(2,1)S(1)} collective-permute-done((bf16[512,1152]{1,0:T(8,128)(2,1)S(1)}, bf16[512,1152]{1,0:T(8,128)(2,1)S(1)}, u32[]{:S(2)}, u32[]{:S(2)}) %collective-permute-start.17) | collective-permute-done | bytes 1179680 | tf_op jit(solution)/shard_map/ppermute | solution.py:437
  465.9 39.0 %expert_chunk.7 = (bf16[512,1152]{1,0:T(8,128)(2,1)}, bf16[4,4,128,1024]{3,2,1,0:T(8,128)(2,1)}, bf16[4,512,4096]{2,1,0:T(8,128)(2,1)}, bf16[4,512,4096]{2,1,0:T(8,128)(2,1)}, bf16[4,512,4096]{2,1,0:T(8,128)(2,1)}) custom-call(s32[2]{0:T(128)} %get-tuple-element.345.me_ref, ...), custom_call_target="tpu_custom_call", output_to_operand_aliasing={{1}: (7, {}), {2}: (8, {}), {3}: (9, {}), {4}: (10, {})} | custom-call | flops 25769803776 | bytes 37748736 | tf_op jit(solution)/shard_map/expert_chunk/pallas_call | solution.py:722
  505.0 14.0 %convolution_convert_fusion = bf16[512,4096]{1,0:T(8,128)(2,1)} fusion(bf16[2048,512]{1,0:T(8,128)(2,1)S(1)} %pad_maximum_fusion.6, bf16[2048,4096]{1,0:T(8,128)(2,1)} %bitcast.240), kind=kOutput, calls=%fused_computation.4 | convolution fusion | flops 8592031744 | bytes 23068672 | tf_op jit(solution)/shard_map/dot_general | solution.py:22
  519.0 10.9 %convolution_convert_fusion.2 = bf16[4096,512]{1,0:T(8,128)(2,1)} fusion(bf16[2048,4096]{1,0:T(8,128)(2,1)S(1)} %bitcast.237, bf16[2048,512]{1,0:T(8,128)(2,1)S(1)} %copy-done.25), kind=kOutput, calls=%fused_computation.6 | convolution fusion | flops 8592031744 | bytes 23068672 | tf_op jit(solution)/shard_map/dot_general | solution.py:22
  529.9 14.0 %convolution_convert_fusion.1 = bf16[512,4096]{1,0:T(8,128)(2,1)} fusion(bf16[2048,512]{1,0:T(8,128)(2,1)S(1)} %pad_maximum_fusion.6, bf16[2048,4096]{1,0:T(8,128)(2,1)} %bitcast.238), kind=kOutput, calls=%fused_computation.5 | convolution fusion | flops 8592031744 | bytes 23068672 | tf_op jit(solution)/shard_map/dot_general | solution.py:22
  545.9 13.3 %collective-permute-done.21 = bf16[512,1152]{1,0:T(8,128)(2,1)S(1)} collective-permute-done((bf16[512,1152]{1,0:T(8,128)(2,1)}, bf16[512,1152]{1,0:T(8,128)(2,1)S(1)}, u32[]{:S(2)}, u32[]{:S(2)}) %collective-permute-start.21) | collective-permute-done | bytes 1179680 | tf_op jit(solution)/shard_map/ppermute | solution.py:437
  567.8 17.4 %add_convert_fusion.1 = bf16[512,4096]{1,0:T(8,128)(2,1)} fusion(bf16[512,4096]{1,0:T(8,128)(2,1)} %collective-permute-done.29, bf16[2048,512]{1,0:T(8,128)(2,1)} %pad_maximum_fusion.7, bf16[2048,4096]{1,0:T(8,128)(2,1)} %bitcast.241), kind=kOutput, calls=%fused_computation.2 | convolution fusion | flops 8596226048 | bytes 27262976 | tf_op jit(solution)/shard_map/dot_general | solution.py:22
  591.9 14.5 %add_convert_fusion = bf16[4096,512]{1,0:T(8,128)(2,1)} fusion(bf16[4096,512]{1,0:T(8,128)(2,1)} %collective-permute-done.30, bf16[2048,4096]{1,0:T(8,128)(2,1)} %bitcast.236, bf16[2048,512]{1,0:T(8,128)(2,1)S(1)} %copy-done.24), kind=kOutput, calls=%fused_computation.1 | convolution fusion | flops 8596226048 | bytes 27262976 | tf_op jit(solution)/shard_map/dot_general | solution.py:22
  606.4 14.7 %add_convert_fusion.2 = bf16[512,4096]{1,0:T(8,128)(2,1)} fusion(bf16[512,4096]{1,0:T(8,128)(2,1)} %collective-permute-done.28, bf16[2048,512]{1,0:T(8,128)(2,1)S(1)} %copy-done.27, bf16[2048,4096]{1,0:T(8,128)(2,1)} %bitcast.239), kind=kOutput, calls=%fused_computation.3 | convolution fusion | flops 8596226048 | bytes 27262976 | tf_op jit(solution)/shard_map/dot_general | solution.py:22
  648.2 43.8 %attend_back.1 = (f32[256,2048]{1,0:T(8,128)}, f32[2048,128]{1,0:T(8,128)}, f32[2048,128]{1,0:T(8,128)}) custom-call(s32[4]{0:T(128)} %get-tuple-element.344.low_ref, s32[4]{0:T(128)} %get-tuple-element.343.mid_ref, bf16[4,128,2048]{2,1,0:T(8,128)(2,1)} %get-tuple-element.96.q_ref.qt_ref, bf16[4,2048,128]{2,1,0:T(8,128)(2,1)} %get-tuple-element.142.q_ref, ...), custom_call_target="tpu_custom_call" | custom-call | flops 21474836480 | bytes 16777216 | tf_op jit(solution)/shard_map/attend_back/pallas_call | solution.py:596
  692.0 15.1 %collective-permute-done.34 = bf16[1536,512]{1,0:T(8,128)(2,1)} collective-permute-done((bf16[1536,512]{1,0:T(8,128)(2,1)}, bf16[1536,512]{1,0:T(8,128)(2,1)}, u32[]{:S(2)}, u32[]{:S(2)}) %collective-permute-start.34) | collective-permute-done | bytes 1572896 | tf_op jit(solution)/shard_map/ppermute | solution.py:1068
  709.7 10.3 %unproject.1 = (f32[512,1024]{1,0:T(8,128)}, f32[8,1024]{1,0:T(8,128)}, bf16[512,512]{1,0:T(8,128)(2,1)}, bf16[512,512]{1,0:T(8,128)(2,1)}, bf16[512,512]{1,0:T(...) custom-call(s32[1]{0:T(128)} %bitcast.9.me_ref, ...), custom_call_target="tpu_custom_call" | custom-call | flops 4294967296 | bytes 12582912 | tf_op jit(solution)/shard_map/unproject/pallas_call | solution.py:1034
  734.3 13.7 %collective-permute-done.44 = f32[40,1024]{1,0:T(8,128)S(1)} collective-permute-done((f32[40,1024]{1,0:T(8,128)S(1)}, f32[40,1024]{1,0:T(8,128)S(1)}, u32[]{:S(2)}, u32[]{:S(2)}) %collective-permute-start.44) | collective-permute-done | bytes 163872 | tf_op jit(solution)/shard_map/ppermute | solution.py:1068
  788.3 17.3 %collective-permute-start.46 = (bf16[128,1024]{1,0:T(8,128)(2,1)S(1)}, bf16[128,1024]{1,0:T(8,128)(2,1)S(1)}, u32[]{:S(2)}, u32[]{:S(2)}) collective-permute-start(bf16[128,1024]{1,0:T(8,128)(2,1)S(1)} %get-tuple-element.317), channel_id=1, source_target_pairs={{0,4},{4,8},{8,12},{12,0},{1,5},{5,9},{9,13},{13,1},{2,6},{6,10},{... | collective-permute-start | bytes 786440 | tf_op jit(solution)/shard_map/ppermute | solution.py:437
  831.1 16.1 %collective-permute-start.57 = (bf16[808,128]{1,0:T(8,128)(2,1)S(1)}, bf16[808,128]{1,0:T(8,128)(2,1)S(1)}, u32[]{:S(2)}, u32[]{:S(2)}) collective-permute-start(bf16[808,128]{1,0:T(8,128)(2,1)S(1)} %get-tuple-element.330), channel_id=1, source_target_pairs={{0,4},{4,8},{8,12},{12,0},{1,5},{5,9},{9,13},{13,1},{2,6},{6,10},{... | collective-permute-start | bytes 620552 | tf_op jit(solution)/shard_map/ppermute | solution.py:437
  (437 shorter events, 301.7 us)
Async XLA Ops:
  7.2 208.1 %all-gather.3.cloned.1.call-start = ((), (), s32[]{:S(2)}) async-start(), calls=%async_computation.2 | async-start | bytes 15728640 | tf_op jit(solution)/shard_map/all_gather | solution.py:1175
  57.6 709.1 %reduce-scatter.2.cloned.1.call-start = ((), (), s32[]{:S(2)}) async-start(), calls=%async_computation.1 | async-start | bytes 5242880 | tf_op jit(solution)/shard_map/reduce_scatter | solution.py:1328
  74.7 65.3 %collective-permute-start.4 = (bf16[512,512]{1,0:T(8,128)(2,1)}, bf16[512,512]{1,0:T(8,128)(2,1)}, u32[]{:S(2)}, u32[]{:S(2)}) collective-permute-start(bf16[512,512]{1,0:T(8,128)(2,1)} %get-tuple-element.328.refs_1_), channel_id=1, source_target_pairs={{0,1},{1,0},{2,3},{3,2},{4,5},{5,4},{6,7},{7,6},{8,9},{9,8},{10,11... | collective-permute-start | bytes 1572872 | tf_op jit(solution)/shard_map/ppermute | solution.py:1068
  75.2 64.7 %collective-permute-start.5 = (bf16[512,512]{1,0:T(8,128)(2,1)}, bf16[512,512]{1,0:T(8,128)(2,1)}, u32[]{:S(2)}, u32[]{:S(2)}) collective-permute-start(bf16[512,512]{1,0:T(8,128)(2,1)} %get-tuple-element.329.refs_0_), channel_id=1, source_target_pairs={{0,2},{1,3},{2,0},{3,1},{4,6},{5,7},{6,4},{7,5},{8,10},{9,11},{10,... | collective-permute-start | bytes 1572872 | tf_op jit(solution)/shard_map/ppermute | solution.py:1068
  93.4 46.6 %collective-permute-start.8 = (bf16[512,512]{1,0:T(8,128)(2,1)}, bf16[512,512]{1,0:T(8,128)(2,1)}, u32[]{:S(2)}, u32[]{:S(2)}) collective-permute-start(bf16[512,512]{1,0:T(8,128)(2,1)} %collective-permute-done.6.refs_5_), channel_id=1, source_target_pairs={{0,1},{1,0},{2,3},{3,2},{4,5},{5,4},{6,7},{7,6},{8,9},{9,8},{10,11... | collective-permute-start | bytes 1572872 | tf_op jit(solution)/shard_map/ppermute | solution.py:1068
  106.6 73.1 %collective-permute-start.10 = (bf16[4,128,1024]{2,1,0:T(8,128)(2,1)S(1)}, bf16[4,128,1024]{2,1,0:T(8,128)(2,1)S(1)}, u32[]{:S(2)}, u32[]{:S(2)}) collective-permute-start(bf16[4,128,1024]{2,1,0:T(8,128)(2,1)S(1)} %get-tuple-element.275), channel_id=1, source_target_pairs={{0,12},{4,0},{8,4},{12,8},{1,13},{5,1},{9,5},{13,9},{2,14},{6,2},{... | collective-permute-start | bytes 3145736 | tf_op jit(solution)/shard_map/ppermute | solution.py:437
  215.3 80.8 %collective-permute-start.16 = (bf16[4,3,512,1024]{3,2,1,0:T(8,128)(2,1)}, bf16[4,3,512,1024]{3,2,1,0:T(8,128)(2,1)}, u32[]{:S(2)}, u32[]{:S(2)}) collective-permute-start(bf16[4,3,512,1024]{3,2,1,0:T(8,128)(2,1)} %bitcast.231), channel_id=1, source_target_pairs={{0,16},{16,0},{1,17},{17,1},{2,18},{18,2},{3,19},{19,3},{4,20},{20... | collective-permute-start | bytes 37748744 | tf_op jit(solution)/shard_map/ppermute | solution.py:1068
  220.4 49.3 %collective-permute-start.15 = (bf16[4,128,1024]{2,1,0:T(8,128)(2,1)}, bf16[4,128,1024]{2,1,0:T(8,128)(2,1)}, u32[]{:S(2)}, u32[]{:S(2)}) collective-permute-start(bf16[4,128,1024]{2,1,0:T(8,128)(2,1)} %constant_dynamic-slice_fusion.58), channel_id=1, source_target_pairs={{0,8},{4,12},{8,0},{12,4},{1,9},{5,13},{9,1},{13,5},{2,10},{6,14},... | collective-permute-start | bytes 3145736 | tf_op jit(solution)/shard_map/ppermute | solution.py:437
  222.8 46.8 %collective-permute-start.11 = (bf16[2,512,512]{2,1,0:T(8,128)(2,1)}, bf16[2,512,512]{2,1,0:T(8,128)(2,1)}, u32[]{:S(2)}, u32[]{:S(2)}) collective-permute-start(bf16[2,512,512]{2,1,0:T(8,128)(2,1)} %get-tuple-element.103), channel_id=1, source_target_pairs={{0,1},{1,0},{2,3},{3,2},{4,5},{5,4},{6,7},{7,6},{8,9},{9,8},{10,11... | collective-permute-start | bytes 3145736 | tf_op jit(solution)/shard_map/ppermute | solution.py:1068
  226.1 46.4 %collective-permute-start.13 = (bf16[2,512,512]{2,1,0:T(8,128)(2,1)}, bf16[2,512,512]{2,1,0:T(8,128)(2,1)}, u32[]{:S(2)}, u32[]{:S(2)}) collective-permute-start(bf16[2,512,512]{2,1,0:T(8,128)(2,1)} %get-tuple-element.106), channel_id=1, source_target_pairs={{0,2},{1,3},{2,0},{3,1},{4,6},{5,7},{6,4},{7,5},{8,10},{9,11},{10,... | collective-permute-start | bytes 3145736 | tf_op jit(solution)/shard_map/ppermute | solution.py:1068
  295.8 50.4 %collective-permute-start.19 = (bf16[512,1152]{1,0:T(8,128)(2,1)S(1)}, bf16[512,1152]{1,0:T(8,128)(2,1)}, u32[]{:S(2)}, u32[]{:S(2)}) collective-permute-start(bf16[512,1152]{1,0:T(8,128)(2,1)S(1)} %concatenate.76.x_ref), channel_id=1, source_target_pairs={{0,4},{4,8},{8,12},{12,0},{1,5},{5,9},{9,13},{13,1},{2,6},{6,10},{... | collective-permute-start | bytes 3538952 | tf_op jit(solution)/shard_map/ppermute | solution.py:437
  385.7 158.2 %collective-permute-start.20 = (bf16[512,1152]{1,0:T(8,128)(2,1)}, bf16[512,1152]{1,0:T(8,128)(2,1)}, u32[]{:S(2)}, u32[]{:S(2)}) collective-permute-start(bf16[512,1152]{1,0:T(8,128)(2,1)} %get-tuple-element.118), channel_id=1, source_target_pairs={{0,4},{4,8},{8,12},{12,0},{1,5},{5,9},{9,13},{13,1},{2,6},{6,10},{... | collective-permute-start | bytes 3538952 | tf_op jit(solution)/shard_map/ppermute | solution.py:437
  387.4 77.1 %collective-permute-start.17 = (bf16[512,1152]{1,0:T(8,128)(2,1)S(1)}, bf16[512,1152]{1,0:T(8,128)(2,1)S(1)}, u32[]{:S(2)}, u32[]{:S(2)}) collective-permute-start(bf16[512,1152]{1,0:T(8,128)(2,1)S(1)} %copy-done.16), channel_id=1, source_target_pairs={{0,8},{4,12},{8,0},{12,4},{1,9},{5,13},{9,1},{13,5},{2,10},{6,14},... | collective-permute-start | bytes 3538952 | tf_op jit(solution)/shard_map/ppermute | solution.py:437
  427.4 116.5 %collective-permute-start.22 = (bf16[512,1152]{1,0:T(8,128)(2,1)}, bf16[512,1152]{1,0:T(8,128)(2,1)}, u32[]{:S(2)}, u32[]{:S(2)}) collective-permute-start(bf16[512,1152]{1,0:T(8,128)(2,1)} %get-tuple-element.126), channel_id=1, source_target_pairs={{0,12},{4,0},{8,4},{12,8},{1,13},{5,1},{9,5},{13,9},{2,14},{6,2},{... | collective-permute-start | bytes 3538952 | tf_op jit(solution)/shard_map/ppermute | solution.py:437
  505.0 54.3 %collective-permute-start.21 = (bf16[512,1152]{1,0:T(8,128)(2,1)}, bf16[512,1152]{1,0:T(8,128)(2,1)S(1)}, u32[]{:S(2)}, u32[]{:S(2)}) collective-permute-start(bf16[512,1152]{1,0:T(8,128)(2,1)} %get-tuple-element.134), channel_id=1, source_target_pairs={{0,8},{4,12},{8,0},{12,4},{1,9},{5,13},{9,1},{13,5},{2,10},{6,14},... | collective-permute-start | bytes 3538952 | tf_op jit(solution)/shard_map/ppermute | solution.py:437
  519.0 48.1 %collective-permute-start.29 = (bf16[512,4096]{1,0:T(8,128)(2,1)}, bf16[512,4096]{1,0:T(8,128)(2,1)}, u32[]{:S(2)}, u32[]{:S(2)}) collective-permute-start(bf16[512,4096]{1,0:T(8,128)(2,1)} %convolution_convert_fusion), channel_id=1, source_target_pairs={{0,16},{16,0},{1,17},{17,1},{2,18},{18,2},{3,19},{19,3},{4,20},{20... | collective-permute-start | bytes 12582920 | tf_op jit(solution)/shard_map/ppermute | solution.py:1068
  543.9 47.3 %collective-permute-start.30 = (bf16[4096,512]{1,0:T(8,128)(2,1)}, bf16[4096,512]{1,0:T(8,128)(2,1)}, u32[]{:S(2)}, u32[]{:S(2)}) collective-permute-start(bf16[4096,512]{1,0:T(8,128)(2,1)} %convolution_convert_fusion.2), channel_id=1, source_target_pairs={{0,16},{16,0},{1,17},{17,1},{2,18},{18,2},{3,19},{19,3},{4,20},{20... | collective-permute-start | bytes 12582920 | tf_op jit(solution)/shard_map/ppermute | solution.py:1068
  544.4 62.0 %collective-permute-start.28 = (bf16[512,4096]{1,0:T(8,128)(2,1)}, bf16[512,4096]{1,0:T(8,128)(2,1)}, u32[]{:S(2)}, u32[]{:S(2)}) collective-permute-start(bf16[512,4096]{1,0:T(8,128)(2,1)} %convolution_convert_fusion.1), channel_id=1, source_target_pairs={{0,16},{16,0},{1,17},{17,1},{2,18},{18,2},{3,19},{19,3},{4,20},{20... | collective-permute-start | bytes 12582920 | tf_op jit(solution)/shard_map/ppermute | solution.py:1068
  565.7 55.5 %collective-permute-start.24 = (bf16[512,512]{1,0:T(8,128)(2,1)}, bf16[512,512]{1,0:T(8,128)(2,1)}, u32[]{:S(2)}, u32[]{:S(2)}) collective-permute-start(bf16[512,512]{1,0:T(8,128)(2,1)} %get-tuple-element.326.refs_1_), channel_id=1, source_target_pairs={{0,1},{1,0},{2,3},{3,2},{4,5},{5,4},{6,7},{7,6},{8,9},{9,8},{10,11... | collective-permute-start | bytes 1572872 | tf_op jit(solution)/shard_map/ppermute | solution.py:1068
  639.4 52.6 %collective-permute-start.32 = (bf16[1536,512]{1,0:T(8,128)(2,1)S(1)}, bf16[1536,512]{1,0:T(8,128)(2,1)}, u32[]{:S(2)}, u32[]{:S(2)}) collective-permute-start(bf16[1536,512]{1,0:T(8,128)(2,1)S(1)} %pad_maximum_fusion.12), channel_id=1, source_target_pairs={{0,1},{1,0},{2,3},{3,2},{4,5},{5,4},{6,7},{7,6},{8,9},{9,8},{10,11... | collective-permute-start | bytes 4718600 | tf_op jit(solution)/shard_map/ppermute | solution.py:1068
  642.2 49.8 %collective-permute-start.35 = (bf16[1536,512]{1,0:T(8,128)(2,1)}, bf16[1536,512]{1,0:T(8,128)(2,1)}, u32[]{:S(2)}, u32[]{:S(2)}) collective-permute-start(bf16[1536,512]{1,0:T(8,128)(2,1)} %pad_maximum_fusion.15), channel_id=1, source_target_pairs={{0,2},{1,3},{2,0},{3,1},{4,6},{5,7},{6,4},{7,5},{8,10},{9,11},{10,... | collective-permute-start | bytes 4718600 | tf_op jit(solution)/shard_map/ppermute | solution.py:1068
  644.1 63.0 %collective-permute-start.34 = (bf16[1536,512]{1,0:T(8,128)(2,1)}, bf16[1536,512]{1,0:T(8,128)(2,1)}, u32[]{:S(2)}, u32[]{:S(2)}) collective-permute-start(bf16[1536,512]{1,0:T(8,128)(2,1)} %pad_maximum_fusion.14), channel_id=1, source_target_pairs={{0,1},{1,0},{2,3},{3,2},{4,5},{5,4},{6,7},{7,6},{8,9},{9,8},{10,11... | collective-permute-start | bytes 4718600 | tf_op jit(solution)/shard_map/ppermute | solution.py:1068
  646.8 62.9 %collective-permute-start.33 = (bf16[1536,512]{1,0:T(8,128)(2,1)}, bf16[1536,512]{1,0:T(8,128)(2,1)}, u32[]{:S(2)}, u32[]{:S(2)}) collective-permute-start(bf16[1536,512]{1,0:T(8,128)(2,1)} %pad_maximum_fusion.13), channel_id=1, source_target_pairs={{0,2},{1,3},{2,0},{3,1},{4,6},{5,7},{6,4},{7,5},{8,10},{9,11},{10,... | collective-permute-start | bytes 4718600 | tf_op jit(solution)/shard_map/ppermute | solution.py:1068
  821.7 48.4 %collective-permute-start.52 = (bf16[4,128,512]{2,1,0:T(8,128)(2,1)}, bf16[4,128,512]{2,1,0:T(8,128)(2,1)}, u32[]{:S(2)}, u32[]{:S(2)}) collective-permute-start(bf16[4,128,512]{2,1,0:T(8,128)(2,1)} %get-tuple-element.309), channel_id=1, source_target_pairs={{0,2},{1,3},{2,0},{3,1},{4,6},{5,7},{6,4},{7,5},{8,10},{9,11},{10,... | collective-permute-start | bytes 1572872 | tf_op jit(solution)/shard_map/ppermute | solution.py:1068
  (123 other events, 1880.8 us)
Sparse Core Ops, SparseCore 0:
  57.7 157.5 all-gather.2
  567.2 86.5 reduce-scatter.1

commit v5 on v4

--- a/solution.py
+++ b/solution.py
@@ -1160,20 +1160,15 @@
         ],
         axis=2,
     )
-    wide_parts = exchange_parts(wide_hidden, "ep")
-    half_start = dp_index * half + sum(zero_of(part) for part in wide_parts[1:])
     gate_part, up_part = [
-        jnp.transpose(
-            lax.dynamic_slice_in_dim(weight, half_start, half, 1), (1, 0, 2)
-        ).reshape(half, inner)
-        for weight in (w_gate, w_up)
+        jnp.transpose(take_part(weight, dp_index, half, 1), (1, 0, 2)).reshape(half, inner)
+        for weight in (after(w_gate, wide_hidden), after(w_up, wide_hidden))
     ]
-    down_part = lax.dynamic_slice_in_dim(
-        w_down.reshape(inner, model_width), half_start, half, 0
-    )
+    down_part = take_part(after(w_down, wide_hidden).reshape(inner, model_width), dp_index, half, 0)
     weights_here = jnp.stack([gate_part, up_part, down_part])
     own_weights = lax.all_gather(weights_here, "tp")
 
+    wide_parts = [after(part, weights_here) for part in exchange_parts(wide_hidden, "ep")]
     wide_mine = in_order(wide_parts, "ep").reshape(mine, -1)
     hidden_mine = wide_mine[:, :model_width]
     routes_mine = wide_mine[:, model_width:].astype(jnp.int32)
@@ -1283,6 +1278,8 @@
             None if step else middle,
         )
         last = grad_part
+        if turn_number == 1 and turns > 3:
+            chunk_tokens[order[2]] = after(chunk_tokens[order[2]], chunk_tokens[order[3]])
         for n in order[turn_number + 1 : turn_number + 3]:
             if n in chunk_tokens:
                 chunk_tokens[n] = after(chunk_tokens[n], last)
@@ -1404,8 +1401,7 @@
         ],
         axis=0,
     )
-    small = small + swap(small, "tp", 1)
-    small = small + swap(small, "tp", 2)
+    small = small + sum(swap(small, "tp", offset) for offset in range(1, tp_count))
     dense_half = dp_half(jnp.concatenate([grad_qkv_t, grad_wo, small], axis=0))
     column = model_width // tp_count
     out_home = after(out_home, grad_qkv_t)

time: 901 us -> 839 us (0.931)
  waiting for transfers between devices: 274 us -> 239 us
  starting transfers between devices: 102 us -> 79 us
    ppermute x18, starting transfers between devices: 63.4 us -> 36.7 us  [shift_by(): lax.ppermute(values, axis_name, [(source, (source + distance) % count) fo...]
    all_gather x1, waiting for transfers between devices: 29.6 us -> 6.37 us  [per_device_by_sequence(): own_weights = lax.all_gather(weights_here, 'tp')]
    ppermute x42 -> x43, waiting for transfers between devices: 117 us -> 108 us  [swap(): lax.ppermute(values, axis_name, [(source, source ^ distance) for source i...]
    ppermute x42 -> x43, starting transfers between devices: 38.8 us -> 42.2 us  [swap(): lax.ppermute(values, axis_name, [(source, source ^ distance) for source i...]
    unnamed x179 -> x157, local copies, waits for them, and re-layouts: 20.8 us -> 18.3 us
  transfers between devices with their start and end apart: 62 -> 63, of which waited for: 27 -> 30; matrix products, arithmetic and copies ran while one was open for 21% -> 23% of each run, Pallas kernels for 25% -> 32%
where the time goes in v5:
time: 839 us; the launch traced here: 830 us
  Pallas kernels  264 us (31%)
  waiting for transfers between devices  239 us (28%)
  matrix products  87.9 us (10%)
  starting transfers between devices  79 us (9%)
  local copies, waits for them, and re-layouts  72 us (9%)
  other arithmetic  69.3 us (8%)
  between operations  19.7 us (2%)
    pallas_call x4, Pallas kernels, expert_chunk(): pl.pallas_call(expert_kernel, grid_spec=pltpu.PrefetchScalarGridSpec(num_...  157 us
    ppermute x18, waiting for transfers between devices, shift_by(): lax.ppermute(values, axis_name, [(source, (source + distance) % count) fo...  124 us
    ppermute x43, waiting for transfers between devices, swap(): lax.ppermute(values, axis_name, [(source, source ^ distance) for source i...  108 us
    dot_general x7, matrix products, contract_rows(): lax.dot_general(left_side, right_side, (((0,), (0,)), ((), ())), preferre...  86.8 us
    pallas_call x1, Pallas kernels, attend_back(): pl.pallas_call(attend_back_kernel, grid_spec=pltpu.PrefetchScalarGridSpec...  43.8 us
    ppermute x43, starting transfers between devices, swap(): lax.ppermute(values, axis_name, [(source, source ^ distance) for source i...  42.2 us
    ppermute x18, starting transfers between devices, shift_by(): lax.ppermute(values, axis_name, [(source, (source + distance) % count) fo...  36.7 us
    pallas_call x1, Pallas kernels, attend(): pl.pallas_call(attend_kernel, grid_spec=pltpu.PrefetchScalarGridSpec(num_...  31.5 us
  transfers between devices with their start and end apart: 63, of which 30 were waited for; matrix products, arithmetic and copies ran while one was open for 23% of the time, Pallas kernels for 32%

profile of v5, /device:TPU:0, one launch (start us, length us, event | category | flops | bytes accessed | tf_op | source)
XLA Modules:
  0.0 830.5 jit_solution(14695609129262841661)
XLA Ops:
  43.9 11.8 %collective-permute-done.1 = bf16[128,1032]{1,0:T(8,128)(2,1)S(1)} collective-permute-done((bf16[128,1032]{1,0:T(8,128)(2,1)S(1)}, bf16[128,1032]{1,0:T(8,128)(2,1)S(1)}, u32[]{:S(2)}, u32[]{:S(2)}) %collective-permute-start.1) | collective-permute-done | bytes 264224 | tf_op jit(solution)/shard_map/ppermute | solution.py:437
  74.0 16.3 %collective-permute-done.6.refs_5_ = bf16[512,512]{1,0:T(8,128)(2,1)} collective-permute-done((bf16[512,512]{1,0:T(8,128)(2,1)}, bf16[512,512]{1,0:T(8,128)(2,1)}, u32[]{:S(2)}, u32[]{:S(2)}) %collective-permute-start.6) | collective-permute-done | bytes 524320 | tf_op jit(solution)/shard_map/ppermute | solution.py:1068
  107.2 20.2 %collective-permute-done.8.refs_7_ = bf16[512,512]{1,0:T(8,128)(2,1)} collective-permute-done((bf16[512,512]{1,0:T(8,128)(2,1)}, bf16[512,512]{1,0:T(8,128)(2,1)}, u32[]{:S(2)}, u32[]{:S(2)}) %collective-permute-start.8) | collective-permute-done | bytes 524320 | tf_op jit(solution)/shard_map/ppermute | solution.py:1068
  128.2 8.0 project.1
  136.2 31.5 %attend.1 = (bf16[256,2048]{1,0:T(8,128)(2,1)}, f32[4,1,2048]{2,1,0:T(1,128)}) custom-call(s32[4]{0:T(128)} %get-tuple-element.360.low_ref, s32[4]{0:T(128)} %get-tuple-element.359.mid_ref, bf16[4,128,2048]{2,1,0:T(8,128)(2,1)} %get-tuple-element.111.q_ref.qt_ref, bf16[2048,128]{1,0:T(8,128)(2,1)} %get-tuple-element.112.k_ref, ...), custom_call_target="tpu_custom_call" | custom-call | flops 8589934592 | bytes 8388608 | tf_op jit(solution)/shard_map/attend/pallas_call | solution.py:484
  194.2 40.3 %collective-permute-done.15 = bf16[4,128,1024]{2,1,0:T(8,128)(2,1)} collective-permute-done((bf16[4,128,1024]{2,1,0:T(8,128)(2,1)}, bf16[4,128,1024]{2,1,0:T(8,128)(2,1)}, u32[]{:S(2)}, u32[]{:S(2)}) %collective-permute-start.15) | collective-permute-done | bytes 1048608 | tf_op jit(solution)/shard_map/ppermute | solution.py:437
  261.1 39.6 %expert_chunk.4 = (bf16[512,1152]{1,0:T(8,128)(2,1)}, bf16[4,4,128,1024]{3,2,1,0:T(8,128)(2,1)}, bf16[4,512,4096]{2,1,0:T(8,128)(2,1)}, bf16[4,512,4096]{2,1,0:T(8,128)(2,1)}, bf16[4,512,4096]{2,1,0:T(8,128)(2,1)}) custom-call(s32[2]{0:T(128)} %pad_add_fusion.1.me_ref, bf16[512,1152]{1,0:T(8,128)(2,1)} %copy-done.16, ...), custom_call_target="tpu_custom_call" | custom-call | flops 25769803776 | bytes 37748736 | tf_op jit(solution)/shard_map/expert_chunk/pallas_call | solution.py:722
  301.0 8.7 %collective-permute-done.18.x_ref = bf16[512,1152]{1,0:T(8,128)(2,1)S(1)} collective-permute-done((bf16[512,1152]{1,0:T(8,128)(2,1)S(1)}, bf16[512,1152]{1,0:T(8,128)(2,1)S(1)}, u32[]{:S(2)}, u32[]{:S(2)}) %collective-permute-start.18) | collective-permute-done | bytes 1179680 | tf_op jit(solution)/shard_map/ppermute | solution.py:437
  310.9 39.4 %expert_chunk.5 = (bf16[512,1152]{1,0:T(8,128)(2,1)}, bf16[4,4,128,1024]{3,2,1,0:T(8,128)(2,1)}, bf16[4,512,4096]{2,1,0:T(8,128)(2,1)}, bf16[4,512,4096]{2,1,0:T(8,128)(2,1)}, bf16[4,512,4096]{2,1,0:T(8,128)(2,1)}) custom-call(s32[2]{0:T(128)} %get-tuple-element.362.me_ref, ...), custom_call_target="tpu_custom_call", output_to_operand_aliasing={{1}: (7, {}), {2}: (8, {}), {3}: (9, {}), {4}: (10, {})} | custom-call | flops 25769803776 | bytes 37748736 | tf_op jit(solution)/shard_map/expert_chunk/pallas_call | solution.py:722
  355.3 31.4 %collective-permute-done.17.x_ref = bf16[512,1152]{1,0:T(8,128)(2,1)S(1)} collective-permute-done((bf16[512,1152]{1,0:T(8,128)(2,1)}, bf16[512,1152]{1,0:T(8,128)(2,1)S(1)}, u32[]{:S(2)}, u32[]{:S(2)}) %collective-permute-start.17) | collective-permute-done | bytes 1179680 | tf_op jit(solution)/shard_map/ppermute | solution.py:437
  388.5 39.0 %expert_chunk.6 = (bf16[512,1152]{1,0:T(8,128)(2,1)}, bf16[4,4,128,1024]{3,2,1,0:T(8,128)(2,1)}, bf16[4,512,4096]{2,1,0:T(8,128)(2,1)}, bf16[4,512,4096]{2,1,0:T(8,128)(2,1)}, bf16[4,512,4096]{2,1,0:T(8,128)(2,1)}) custom-call(s32[2]{0:T(128)} %pad_add_fusion.3.me_ref, ...), custom_call_target="tpu_custom_call", output_to_operand_aliasing={{1}: (7, {}), {2}: (8, {}), {3}: (9, {}), {4}: (10, {})} | custom-call | flops 25769803776 | bytes 37748736 | tf_op jit(solution)/shard_map/expert_chunk/pallas_call | solution.py:722
  428.5 39.1 %expert_chunk.7 = (bf16[512,1152]{1,0:T(8,128)(2,1)}, bf16[4,4,128,1024]{3,2,1,0:T(8,128)(2,1)}, bf16[4,512,4096]{2,1,0:T(8,128)(2,1)}, bf16[4,512,4096]{2,1,0:T(8,128)(2,1)}, bf16[4,512,4096]{2,1,0:T(8,128)(2,1)}) custom-call(s32[2]{0:T(128)} %get-tuple-element.361.me_ref, ...), custom_call_target="tpu_custom_call", output_to_operand_aliasing={{1}: (7, {}), {2}: (8, {}), {3}: (9, {}), {4}: (10, {})} | custom-call | flops 25769803776 | bytes 37748736 | tf_op jit(solution)/shard_map/expert_chunk/pallas_call | solution.py:722
  467.7 14.1 %convolution_convert_fusion = bf16[512,4096]{1,0:T(8,128)(2,1)} fusion(bf16[2048,512]{1,0:T(8,128)(2,1)S(1)} %pad_maximum_fusion.7, bf16[2048,4096]{1,0:T(8,128)(2,1)} %bitcast.243), kind=kOutput, calls=%fused_computation.4 | convolution fusion | flops 8592031744 | bytes 23068672 | tf_op jit(solution)/shard_map/dot_general | solution.py:22
  481.9 10.9 %convolution_convert_fusion.2 = bf16[4096,512]{1,0:T(8,128)(2,1)} fusion(bf16[2048,4096]{1,0:T(8,128)(2,1)S(1)} %bitcast.240, bf16[2048,512]{1,0:T(8,128)(2,1)S(1)} %copy-done.25), kind=kOutput, calls=%fused_computation.6 | convolution fusion | flops 8592031744 | bytes 23068672 | tf_op jit(solution)/shard_map/dot_general | solution.py:22
  492.8 14.0 %convolution_convert_fusion.1 = bf16[512,4096]{1,0:T(8,128)(2,1)} fusion(bf16[2048,512]{1,0:T(8,128)(2,1)S(1)} %pad_maximum_fusion.7, bf16[2048,4096]{1,0:T(8,128)(2,1)} %bitcast.241), kind=kOutput, calls=%fused_computation.5 | convolution fusion | flops 8592031744 | bytes 23068672 | tf_op jit(solution)/shard_map/dot_general | solution.py:22
  508.8 13.3 %collective-permute-done.21 = bf16[512,1152]{1,0:T(8,128)(2,1)S(1)} collective-permute-done((bf16[512,1152]{1,0:T(8,128)(2,1)}, bf16[512,1152]{1,0:T(8,128)(2,1)S(1)}, u32[]{:S(2)}, u32[]{:S(2)}) %collective-permute-start.21) | collective-permute-done | bytes 1179680 | tf_op jit(solution)/shard_map/ppermute | solution.py:437
  531.1 18.3 %add_convert_fusion.1 = bf16[512,4096]{1,0:T(8,128)(2,1)} fusion(bf16[512,4096]{1,0:T(8,128)(2,1)} %collective-permute-done.29, bf16[2048,512]{1,0:T(8,128)(2,1)} %pad_maximum_fusion.8, bf16[2048,4096]{1,0:T(8,128)(2,1)} %bitcast.244), kind=kOutput, calls=%fused_computation.2 | convolution fusion | flops 8596226048 | bytes 27262976 | tf_op jit(solution)/shard_map/dot_general | solution.py:22
  555.4 14.4 %add_convert_fusion = bf16[4096,512]{1,0:T(8,128)(2,1)} fusion(bf16[4096,512]{1,0:T(8,128)(2,1)} %collective-permute-done.30, bf16[2048,4096]{1,0:T(8,128)(2,1)} %bitcast.239, bf16[2048,512]{1,0:T(8,128)(2,1)S(1)} %copy-done.24), kind=kOutput, calls=%fused_computation.1 | convolution fusion | flops 8596226048 | bytes 27262976 | tf_op jit(solution)/shard_map/dot_general | solution.py:22
  569.8 14.8 %add_convert_fusion.2 = bf16[512,4096]{1,0:T(8,128)(2,1)} fusion(bf16[512,4096]{1,0:T(8,128)(2,1)} %collective-permute-done.28, bf16[2048,512]{1,0:T(8,128)(2,1)S(1)} %copy-done.27, bf16[2048,4096]{1,0:T(8,128)(2,1)} %bitcast.242), kind=kOutput, calls=%fused_computation.3 | convolution fusion | flops 8596226048 | bytes 27262976 | tf_op jit(solution)/shard_map/dot_general | solution.py:22
  612.0 43.8 %attend_back.1 = (f32[256,2048]{1,0:T(8,128)}, f32[2048,128]{1,0:T(8,128)}, f32[2048,128]{1,0:T(8,128)}) custom-call(s32[4]{0:T(128)} %get-tuple-element.360.low_ref, s32[4]{0:T(128)} %get-tuple-element.359.mid_ref, bf16[4,128,2048]{2,1,0:T(8,128)(2,1)} %get-tuple-element.111.q_ref.qt_ref, bf16[4,2048,128]{2,1,0:T(8,128)(2,1)} %get-tuple-element.158.q_ref, ...), custom_call_target="tpu_custom_call" | custom-call | flops 21474836480 | bytes 16777216 | tf_op jit(solution)/shard_map/attend_back/pallas_call | solution.py:596
  655.8 15.7 %collective-permute-done.34 = bf16[1536,512]{1,0:T(8,128)(2,1)} collective-permute-done((bf16[1536,512]{1,0:T(8,128)(2,1)}, bf16[1536,512]{1,0:T(8,128)(2,1)}, u32[]{:S(2)}, u32[]{:S(2)}) %collective-permute-start.34) | collective-permute-done | bytes 1572896 | tf_op jit(solution)/shard_map/ppermute | solution.py:1068
  673.5 10.3 %unproject.1 = (f32[512,1024]{1,0:T(8,128)}, f32[8,1024]{1,0:T(8,128)}, bf16[512,512]{1,0:T(8,128)(2,1)}, bf16[512,512]{1,0:T(8,128)(2,1)}, bf16[512,512]{1,0:T(...) custom-call(s32[1]{0:T(128)} %bitcast.17.me_ref, ...), custom_call_target="tpu_custom_call" | custom-call | flops 4294967296 | bytes 12582912 | tf_op jit(solution)/shard_map/unproject/pallas_call | solution.py:1034
  697.6 16.1 %collective-permute-done.39 = bf16[2,512,512]{2,1,0:T(8,128)(2,1)S(1)} collective-permute-done((bf16[2,512,512]{2,1,0:T(8,128)(2,1)}, bf16[2,512,512]{2,1,0:T(8,128)(2,1)S(1)}, u32[]{:S(2)}, u32[]{:S(2)}) %collective-permute-start.39) | collective-permute-done | bytes 1048608 | tf_op jit(solution)/shard_map/ppermute | solution.py:1068
  764.8 11.0 %collective-permute-done.50 = bf16[1536,512]{1,0:T(8,128)(2,1)} collective-permute-done((bf16[1536,512]{1,0:T(8,128)(2,1)}, bf16[1536,512]{1,0:T(8,128)(2,1)}, u32[]{:S(2)}, u32[]{:S(2)}) %collective-permute-start.50) | collective-permute-done | bytes 1572896 | tf_op jit(solution)/shard_map/ppermute | solution.py:1068
  (415 shorter events, 288.8 us)
Async XLA Ops:
  7.2 172.9 %all-gather.3.cloned.1.call-start = ((), (), s32[]{:S(2)}) async-start(), calls=%async_computation.2 | async-start | bytes 15728640 | tf_op jit(solution)/shard_map/all_gather | solution.py:1169
  28.7 699.1 %reduce-scatter.2.cloned.1.call-start = ((), (), s32[]{:S(2)}) async-start(), calls=%async_computation.1 | async-start | bytes 5242880 | tf_op jit(solution)/shard_map/reduce_scatter | solution.py:1325
  59.6 38.1 %collective-permute-start.9 = (bf16[4,128,1024]{2,1,0:T(8,128)(2,1)S(1)}, bf16[4,128,1024]{2,1,0:T(8,128)(2,1)}, u32[]{:S(2)}, u32[]{:S(2)}) collective-permute-start(bf16[4,128,1024]{2,1,0:T(8,128)(2,1)S(1)} %constant_dynamic-slice_fusion.57), channel_id=1, source_target_pairs={{0,4},{4,8},{8,12},{12,0},{1,5},{5,9},{9,13},{13,1},{2,6},{6,10},{... | collective-permute-start | bytes 3145736 | tf_op jit(solution)/shard_map/ppermute | solution.py:437
  73.0 54.4 %collective-permute-start.4 = (bf16[512,512]{1,0:T(8,128)(2,1)}, bf16[512,512]{1,0:T(8,128)(2,1)}, u32[]{:S(2)}, u32[]{:S(2)}) collective-permute-start(bf16[512,512]{1,0:T(8,128)(2,1)} %get-tuple-element.344.refs_1_), channel_id=1, source_target_pairs={{0,1},{1,0},{2,3},{3,2},{4,5},{5,4},{6,7},{7,6},{8,9},{9,8},{10,11... | collective-permute-start | bytes 1572872 | tf_op jit(solution)/shard_map/ppermute | solution.py:1068
  73.5 53.8 %collective-permute-start.5 = (bf16[512,512]{1,0:T(8,128)(2,1)}, bf16[512,512]{1,0:T(8,128)(2,1)}, u32[]{:S(2)}, u32[]{:S(2)}) collective-permute-start(bf16[512,512]{1,0:T(8,128)(2,1)} %get-tuple-element.345.refs_0_), channel_id=1, source_target_pairs={{0,2},{1,3},{2,0},{3,1},{4,6},{5,7},{6,4},{7,5},{8,10},{9,11},{10,... | collective-permute-start | bytes 1572872 | tf_op jit(solution)/shard_map/ppermute | solution.py:1068
  102.2 65.5 %collective-permute-start.10 = (bf16[4,128,1024]{2,1,0:T(8,128)(2,1)S(1)}, bf16[4,128,1024]{2,1,0:T(8,128)(2,1)S(1)}, u32[]{:S(2)}, u32[]{:S(2)}) collective-permute-start(bf16[4,128,1024]{2,1,0:T(8,128)(2,1)S(1)} %get-tuple-element.291), channel_id=1, source_target_pairs={{0,12},{4,0},{8,4},{12,8},{1,13},{5,1},{9,5},{13,9},{2,14},{6,2},{... | collective-permute-start | bytes 3145736 | tf_op jit(solution)/shard_map/ppermute | solution.py:437
  180.1 80.9 %collective-permute-start.16 = (bf16[4,3,512,1024]{3,2,1,0:T(8,128)(2,1)}, bf16[4,3,512,1024]{3,2,1,0:T(8,128)(2,1)}, u32[]{:S(2)}, u32[]{:S(2)}) collective-permute-start(bf16[4,3,512,1024]{3,2,1,0:T(8,128)(2,1)} %bitcast.234), channel_id=1, source_target_pairs={{0,16},{16,0},{1,17},{17,1},{2,18},{18,2},{3,19},{19,3},{4,20},{20... | collective-permute-start | bytes 37748744 | tf_op jit(solution)/shard_map/ppermute | solution.py:1068
  185.3 49.2 %collective-permute-start.15 = (bf16[4,128,1024]{2,1,0:T(8,128)(2,1)}, bf16[4,128,1024]{2,1,0:T(8,128)(2,1)}, u32[]{:S(2)}, u32[]{:S(2)}) collective-permute-start(bf16[4,128,1024]{2,1,0:T(8,128)(2,1)} %constant_dynamic-slice_fusion.55), channel_id=1, source_target_pairs={{0,8},{4,12},{8,0},{12,4},{1,9},{5,13},{9,1},{13,5},{2,10},{6,14},... | collective-permute-start | bytes 3145736 | tf_op jit(solution)/shard_map/ppermute | solution.py:437
  187.7 46.8 %collective-permute-start.11 = (bf16[2,512,512]{2,1,0:T(8,128)(2,1)}, bf16[2,512,512]{2,1,0:T(8,128)(2,1)}, u32[]{:S(2)}, u32[]{:S(2)}) collective-permute-start(bf16[2,512,512]{2,1,0:T(8,128)(2,1)} %get-tuple-element.118), channel_id=1, source_target_pairs={{0,1},{1,0},{2,3},{3,2},{4,5},{5,4},{6,7},{7,6},{8,9},{9,8},{10,11... | collective-permute-start | bytes 3145736 | tf_op jit(solution)/shard_map/ppermute | solution.py:1068
  191.1 45.8 %collective-permute-start.13 = (bf16[2,512,512]{2,1,0:T(8,128)(2,1)}, bf16[2,512,512]{2,1,0:T(8,128)(2,1)}, u32[]{:S(2)}, u32[]{:S(2)}) collective-permute-start(bf16[2,512,512]{2,1,0:T(8,128)(2,1)} %get-tuple-element.121), channel_id=1, source_target_pairs={{0,2},{1,3},{2,0},{3,1},{4,6},{5,7},{6,4},{7,5},{8,10},{9,11},{10,... | collective-permute-start | bytes 3145736 | tf_op jit(solution)/shard_map/ppermute | solution.py:1068
  256.8 93.4 %collective-permute-start.19 = (bf16[512,1152]{1,0:T(8,128)(2,1)S(1)}, bf16[512,1152]{1,0:T(8,128)(2,1)}, u32[]{:S(2)}, u32[]{:S(2)}) collective-permute-start(bf16[512,1152]{1,0:T(8,128)(2,1)S(1)} %concatenate.76.x_ref), channel_id=1, source_target_pairs={{0,4},{4,8},{8,12},{12,0},{1,5},{5,9},{9,13},{13,1},{2,6},{6,10},{... | collective-permute-start | bytes 3538952 | tf_op jit(solution)/shard_map/ppermute | solution.py:437
  257.8 52.0 %collective-permute-start.18 = (bf16[512,1152]{1,0:T(8,128)(2,1)S(1)}, bf16[512,1152]{1,0:T(8,128)(2,1)S(1)}, u32[]{:S(2)}, u32[]{:S(2)}) collective-permute-start(bf16[512,1152]{1,0:T(8,128)(2,1)S(1)} %concatenate.76.x_ref), channel_id=1, source_target_pairs={{0,12},{4,0},{8,4},{12,8},{1,13},{5,1},{9,5},{13,9},{2,14},{6,2},{... | collective-permute-start | bytes 3538952 | tf_op jit(solution)/shard_map/ppermute | solution.py:437
  300.6 86.1 %collective-permute-start.17 = (bf16[512,1152]{1,0:T(8,128)(2,1)}, bf16[512,1152]{1,0:T(8,128)(2,1)S(1)}, u32[]{:S(2)}, u32[]{:S(2)}) collective-permute-start(bf16[512,1152]{1,0:T(8,128)(2,1)} %copy-done.16), channel_id=1, source_target_pairs={{0,8},{4,12},{8,0},{12,4},{1,9},{5,13},{9,1},{13,5},{2,10},{6,14},... | collective-permute-start | bytes 3538952 | tf_op jit(solution)/shard_map/ppermute | solution.py:437
  350.3 156.6 %collective-permute-start.20 = (bf16[512,1152]{1,0:T(8,128)(2,1)}, bf16[512,1152]{1,0:T(8,128)(2,1)}, u32[]{:S(2)}, u32[]{:S(2)}) collective-permute-start(bf16[512,1152]{1,0:T(8,128)(2,1)} %get-tuple-element.133), channel_id=1, source_target_pairs={{0,4},{4,8},{8,12},{12,0},{1,5},{5,9},{9,13},{13,1},{2,6},{6,10},{... | collective-permute-start | bytes 3538952 | tf_op jit(solution)/shard_map/ppermute | solution.py:437
  427.5 94.6 %collective-permute-start.22 = (bf16[512,1152]{1,0:T(8,128)(2,1)}, bf16[512,1152]{1,0:T(8,128)(2,1)}, u32[]{:S(2)}, u32[]{:S(2)}) collective-permute-start(bf16[512,1152]{1,0:T(8,128)(2,1)} %get-tuple-element.142), channel_id=1, source_target_pairs={{0,12},{4,0},{8,4},{12,8},{1,13},{5,1},{9,5},{13,9},{2,14},{6,2},{... | collective-permute-start | bytes 3538952 | tf_op jit(solution)/shard_map/ppermute | solution.py:437
  467.7 54.4 %collective-permute-start.21 = (bf16[512,1152]{1,0:T(8,128)(2,1)}, bf16[512,1152]{1,0:T(8,128)(2,1)S(1)}, u32[]{:S(2)}, u32[]{:S(2)}) collective-permute-start(bf16[512,1152]{1,0:T(8,128)(2,1)} %get-tuple-element.150), channel_id=1, source_target_pairs={{0,8},{4,12},{8,0},{12,4},{1,9},{5,13},{9,1},{13,5},{2,10},{6,14},... | collective-permute-start | bytes 3538952 | tf_op jit(solution)/shard_map/ppermute | solution.py:437
  481.8 48.7 %collective-permute-start.29 = (bf16[512,4096]{1,0:T(8,128)(2,1)}, bf16[512,4096]{1,0:T(8,128)(2,1)}, u32[]{:S(2)}, u32[]{:S(2)}) collective-permute-start(bf16[512,4096]{1,0:T(8,128)(2,1)} %convolution_convert_fusion), channel_id=1, source_target_pairs={{0,16},{16,0},{1,17},{17,1},{2,18},{18,2},{3,19},{19,3},{4,20},{20... | collective-permute-start | bytes 12582920 | tf_op jit(solution)/shard_map/ppermute | solution.py:1068
  506.8 47.9 %collective-permute-start.30 = (bf16[4096,512]{1,0:T(8,128)(2,1)}, bf16[4096,512]{1,0:T(8,128)(2,1)}, u32[]{:S(2)}, u32[]{:S(2)}) collective-permute-start(bf16[4096,512]{1,0:T(8,128)(2,1)} %convolution_convert_fusion.2), channel_id=1, source_target_pairs={{0,16},{16,0},{1,17},{17,1},{2,18},{18,2},{3,19},{19,3},{4,20},{20... | collective-permute-start | bytes 12582920 | tf_op jit(solution)/shard_map/ppermute | solution.py:1068
  507.2 62.6 %collective-permute-start.28 = (bf16[512,4096]{1,0:T(8,128)(2,1)}, bf16[512,4096]{1,0:T(8,128)(2,1)}, u32[]{:S(2)}, u32[]{:S(2)}) collective-permute-start(bf16[512,4096]{1,0:T(8,128)(2,1)} %convolution_convert_fusion.1), channel_id=1, source_target_pairs={{0,16},{16,0},{1,17},{17,1},{2,18},{18,2},{3,19},{19,3},{4,20},{20... | collective-permute-start | bytes 12582920 | tf_op jit(solution)/shard_map/ppermute | solution.py:1068
  529.0 55.7 %collective-permute-start.24 = (bf16[512,512]{1,0:T(8,128)(2,1)}, bf16[512,512]{1,0:T(8,128)(2,1)}, u32[]{:S(2)}, u32[]{:S(2)}) collective-permute-start(bf16[512,512]{1,0:T(8,128)(2,1)} %get-tuple-element.342.refs_1_), channel_id=1, source_target_pairs={{0,1},{1,0},{2,3},{3,2},{4,5},{5,4},{6,7},{7,6},{8,9},{9,8},{10,11... | collective-permute-start | bytes 1572872 | tf_op jit(solution)/shard_map/ppermute | solution.py:1068
  603.3 52.5 %collective-permute-start.32 = (bf16[1536,512]{1,0:T(8,128)(2,1)}, bf16[1536,512]{1,0:T(8,128)(2,1)}, u32[]{:S(2)}, u32[]{:S(2)}) collective-permute-start(bf16[1536,512]{1,0:T(8,128)(2,1)} %pad_maximum_fusion.13), channel_id=1, source_target_pairs={{0,1},{1,0},{2,3},{3,2},{4,5},{5,4},{6,7},{7,6},{8,9},{9,8},{10,11... | collective-permute-start | bytes 4718600 | tf_op jit(solution)/shard_map/ppermute | solution.py:1068
  605.6 50.2 %collective-permute-start.35 = (bf16[1536,512]{1,0:T(8,128)(2,1)}, bf16[1536,512]{1,0:T(8,128)(2,1)}, u32[]{:S(2)}, u32[]{:S(2)}) collective-permute-start(bf16[1536,512]{1,0:T(8,128)(2,1)} %pad_maximum_fusion.16), channel_id=1, source_target_pairs={{0,2},{1,3},{2,0},{3,1},{4,6},{5,7},{6,4},{7,5},{8,10},{9,11},{10,... | collective-permute-start | bytes 4718600 | tf_op jit(solution)/shard_map/ppermute | solution.py:1068
  607.8 63.7 %collective-permute-start.34 = (bf16[1536,512]{1,0:T(8,128)(2,1)}, bf16[1536,512]{1,0:T(8,128)(2,1)}, u32[]{:S(2)}, u32[]{:S(2)}) collective-permute-start(bf16[1536,512]{1,0:T(8,128)(2,1)} %pad_maximum_fusion.15), channel_id=1, source_target_pairs={{0,1},{1,0},{2,3},{3,2},{4,5},{5,4},{6,7},{7,6},{8,9},{9,8},{10,11... | collective-permute-start | bytes 4718600 | tf_op jit(solution)/shard_map/ppermute | solution.py:1068
  610.7 62.9 %collective-permute-start.33 = (bf16[1536,512]{1,0:T(8,128)(2,1)}, bf16[1536,512]{1,0:T(8,128)(2,1)}, u32[]{:S(2)}, u32[]{:S(2)}) collective-permute-start(bf16[1536,512]{1,0:T(8,128)(2,1)} %pad_maximum_fusion.14), channel_id=1, source_target_pairs={{0,2},{1,3},{2,0},{3,1},{4,6},{5,7},{6,4},{7,5},{8,10},{9,11},{10,... | collective-permute-start | bytes 4718600 | tf_op jit(solution)/shard_map/ppermute | solution.py:1068
  (114 other events, 1675.8 us)
Sparse Core Ops, SparseCore 0:
  28.8 151.2 all-gather.2
  530.6 74.1 reduce-scatter.1

commit v6 on v5

--- a/solution.py
+++ b/solution.py
@@ -1187,7 +1187,7 @@
     grads_parts = [take_part(cotangent, tp_index, quarter, 1)]
     grads_parts.append(shift_by(own_grads(hidden_mine), "ep", 1))
     first_rows[7] = after(first_rows[7], grads_parts[1])
-    for distance in range(3, ep_count, 2):
+    for distance in range(2, ep_count, 2):
         grads_parts.append(shift_by(own_grads(grads_parts[-1]), "ep", distance))
 
     weights_t = jnp.concatenate([w_query, key_projection_weight, value_projection_weight], axis=1).T
@@ -1209,10 +1209,18 @@
     grads_parts[2:] = [after(part, attn_t) for part in grads_parts[2:]]
     attn_t = after(attn_t, *grads_parts[2:])
     mixed = mix_heads(tp_me, attn_t, w_out, tp_count, quarter)
-    for distance in range(2, ep_count, 2):
-        part = shift_by(own_grads(attn_t), "ep", distance)
-        grads_parts.insert(distance, after(part, mixed[0]))
+    late_parts = [
+        shift_by(own_grads(attn_t), "ep", distance) for distance in range(3, ep_count, 2)
+    ]
     own_weights = after(own_weights, mixed[0])
+    attn_out = jnp.concatenate(reduce_halves(*mixed), axis=1)
+    middle = hidden + attn_out
+    gain_second = moe_gain.astype(jnp.float32)
+    factor_second = inverse_rms(middle)
+    normed_second = middle * factor_second
+    second_in = (normed_second * gain_second).astype(jnp.bfloat16)
+    for distance, part in zip(range(3, ep_count, 2), late_parts):
+        grads_parts.insert(distance, after(part, second_in))
     grads_all = in_order(grads_parts, "ep")
     other_weights = swap(own_weights, "dp", 1)
     chunk_grads = jnp.stack(
@@ -1221,12 +1229,6 @@
             for step in range(ep_count)
         ]
     ).reshape(ep_count, mine, model_width)
-    attn_out = jnp.concatenate(reduce_halves(*mixed), axis=1)
-    middle = hidden + attn_out
-    gain_second = moe_gain.astype(jnp.float32)
-    factor_second = inverse_rms(middle)
-    normed_second = middle * factor_second
-    second_in = (normed_second * gain_second).astype(jnp.bfloat16)
     logits = matrix_multiply(second_in, w_router)
     chosen = (
         routes_mine[:, :, None] == jnp.arange(expert_count, dtype=jnp.int32)[None, None, :]
@@ -1256,7 +1258,7 @@
     order = [0, *range(1, ep_count, 2), *range(2, ep_count, 2)]
     turns = len(order)
     chunk_tokens, grad_parts = {0: tokens}, {}
-    kept, last = None, tokens
+    kept, last, early = None, tokens, {}
     for turn_number, step in enumerate(order):
         incoming = []
         if turn_number == 0:
@@ -1264,7 +1266,14 @@
         elif turn_number == 1:
             incoming = [n for n in order if n and n % 2 == 0]
         for n in incoming:
-            chunk_tokens[n] = shift_by(after(tokens, last), "ep", -n)
+            sent = after(tokens, last)
+            if turn_number:
+                arrived = [
+                    shift_by(part, "ep", -n) for part in (sent[: mine // 2], sent[mine // 2 :])
+                ]
+                early[n] = arrived
+            else:
+                chunk_tokens[n] = shift_by(sent, "ep", -n)
         grad_part, *kept = expert_chunk(
             step,
             jnp.stack([dp_index, (ep_index + step) % ep_count]),
@@ -1279,7 +1288,12 @@
         )
         last = grad_part
         if turn_number == 1 and turns > 3:
-            chunk_tokens[order[2]] = after(chunk_tokens[order[2]], chunk_tokens[order[3]])
+            chunk_tokens[order[2]] = after(
+                chunk_tokens[order[2]], *(arrived[0] for arrived in early.values())
+            )
+        if turn_number == 2 or turns < 4:
+            for n, arrived in early.items():
+                chunk_tokens[n] = jnp.concatenate([arrived[0], after(arrived[1], last)], axis=0)
         for n in order[turn_number + 1 : turn_number + 3]:
             if n in chunk_tokens:
                 chunk_tokens[n] = after(chunk_tokens[n], last)
@@ -1306,7 +1320,7 @@
             contract_rows(active, grads_part),
         ]
 
-    far_sums = [part.astype(jnp.bfloat16) for part in weight_products(1 - dp_index)]
+    far_sums = [part.astype(jnp.bfloat16) for part in weight_products(1 - dp_index, grad_parts[order[-2]])]
     final = order[-1]
     grad_parts[final] = after(grad_parts[final], *far_sums)
     grad_sum = sum(grad_parts[step].astype(jnp.float32) for step in range(ep_count))

time: 839 us -> 817 us (0.974)
  waiting for transfers between devices: 239 us -> 180 us
  starting transfers between devices: 79 us -> 115 us
    ppermute x18 -> x19, waiting for transfers between devices: 124 us -> 55.6 us  [shift_by(): lax.ppermute(values, axis_name, [(source, (source + distance) % count) fo...]
    ppermute x18 -> x19, starting transfers between devices: 36.7 us -> 75.4 us  [shift_by(): lax.ppermute(values, axis_name, [(source, (source + distance) % count) fo...]
    ppermute x43, waiting for transfers between devices: 108 us -> 118 us  [swap(): lax.ppermute(values, axis_name, [(source, source ^ distance) for source i...]
    unnamed x157 -> x167, local copies, waits for them, and re-layouts: 18.3 us -> 18.2 us
  transfers between devices with their start and end apart: 63 -> 64, of which waited for: 30 -> 28; matrix products, arithmetic and copies ran while one was open for 23% -> 23% of each run, Pallas kernels for 32% -> 33%
where the time goes in v6:
time: 817 us; the launch traced here: 812 us
  Pallas kernels  267 us (33%)
  waiting for transfers between devices  180 us (22%)
  starting transfers between devices  115 us (14%)
  matrix products  87 us (11%)
  local copies, waits for them, and re-layouts  72.8 us (9%)
  other arithmetic  70.8 us (9%)
  between operations  19.6 us (2%)
    pallas_call x4, Pallas kernels, expert_chunk(): pl.pallas_call(expert_kernel, grid_spec=pltpu.PrefetchScalarGridSpec(num_...  160 us
    ppermute x43, waiting for transfers between devices, swap(): lax.ppermute(values, axis_name, [(source, source ^ distance) for source i...  118 us
    dot_general x7, matrix products, contract_rows(): lax.dot_general(left_side, right_side, (((0,), (0,)), ((), ())), preferre...  85.9 us
    ppermute x19, starting transfers between devices, shift_by(): lax.ppermute(values, axis_name, [(source, (source + distance) % count) fo...  75.4 us
    ppermute x19, waiting for transfers between devices, shift_by(): lax.ppermute(values, axis_name, [(source, (source + distance) % count) fo...  55.6 us
    pallas_call x1, Pallas kernels, attend_back(): pl.pallas_call(attend_back_kernel, grid_spec=pltpu.PrefetchScalarGridSpec...  44.1 us
    ppermute x43, starting transfers between devices, swap(): lax.ppermute(values, axis_name, [(source, source ^ distance) for source i...  39.1 us
    pallas_call x1, Pallas kernels, attend(): pl.pallas_call(attend_kernel, grid_spec=pltpu.PrefetchScalarGridSpec(num_...  31.5 us
  transfers between devices with their start and end apart: 64, of which 28 were waited for; matrix products, arithmetic and copies ran while one was open for 23% of the time, Pallas kernels for 33%

profile of v6, /device:TPU:0, one launch (start us, length us, event | category | flops | bytes accessed | tf_op | source)
XLA Modules:
  0.0 812.0 jit_solution(9566612233137511381)
XLA Ops:
  43.9 11.8 %collective-permute-done.1 = bf16[128,1032]{1,0:T(8,128)(2,1)S(1)} collective-permute-done((bf16[128,1032]{1,0:T(8,128)(2,1)S(1)}, bf16[128,1032]{1,0:T(8,128)(2,1)S(1)}, u32[]{:S(2)}, u32[]{:S(2)}) %collective-permute-start.1) | collective-permute-done | bytes 264224 | tf_op jit(solution)/shard_map/ppermute | solution.py:437
  74.2 16.1 %collective-permute-done.6.refs_5_ = bf16[512,512]{1,0:T(8,128)(2,1)} collective-permute-done((bf16[512,512]{1,0:T(8,128)(2,1)}, bf16[512,512]{1,0:T(8,128)(2,1)}, u32[]{:S(2)}, u32[]{:S(2)}) %collective-permute-start.6) | collective-permute-done | bytes 524320 | tf_op jit(solution)/shard_map/ppermute | solution.py:1068
  106.8 20.7 %collective-permute-done.8.refs_7_ = bf16[512,512]{1,0:T(8,128)(2,1)} collective-permute-done((bf16[512,512]{1,0:T(8,128)(2,1)}, bf16[512,512]{1,0:T(8,128)(2,1)}, u32[]{:S(2)}, u32[]{:S(2)}) %collective-permute-start.8) | collective-permute-done | bytes 524320 | tf_op jit(solution)/shard_map/ppermute | solution.py:1068
  128.4 8.0 project.1
  136.3 31.5 %attend.1 = (bf16[256,2048]{1,0:T(8,128)(2,1)}, f32[4,1,2048]{2,1,0:T(1,128)}) custom-call(s32[4]{0:T(128)} %get-tuple-element.366.low_ref, s32[4]{0:T(128)} %get-tuple-element.365.mid_ref, bf16[4,128,2048]{2,1,0:T(8,128)(2,1)} %get-tuple-element.113.q_ref.qt_ref, bf16[2048,128]{1,0:T(8,128)(2,1)} %get-tuple-element.114.k_ref, ...), custom_call_target="tpu_custom_call" | custom-call | flops 8589934592 | bytes 8388608 | tf_op jit(solution)/shard_map/attend/pallas_call | solution.py:484
  186.5 19.4 %collective-permute-done.11 = bf16[2,512,512]{2,1,0:T(8,128)(2,1)S(1)} collective-permute-done((bf16[2,512,512]{2,1,0:T(8,128)(2,1)}, bf16[2,512,512]{2,1,0:T(8,128)(2,1)S(1)}, u32[]{:S(2)}, u32[]{:S(2)}) %collective-permute-start.11) | collective-permute-done | bytes 1048608 | tf_op jit(solution)/shard_map/ppermute | solution.py:1068
  233.5 10.9 %collective-permute-done.15 = bf16[4,128,1024]{2,1,0:T(8,128)(2,1)} collective-permute-done((bf16[4,128,1024]{2,1,0:T(8,128)(2,1)}, bf16[4,128,1024]{2,1,0:T(8,128)(2,1)}, u32[]{:S(2)}, u32[]{:S(2)}) %collective-permute-start.15) | collective-permute-done | bytes 1048608 | tf_op jit(solution)/shard_map/ppermute | solution.py:437
  253.6 41.3 %expert_chunk.4 = (bf16[512,1152]{1,0:T(8,128)(2,1)}, bf16[4,4,128,1024]{3,2,1,0:T(8,128)(2,1)}, bf16[4,512,4096]{2,1,0:T(8,128)(2,1)}, bf16[4,512,4096]{2,1,0:T(8,128)(2,1)}, bf16[4,512,4096]{2,1,0:T(8,128)(2,1)}) custom-call(s32[2]{0:T(128)} %pad_add_fusion.1.me_ref, bf16[512,1152]{1,0:T(8,128)(2,1)} %copy-done.15, ...), custom_call_target="tpu_custom_call" | custom-call | flops 25769803776 | bytes 37748736 | tf_op jit(solution)/shard_map/expert_chunk/pallas_call | solution.py:722
  297.6 39.2 %expert_chunk.5 = (bf16[512,1152]{1,0:T(8,128)(2,1)}, bf16[4,4,128,1024]{3,2,1,0:T(8,128)(2,1)}, bf16[4,512,4096]{2,1,0:T(8,128)(2,1)}, bf16[4,512,4096]{2,1,0:T(8,128)(2,1)}, bf16[4,512,4096]{2,1,0:T(8,128)(2,1)}) custom-call(s32[2]{0:T(128)} %pad_add_fusion.3.me_ref, ...), custom_call_target="tpu_custom_call", output_to_operand_aliasing={{1}: (7, {}), {2}: (8, {}), {3}: (9, {}), {4}: (10, {})} | custom-call | flops 25769803776 | bytes 37748736 | tf_op jit(solution)/shard_map/expert_chunk/pallas_call | solution.py:722
  341.6 39.1 %expert_chunk.6 = (bf16[512,1152]{1,0:T(8,128)(2,1)}, bf16[4,4,128,1024]{3,2,1,0:T(8,128)(2,1)}, bf16[4,512,4096]{2,1,0:T(8,128)(2,1)}, bf16[4,512,4096]{2,1,0:T(8,128)(2,1)}, bf16[4,512,4096]{2,1,0:T(8,128)(2,1)}) custom-call(s32[2]{0:T(128)} %get-tuple-element.368.me_ref, ...), custom_call_target="tpu_custom_call", output_to_operand_aliasing={{1}: (7, {}), {2}: (8, {}), {3}: (9, {}), {4}: (10, {})} | custom-call | flops 25769803776 | bytes 37748736 | tf_op jit(solution)/shard_map/expert_chunk/pallas_call | solution.py:722
  389.4 40.9 %expert_chunk.7 = (bf16[512,1152]{1,0:T(8,128)(2,1)}, bf16[4,4,128,1024]{3,2,1,0:T(8,128)(2,1)}, bf16[4,512,4096]{2,1,0:T(8,128)(2,1)}, bf16[4,512,4096]{2,1,0:T(8,128)(2,1)}, bf16[4,512,4096]{2,1,0:T(8,128)(2,1)}) custom-call(s32[2]{0:T(128)} %get-tuple-element.367.me_ref, ...), custom_call_target="tpu_custom_call", output_to_operand_aliasing={{1}: (7, {}), {2}: (8, {}), {3}: (9, {}), {4}: (10, {})} | custom-call | flops 25769803776 | bytes 37748736 | tf_op jit(solution)/shard_map/expert_chunk/pallas_call | solution.py:722
  433.4 14.3 %convolution_convert_fusion.2 = bf16[4096,512]{1,0:T(8,128)(2,1)} fusion(bf16[2048,4096]{1,0:T(8,128)(2,1)} %bitcast.239, bf16[2048,512]{1,0:T(8,128)(2,1)S(1)} %get-tuple-element.159), kind=kOutput, calls=%fused_computation.6 | convolution fusion | flops 8592031744 | bytes 23068672 | tf_op jit(solution)/shard_map/dot_general | solution.py:22
  447.7 14.0 %convolution_convert_fusion = bf16[512,4096]{1,0:T(8,128)(2,1)} fusion(bf16[2048,512]{1,0:T(8,128)(2,1)S(1)} %pad_maximum_fusion.7, bf16[2048,4096]{1,0:T(8,128)(2,1)} %bitcast.245), kind=kOutput, calls=%fused_computation.4 | convolution fusion | flops 8592031744 | bytes 23068672 | tf_op jit(solution)/shard_map/dot_general | solution.py:22
  462.2 10.9 %convolution_convert_fusion.1 = bf16[512,4096]{1,0:T(8,128)(2,1)} fusion(bf16[2048,512]{1,0:T(8,128)(2,1)S(1)} %pad_maximum_fusion.7, bf16[2048,4096]{1,0:T(8,128)(2,1)S(1)} %bitcast.244), kind=kOutput, calls=%fused_computation.5 | convolution fusion | flops 8592031744 | bytes 23068672 | tf_op jit(solution)/shard_map/dot_general | solution.py:22
  473.2 11.4 %collective-permute-done.22 = bf16[512,1152]{1,0:T(8,128)(2,1)S(1)} collective-permute-done((bf16[512,1152]{1,0:T(8,128)(2,1)}, bf16[512,1152]{1,0:T(8,128)(2,1)S(1)}, u32[]{:S(2)}, u32[]{:S(2)}) %collective-permute-start.22) | collective-permute-done | bytes 1179680 | tf_op jit(solution)/shard_map/ppermute | solution.py:437
  494.1 17.3 %add_convert_fusion.1 = bf16[512,4096]{1,0:T(8,128)(2,1)} fusion(bf16[512,4096]{1,0:T(8,128)(2,1)} %collective-permute-done.30, bf16[2048,512]{1,0:T(8,128)(2,1)} %pad_maximum_fusion.8, bf16[2048,4096]{1,0:T(8,128)(2,1)} %bitcast.246), kind=kOutput, calls=%fused_computation.2 | convolution fusion | flops 8596226048 | bytes 27262976 | tf_op jit(solution)/shard_map/dot_general | solution.py:22
  517.6 14.7 %add_convert_fusion = bf16[4096,512]{1,0:T(8,128)(2,1)} fusion(bf16[4096,512]{1,0:T(8,128)(2,1)} %collective-permute-done.31, bf16[2048,4096]{1,0:T(8,128)(2,1)} %bitcast.240, bf16[2048,512]{1,0:T(8,128)(2,1)S(1)} %copy-done.27), kind=kOutput, calls=%fused_computation.1 | convolution fusion | flops 8596226048 | bytes 27262976 | tf_op jit(solution)/shard_map/dot_general | solution.py:22
  532.3 14.5 %add_convert_fusion.2 = bf16[512,4096]{1,0:T(8,128)(2,1)} fusion(bf16[512,4096]{1,0:T(8,128)(2,1)} %collective-permute-done.29, bf16[2048,512]{1,0:T(8,128)(2,1)S(1)} %copy-done.29, bf16[2048,4096]{1,0:T(8,128)(2,1)} %bitcast.241), kind=kOutput, calls=%fused_computation.3 | convolution fusion | flops 8596226048 | bytes 27262976 | tf_op jit(solution)/shard_map/dot_general | solution.py:22
  574.1 44.1 %attend_back.1 = (f32[256,2048]{1,0:T(8,128)}, f32[2048,128]{1,0:T(8,128)}, f32[2048,128]{1,0:T(8,128)}) custom-call(s32[4]{0:T(128)} %get-tuple-element.366.low_ref, s32[4]{0:T(128)} %get-tuple-element.365.mid_ref, bf16[4,128,2048]{2,1,0:T(8,128)(2,1)} %get-tuple-element.113.q_ref.qt_ref, bf16[4,2048,128]{2,1,0:T(8,128)(2,1)} %get-tuple-element.162.q_ref, ...), custom_call_target="tpu_custom_call" | custom-call | flops 21474836480 | bytes 16777216 | tf_op jit(solution)/shard_map/attend_back/pallas_call | solution.py:596
  618.2 15.0 %collective-permute-done.35 = bf16[1536,512]{1,0:T(8,128)(2,1)} collective-permute-done((bf16[1536,512]{1,0:T(8,128)(2,1)}, bf16[1536,512]{1,0:T(8,128)(2,1)}, u32[]{:S(2)}, u32[]{:S(2)}) %collective-permute-start.35) | collective-permute-done | bytes 1572896 | tf_op jit(solution)/shard_map/ppermute | solution.py:1068
  635.2 10.0 %unproject.1 = (f32[512,1024]{1,0:T(8,128)}, f32[8,1024]{1,0:T(8,128)}, bf16[512,512]{1,0:T(8,128)(2,1)}, bf16[512,512]{1,0:T(8,128)(2,1)}, bf16[512,512]{1,0:T(...) custom-call(s32[1]{0:T(128)} %bitcast.17.me_ref, ...), custom_call_target="tpu_custom_call" | custom-call | flops 4294967296 | bytes 12582912 | tf_op jit(solution)/shard_map/unproject/pallas_call | solution.py:1034
  659.6 15.0 %collective-permute-done.40 = bf16[2,512,512]{2,1,0:T(8,128)(2,1)S(1)} collective-permute-done((bf16[2,512,512]{2,1,0:T(8,128)(2,1)}, bf16[2,512,512]{2,1,0:T(8,128)(2,1)S(1)}, u32[]{:S(2)}, u32[]{:S(2)}) %collective-permute-start.40) | collective-permute-done | bytes 1048608 | tf_op jit(solution)/shard_map/ppermute | solution.py:1068
  707.8 22.1 %collective-permute-start.48 = (bf16[128,1024]{1,0:T(8,128)(2,1)S(1)}, bf16[128,1024]{1,0:T(8,128)(2,1)S(1)}, u32[]{:S(2)}, u32[]{:S(2)}) collective-permute-start(bf16[128,1024]{1,0:T(8,128)(2,1)S(1)} %get-tuple-element.339), channel_id=1, source_target_pairs={{0,4},{4,8},{8,12},{12,0},{1,5},{5,9},{9,13},{13,1},{2,6},{6,10},{... | collective-permute-start | bytes 786440 | tf_op jit(solution)/shard_map/ppermute | solution.py:437
  755.4 16.9 %collective-permute-start.59 = (bf16[808,128]{1,0:T(8,128)(2,1)S(1)}, bf16[808,128]{1,0:T(8,128)(2,1)S(1)}, u32[]{:S(2)}, u32[]{:S(2)}) collective-permute-start(bf16[808,128]{1,0:T(8,128)(2,1)S(1)} %get-tuple-element.352), channel_id=1, source_target_pairs={{0,4},{4,8},{8,12},{12,0},{1,5},{5,9},{9,13},{13,1},{2,6},{6,10},{... | collective-permute-start | bytes 620552 | tf_op jit(solution)/shard_map/ppermute | solution.py:437
  (430 shorter events, 293.6 us)
Async XLA Ops:
  7.2 172.9 %all-gather.3.cloned.1.call-start = ((), (), s32[]{:S(2)}) async-start(), calls=%async_computation.2 | async-start | bytes 15728640 | tf_op jit(solution)/shard_map/all_gather | solution.py:1169
  28.7 660.3 %reduce-scatter.2.cloned.1.call-start = ((), (), s32[]{:S(2)}) async-start(), calls=%async_computation.1 | async-start | bytes 5242880 | tf_op jit(solution)/shard_map/reduce_scatter | solution.py:1339
  59.6 38.0 %collective-permute-start.9 = (bf16[4,128,1024]{2,1,0:T(8,128)(2,1)S(1)}, bf16[4,128,1024]{2,1,0:T(8,128)(2,1)}, u32[]{:S(2)}, u32[]{:S(2)}) collective-permute-start(bf16[4,128,1024]{2,1,0:T(8,128)(2,1)S(1)} %constant_dynamic-slice_fusion.57), channel_id=1, source_target_pairs={{0,4},{4,8},{8,12},{12,0},{1,5},{5,9},{9,13},{13,1},{2,6},{6,10},{... | collective-permute-start | bytes 3145736 | tf_op jit(solution)/shard_map/ppermute | solution.py:437
  73.2 54.4 %collective-permute-start.4 = (bf16[512,512]{1,0:T(8,128)(2,1)}, bf16[512,512]{1,0:T(8,128)(2,1)}, u32[]{:S(2)}, u32[]{:S(2)}) collective-permute-start(bf16[512,512]{1,0:T(8,128)(2,1)} %get-tuple-element.350.refs_1_), channel_id=1, source_target_pairs={{0,1},{1,0},{2,3},{3,2},{4,5},{5,4},{6,7},{7,6},{8,9},{9,8},{10,11... | collective-permute-start | bytes 1572872 | tf_op jit(solution)/shard_map/ppermute | solution.py:1068
  73.7 53.8 %collective-permute-start.5 = (bf16[512,512]{1,0:T(8,128)(2,1)}, bf16[512,512]{1,0:T(8,128)(2,1)}, u32[]{:S(2)}, u32[]{:S(2)}) collective-permute-start(bf16[512,512]{1,0:T(8,128)(2,1)} %get-tuple-element.351.refs_0_), channel_id=1, source_target_pairs={{0,2},{1,3},{2,0},{3,1},{4,6},{5,7},{6,4},{7,5},{8,10},{9,11},{10,... | collective-permute-start | bytes 1572872 | tf_op jit(solution)/shard_map/ppermute | solution.py:1068
  103.0 64.9 %collective-permute-start.10 = (bf16[4,128,1024]{2,1,0:T(8,128)(2,1)S(1)}, bf16[4,128,1024]{2,1,0:T(8,128)(2,1)S(1)}, u32[]{:S(2)}, u32[]{:S(2)}) collective-permute-start(bf16[4,128,1024]{2,1,0:T(8,128)(2,1)S(1)} %get-tuple-element.295), channel_id=1, source_target_pairs={{0,8},{4,12},{8,0},{12,4},{1,9},{5,13},{9,1},{13,5},{2,10},{6,14},... | collective-permute-start | bytes 3145736 | tf_op jit(solution)/shard_map/ppermute | solution.py:437
  180.1 73.4 %collective-permute-start.16 = (bf16[4,3,512,1024]{3,2,1,0:T(8,128)(2,1)}, bf16[4,3,512,1024]{3,2,1,0:T(8,128)(2,1)}, u32[]{:S(2)}, u32[]{:S(2)}) collective-permute-start(bf16[4,3,512,1024]{3,2,1,0:T(8,128)(2,1)} %bitcast.234), channel_id=1, source_target_pairs={{0,16},{16,0},{1,17},{17,1},{2,18},{18,2},{3,19},{19,3},{4,20},{20... | collective-permute-start | bytes 37748744 | tf_op jit(solution)/shard_map/ppermute | solution.py:1068
  229.9 65.0 %collective-permute-start.20 = (bf16[512,1152]{1,0:T(8,128)(2,1)S(1)}, bf16[512,1152]{1,0:T(8,128)(2,1)}, u32[]{:S(2)}, u32[]{:S(2)}) collective-permute-start(bf16[512,1152]{1,0:T(8,128)(2,1)S(1)} %concatenate.79.x_ref), channel_id=1, source_target_pairs={{0,12},{4,0},{8,4},{12,8},{1,13},{5,1},{9,5},{13,9},{2,14},{6,2},{... | collective-permute-start | bytes 3538952 | tf_op jit(solution)/shard_map/ppermute | solution.py:437
  233.3 103.5 %collective-permute-start.19 = (bf16[512,1152]{1,0:T(8,128)(2,1)S(1)}, bf16[512,1152]{1,0:T(8,128)(2,1)}, u32[]{:S(2)}, u32[]{:S(2)}) collective-permute-start(bf16[512,1152]{1,0:T(8,128)(2,1)S(1)} %concatenate.79.x_ref), channel_id=1, source_target_pairs={{0,4},{4,8},{8,12},{12,0},{1,5},{5,9},{9,13},{13,1},{2,6},{6,10},{... | collective-permute-start | bytes 3538952 | tf_op jit(solution)/shard_map/ppermute | solution.py:437
  296.0 45.5 %collective-permute-start.17 = (bf16[256,1152]{1,0:T(8,128)(2,1)}, bf16[256,1152]{1,0:T(8,128)(2,1)S(1)}, u32[]{:S(2)}, u32[]{:S(2)}) collective-permute-start(bf16[256,1152]{1,0:T(8,128)(2,1)} %get-tuple-element.318), channel_id=1, source_target_pairs={{0,8},{4,12},{8,0},{12,4},{1,9},{5,13},{9,1},{13,5},{2,10},{6,14},... | collective-permute-start | bytes 1769480 | tf_op jit(solution)/shard_map/ppermute | solution.py:437
  336.8 96.6 %collective-permute-start.21 = (bf16[512,1152]{1,0:T(8,128)(2,1)}, bf16[512,1152]{1,0:T(8,128)(2,1)}, u32[]{:S(2)}, u32[]{:S(2)}) collective-permute-start(bf16[512,1152]{1,0:T(8,128)(2,1)} %get-tuple-element.137), channel_id=1, source_target_pairs={{0,4},{4,8},{8,12},{12,0},{1,5},{5,9},{9,13},{13,1},{2,6},{6,10},{... | collective-permute-start | bytes 3538952 | tf_op jit(solution)/shard_map/ppermute | solution.py:437
  340.3 48.0 %collective-permute-start.18 = (bf16[256,1152]{1,0:T(8,128)(2,1)}, bf16[256,1152]{1,0:T(8,128)(2,1)S(1)}, u32[]{:S(2)}, u32[]{:S(2)}) collective-permute-start(bf16[256,1152]{1,0:T(8,128)(2,1)} %get-tuple-element.319), channel_id=1, source_target_pairs={{0,8},{4,12},{8,0},{12,4},{1,9},{5,13},{9,1},{13,5},{2,10},{6,14},... | collective-permute-start | bytes 1769480 | tf_op jit(solution)/shard_map/ppermute | solution.py:437
  380.6 52.8 %collective-permute-start.23 = (bf16[512,1152]{1,0:T(8,128)(2,1)}, bf16[512,1152]{1,0:T(8,128)(2,1)}, u32[]{:S(2)}, u32[]{:S(2)}) collective-permute-start(bf16[512,1152]{1,0:T(8,128)(2,1)} %get-tuple-element.143), channel_id=1, source_target_pairs={{0,12},{4,0},{8,4},{12,8},{1,13},{5,1},{9,5},{13,9},{2,14},{6,2},{... | collective-permute-start | bytes 3538952 | tf_op jit(solution)/shard_map/ppermute | solution.py:437
  430.3 54.3 %collective-permute-start.22 = (bf16[512,1152]{1,0:T(8,128)(2,1)}, bf16[512,1152]{1,0:T(8,128)(2,1)S(1)}, u32[]{:S(2)}, u32[]{:S(2)}) collective-permute-start(bf16[512,1152]{1,0:T(8,128)(2,1)} %get-tuple-element.152), channel_id=1, source_target_pairs={{0,8},{4,12},{8,0},{12,4},{1,9},{5,13},{9,1},{13,5},{2,10},{6,14},... | collective-permute-start | bytes 3538952 | tf_op jit(solution)/shard_map/ppermute | solution.py:437
  447.7 68.9 %collective-permute-start.31 = (bf16[4096,512]{1,0:T(8,128)(2,1)}, bf16[4096,512]{1,0:T(8,128)(2,1)}, u32[]{:S(2)}, u32[]{:S(2)}) collective-permute-start(bf16[4096,512]{1,0:T(8,128)(2,1)} %convolution_convert_fusion.2), channel_id=1, source_target_pairs={{0,16},{16,0},{1,17},{17,1},{2,18},{18,2},{3,19},{19,3},{4,20},{20... | collective-permute-start | bytes 12582920 | tf_op jit(solution)/shard_map/ppermute | solution.py:1068
  473.2 59.1 %collective-permute-start.29 = (bf16[512,4096]{1,0:T(8,128)(2,1)}, bf16[512,4096]{1,0:T(8,128)(2,1)}, u32[]{:S(2)}, u32[]{:S(2)}) collective-permute-start(bf16[512,4096]{1,0:T(8,128)(2,1)} %convolution_convert_fusion.1), channel_id=1, source_target_pairs={{0,16},{16,0},{1,17},{17,1},{2,18},{18,2},{3,19},{19,3},{4,20},{20... | collective-permute-start | bytes 12582920 | tf_op jit(solution)/shard_map/ppermute | solution.py:1068
  491.9 54.9 %collective-permute-start.25 = (bf16[512,512]{1,0:T(8,128)(2,1)}, bf16[512,512]{1,0:T(8,128)(2,1)}, u32[]{:S(2)}, u32[]{:S(2)}) collective-permute-start(bf16[512,512]{1,0:T(8,128)(2,1)} %get-tuple-element.348.refs_1_), channel_id=1, source_target_pairs={{0,1},{1,0},{2,3},{3,2},{4,5},{5,4},{6,7},{7,6},{8,9},{9,8},{10,11... | collective-permute-start | bytes 1572872 | tf_op jit(solution)/shard_map/ppermute | solution.py:1068
  565.5 52.7 %collective-permute-start.33 = (bf16[1536,512]{1,0:T(8,128)(2,1)}, bf16[1536,512]{1,0:T(8,128)(2,1)}, u32[]{:S(2)}, u32[]{:S(2)}) collective-permute-start(bf16[1536,512]{1,0:T(8,128)(2,1)} %pad_maximum_fusion.13), channel_id=1, source_target_pairs={{0,1},{1,0},{2,3},{3,2},{4,5},{5,4},{6,7},{7,6},{8,9},{9,8},{10,11... | collective-permute-start | bytes 4718600 | tf_op jit(solution)/shard_map/ppermute | solution.py:1068
  567.7 50.5 %collective-permute-start.36 = (bf16[1536,512]{1,0:T(8,128)(2,1)}, bf16[1536,512]{1,0:T(8,128)(2,1)}, u32[]{:S(2)}, u32[]{:S(2)}) collective-permute-start(bf16[1536,512]{1,0:T(8,128)(2,1)} %pad_maximum_fusion.16), channel_id=1, source_target_pairs={{0,2},{1,3},{2,0},{3,1},{4,6},{5,7},{6,4},{7,5},{8,10},{9,11},{10,... | collective-permute-start | bytes 4718600 | tf_op jit(solution)/shard_map/ppermute | solution.py:1068
  570.4 62.8 %collective-permute-start.35 = (bf16[1536,512]{1,0:T(8,128)(2,1)}, bf16[1536,512]{1,0:T(8,128)(2,1)}, u32[]{:S(2)}, u32[]{:S(2)}) collective-permute-start(bf16[1536,512]{1,0:T(8,128)(2,1)} %pad_maximum_fusion.15), channel_id=1, source_target_pairs={{0,1},{1,0},{2,3},{3,2},{4,5},{5,4},{6,7},{7,6},{8,9},{9,8},{10,11... | collective-permute-start | bytes 4718600 | tf_op jit(solution)/shard_map/ppermute | solution.py:1068
  572.3 62.9 %collective-permute-start.34 = (bf16[1536,512]{1,0:T(8,128)(2,1)}, bf16[1536,512]{1,0:T(8,128)(2,1)}, u32[]{:S(2)}, u32[]{:S(2)}) collective-permute-start(bf16[1536,512]{1,0:T(8,128)(2,1)} %pad_maximum_fusion.14), channel_id=1, source_target_pairs={{0,2},{1,3},{2,0},{3,1},{4,6},{5,7},{6,4},{7,5},{8,10},{9,11},{10,... | collective-permute-start | bytes 4718600 | tf_op jit(solution)/shard_map/ppermute | solution.py:1068
  705.3 39.2 %collective-permute-start.51 = (bf16[1536,512]{1,0:T(8,128)(2,1)}, bf16[1536,512]{1,0:T(8,128)(2,1)}, u32[]{:S(2)}, u32[]{:S(2)}) collective-permute-start(bf16[1536,512]{1,0:T(8,128)(2,1)} %add_convert_fusion.4), channel_id=1, source_target_pairs={{0,2},{1,3},{2,0},{3,1},{4,6},{5,7},{6,4},{7,5},{8,10},{9,11},{10,... | collective-permute-start | bytes 4718600 | tf_op jit(solution)/shard_map/ppermute | solution.py:1068
  706.1 38.3 %collective-permute-start.52 = (bf16[1536,512]{1,0:T(8,128)(2,1)}, bf16[1536,512]{1,0:T(8,128)(2,1)}, u32[]{:S(2)}, u32[]{:S(2)}) collective-permute-start(bf16[1536,512]{1,0:T(8,128)(2,1)} %add_convert_fusion.3), channel_id=1, source_target_pairs={{0,1},{1,0},{2,3},{3,2},{4,5},{5,4},{6,7},{7,6},{8,9},{9,8},{10,11... | collective-permute-start | bytes 4718600 | tf_op jit(solution)/shard_map/ppermute | solution.py:1068
  747.3 44.1 %collective-permute-start.54 = (bf16[4,128,512]{2,1,0:T(8,128)(2,1)}, bf16[4,128,512]{2,1,0:T(8,128)(2,1)}, u32[]{:S(2)}, u32[]{:S(2)}) collective-permute-start(bf16[4,128,512]{2,1,0:T(8,128)(2,1)} %get-tuple-element.331), channel_id=1, source_target_pairs={{0,2},{1,3},{2,0},{3,1},{4,6},{5,7},{6,4},{7,5},{8,10},{9,11},{10,... | collective-permute-start | bytes 1572872 | tf_op jit(solution)/shard_map/ppermute | solution.py:1068
  (120 other events, 1844.8 us)
Sparse Core Ops, SparseCore 0:
  28.8 151.2 all-gather.2
  492.6 89.9 reduce-scatter.1
